TPU v7x, 32 devices: a whole 2x2x4 slice. The times are simulated.
32 devices in a mesh: ctx: 4 (over z), fsdp: 8 (over y, x, core).
Axes of the slice: x: 2, y: 2, z: 4, core: 2. Of those that a mesh axis runs over, the one named last changes fastest.
Arguments:
- tokens: bfloat16 [8, 512, 2048], P('fsdp', 'ctx'), may hold values from -6 to 6
- block_pairs: int32 [8, 4], P('fsdp'), may hold values from 0 to 3, each once within a row
- w_query: bfloat16 [2048, 2048], P('fsdp'), may hold values from -0.125 to 0.125
- w_key: bfloat16 [2048, 2048], P('fsdp'), may hold values from -0.125 to 0.125
- w_value: bfloat16 [2048, 2048], P('fsdp'), may hold values from -0.125 to 0.125
- w_out: bfloat16 [2048, 2048], P('fsdp'), may hold values from -0.125 to 0.125
- w_gate: bfloat16 [2048, 8192], P('fsdp'), may hold values from -0.125 to 0.125
- w_up: bfloat16 [2048, 8192], P('fsdp'), may hold values from -0.125 to 0.125
- w_down: bfloat16 [8192, 2048], P('fsdp'), may hold values from -0.0625 to 0.0625
- gain_query: float32 [2048], replicated, may hold values from 0.25 to 1.75
- gain_key: float32 [2048], replicated, may hold values from 0.25 to 1.75
- gain_attn: float32 [2048], replicated, may hold values from 0.25 to 1.75
- gain_mlp: float32 [2048], replicated, may hold values from 0.25 to 1.75
- cotangent: bfloat16 [8, 512, 2048], P('fsdp', 'ctx'), may hold values from -6 to 6
Outputs:
- output: bfloat16 [8, 512, 2048], P('fsdp', 'ctx')
- d_tokens: bfloat16 [8, 512, 2048], P('fsdp', 'ctx')
- grad_w_query: float32 [2048, 2048], P(('ctx', 'fsdp'))
- grad_w_key: float32 [2048, 2048], P(('ctx', 'fsdp'))
- grad_w_value: float32 [2048, 2048], P(('ctx', 'fsdp'))
- grad_w_out: float32 [2048, 2048], P(('ctx', 'fsdp'))
- grad_w_gate: float32 [2048, 8192], P(('ctx', 'fsdp'))
- grad_w_up: float32 [2048, 8192], P(('ctx', 'fsdp'))
- grad_w_down: float32 [8192, 2048], P(('ctx', 'fsdp'))
- grad_gain_query: float32 [2048], P(('ctx', 'fsdp'))
- grad_gain_key: float32 [2048], P(('ctx', 'fsdp'))
- grad_gain_attn: float32 [2048], P(('ctx', 'fsdp'))
- grad_gain_mlp: float32 [2048], P(('ctx', 'fsdp'))
Inputs may be any that keep to these rules, and one draw needn't show every extreme that they name: Each row of block_pairs names every number from 0 to 3 once.
All inputs are finite; a program needn't handle non-finite values.
Results may differ from a plain program's by a relative error of at most 0.019.
Values may be sent and summed in bfloat16 or wider, within the bound.
A program may use at most 704 MiB of HBM per device.

v0:
```python
import jax
import jax.numpy as jnp
from jax import lax
from jax.sharding import PartitionSpec as P

HD = 128


EPSILON = 1e-06
ROPE_BASE = 500000.0
NEGATIVE = -1e30
HEAD_GROUP = 4


def norm_scale(values, gain_vec):
    return (
        values * lax.rsqrt(jnp.mean(values * values, axis=-1, keepdims=True) + EPSILON) * gain_vec
    )


def turn_half(values, cosine, sine):
    half_size = values.shape[-1] // 2
    turned = jnp.concatenate([-values[..., half_size:], values[..., :half_size]], axis=-1)
    return values * cosine + turned * sine


def angle_tables(positions, head_size):
    half_size = head_size // 2
    frequency = jnp.power(ROPE_BASE, -(jnp.arange(half_size).astype(jnp.float32) * 2.0 / head_size))
    angles = positions.astype(jnp.float32)[:, None] * frequency[None, :]
    angles = jnp.concatenate([angles, angles], axis=-1)
    return (jnp.cos(angles)[:, None, :], jnp.sin(angles)[:, None, :])


def row_positions(row_ids, pair_row, block_rows, ctx_count):
    rank_of = row_ids // (2 * block_rows)
    second = row_ids // block_rows % 2
    offset = row_ids % block_rows
    rank_match = (rank_of[:, None] == jnp.arange(ctx_count, dtype=jnp.int32)[None, :]).astype(
        jnp.int32
    )
    chosen = jnp.sum(rank_match * pair_row[None, :], axis=1)
    block_index = jnp.where(second == 0, chosen, 2 * ctx_count - 1 - chosen)
    return block_index * block_rows + offset


def times_transpose(left, right):
    return lax.dot_general(
        left, right, (((1,), (1,)), ((), ())), preferred_element_type=jnp.float32
    )


def transpose_times(left, right):
    return lax.dot_general(
        left, right, (((0,), (0,)), ((), ())), preferred_element_type=jnp.float32
    )


def activate(gate_in, up_in):
    return jax.nn.silu(gate_in) * up_in


def shards(
    tokens,
    block_pairs,
    w_query,
    w_key,
    w_value,
    w_out,
    w_gate,
    w_up,
    w_down,
    gain_query,
    gain_key,
    gain_attn,
    gain_mlp,
    cotangent,
):
    local_rows = tokens.shape[1]
    block_rows = local_rows // 2
    model_width = w_query.shape[1]
    hidden_width = w_gate.shape[1]
    head_size = HD
    head_count = model_width // head_size
    ctx_count = lax.axis_size("ctx")
    ctx_index = lax.axis_index("ctx")
    seq_length = local_rows * ctx_count
    score_scale = head_size ** (-0.5)
    group_span = HEAD_GROUP * head_size
    group_count = head_count // HEAD_GROUP
    key_pos = row_positions(
        jnp.arange(seq_length, dtype=jnp.int32), block_pairs[0], block_rows, ctx_count
    )
    own_pos = lax.dynamic_slice_in_dim(key_pos, ctx_index * local_rows, local_rows)
    cosine, sine = angle_tables(own_pos, head_size)
    causal_mask = key_pos[None, :] <= own_pos[:, None]
    token_rows = tokens[0]

    def query_side(raw_rows, gain_vec):
        return turn_half(
            norm_scale(raw_rows, gain_vec).reshape(local_rows, head_count, head_size), cosine, sine
        )

    q_weight, k_weight, v_weight, o_weight = (
        lax.all_gather(w_query, "fsdp", axis=0, tiled=True),
        lax.all_gather(w_key, "fsdp", axis=0, tiled=True),
        lax.all_gather(w_value, "fsdp", axis=0, tiled=True),
        lax.all_gather(w_out, "fsdp", axis=0, tiled=True),
    )
    q_raw = jnp.dot(token_rows, q_weight, preferred_element_type=jnp.float32)
    k_raw = jnp.dot(token_rows, k_weight, preferred_element_type=jnp.float32)
    v_raw = jnp.dot(token_rows, v_weight, preferred_element_type=jnp.float32)
    queries = query_side(q_raw, gain_query).astype(jnp.bfloat16).reshape(local_rows, model_width)
    key_local = query_side(k_raw, gain_key).astype(jnp.bfloat16).reshape(local_rows, model_width)
    value_local = v_raw.astype(jnp.bfloat16)
    key_all, value_all = (
        lax.all_gather(key_local, "ctx", axis=0, tiled=True),
        lax.all_gather(value_local, "ctx", axis=0, tiled=True),
    )

    def scores_of(group_index, key_source):
        part_q = lax.dynamic_slice_in_dim(queries, group_index * group_span, group_span, 1).reshape(
            local_rows, HEAD_GROUP, head_size
        )
        part_k = lax.dynamic_slice_in_dim(
            key_source, group_index * group_span, group_span, 1
        ).reshape(seq_length, HEAD_GROUP, head_size)
        raw_scores = (
            jnp.einsum("qhd,khd->hqk", part_q, part_k, preferred_element_type=jnp.float32)
            * score_scale
        )
        return (jnp.where(causal_mask[None], raw_scores, NEGATIVE), part_q, part_k)

    def forward_group(group_index, loop_state):
        attended_acc, row_maxima, row_totals = loop_state
        scores, part_q, part_k = scores_of(group_index, key_all)
        row_max = jnp.max(scores, axis=-1, keepdims=True)
        exponent = jnp.exp(scores - row_max)
        row_total = jnp.sum(exponent, axis=-1, keepdims=True)
        prob_low = (exponent / row_total).astype(jnp.bfloat16)
        part_v = lax.dynamic_slice_in_dim(
            value_all, group_index * group_span, group_span, 1
        ).reshape(seq_length, HEAD_GROUP, head_size)
        group_out = jnp.einsum(
            "hqk,khd->qhd", prob_low, part_v, preferred_element_type=jnp.float32
        ).reshape(local_rows, group_span)
        attended_acc = lax.dynamic_update_slice_in_dim(
            attended_acc, group_out, group_index * group_span, 1
        )
        row_maxima = lax.dynamic_update_slice_in_dim(
            row_maxima, row_max, group_index * HEAD_GROUP, 0
        )
        row_totals = lax.dynamic_update_slice_in_dim(
            row_totals, row_total, group_index * HEAD_GROUP, 0
        )
        return (attended_acc, row_maxima, row_totals)

    start_state = (
        jnp.zeros((local_rows, model_width), jnp.float32),
        jnp.zeros((head_count, local_rows, 1), jnp.float32),
        jnp.zeros((head_count, local_rows, 1), jnp.float32),
    )
    attended, row_maxima, row_totals = lax.fori_loop(0, group_count, forward_group, start_state)
    attended_low = attended.astype(jnp.bfloat16)
    branch = jnp.dot(attended_low, o_weight, preferred_element_type=jnp.float32)
    mid_stream = token_rows.astype(jnp.float32) + norm_scale(branch, gain_attn)
    mid_low = mid_stream.astype(jnp.bfloat16)
    g_weight, u_weight, d_weight = (
        lax.all_gather(w_gate, "fsdp", axis=0, tiled=True),
        lax.all_gather(w_up, "fsdp", axis=0, tiled=True),
        lax.all_gather(w_down, "fsdp", axis=0, tiled=True),
    )
    gate_act = jnp.dot(mid_low, g_weight, preferred_element_type=jnp.float32)
    up_act = jnp.dot(mid_low, u_weight, preferred_element_type=jnp.float32)
    hidden = activate(gate_act, up_act).astype(jnp.bfloat16)
    mlp_out = jnp.dot(hidden, d_weight, preferred_element_type=jnp.float32)
    output = (mid_stream + norm_scale(mlp_out, gain_mlp)).astype(jnp.bfloat16)
    d_output = cotangent[0].astype(jnp.float32)
    unused_mlp, pull_mlp = jax.vjp(norm_scale, mlp_out, gain_mlp)
    d_mlp, grad_gm = pull_mlp(d_output)
    d_mlp_low = d_mlp.astype(jnp.bfloat16)
    g_back, u_back, d_back = (
        lax.all_gather(w_gate, "fsdp", axis=0, tiled=True),
        lax.all_gather(w_up, "fsdp", axis=0, tiled=True),
        lax.all_gather(w_down, "fsdp", axis=0, tiled=True),
    )
    d_hidden = times_transpose(d_mlp_low, d_back)
    unused_act, pull_act = jax.vjp(activate, gate_act, up_act)
    d_gate, d_up = pull_act(d_hidden)
    d_gate_low = d_gate.astype(jnp.bfloat16)
    d_up_low = d_up.astype(jnp.bfloat16)
    d_mid = d_output + times_transpose(d_gate_low, g_back) + times_transpose(d_up_low, u_back)
    gate_up = jnp.concatenate([d_gate_low, d_up_low], axis=1)
    column_part = mid_low
    gate_up_grads = lax.psum_scatter(
        transpose_times(column_part, gate_up), ("ctx", "fsdp"), scatter_dimension=0, tiled=True
    )
    column_part = hidden
    grad_down = lax.psum_scatter(
        transpose_times(column_part, d_mlp_low), ("ctx", "fsdp"), scatter_dimension=0, tiled=True
    )
    unused_branch, pull_branch = jax.vjp(norm_scale, branch, gain_attn)
    d_branch, grad_ga = pull_branch(d_mid)
    d_branch_low = d_branch.astype(jnp.bfloat16)
    q_back, k_back, v_back, o_back = (
        lax.all_gather(w_query, "fsdp", axis=0, tiled=True),
        lax.all_gather(w_key, "fsdp", axis=0, tiled=True),
        lax.all_gather(w_value, "fsdp", axis=0, tiled=True),
        lax.all_gather(w_out, "fsdp", axis=0, tiled=True),
    )
    d_attended = times_transpose(d_branch_low, o_back).astype(jnp.bfloat16)
    out_term = transpose_times(attended_low, d_branch_low)
    key_back, value_back = (key_all, value_all)

    def backward_group(group_index, loop_state):
        d_query_acc, d_kv_acc = loop_state
        scores, part_q, part_k = scores_of(group_index, key_back)
        row_max = lax.dynamic_slice_in_dim(row_maxima, group_index * HEAD_GROUP, HEAD_GROUP, 0)
        row_total = lax.dynamic_slice_in_dim(row_totals, group_index * HEAD_GROUP, HEAD_GROUP, 0)
        probs = jnp.exp(scores - row_max) / row_total
        prob_low = probs.astype(jnp.bfloat16)
        part_v = lax.dynamic_slice_in_dim(
            value_back, group_index * group_span, group_span, 1
        ).reshape(seq_length, HEAD_GROUP, head_size)
        part_d = lax.dynamic_slice_in_dim(
            d_attended, group_index * group_span, group_span, 1
        ).reshape(local_rows, HEAD_GROUP, head_size)
        d_value = jnp.einsum(
            "hqk,qhd->khd", prob_low, part_d, preferred_element_type=jnp.float32
        ).reshape(seq_length, group_span)
        d_probs = jnp.einsum("qhd,khd->hqk", part_d, part_v, preferred_element_type=jnp.float32)
        row_delta = jnp.sum(probs * d_probs, axis=-1, keepdims=True)
        d_scores = (probs * (d_probs - row_delta)).astype(jnp.bfloat16)
        d_query = (
            jnp.einsum(
                "hqk,khd->qhd", d_scores, part_k, preferred_element_type=jnp.float32
            ).reshape(local_rows, group_span)
            * score_scale
        )
        d_key = (
            jnp.einsum(
                "hqk,qhd->khd", d_scores, part_q, preferred_element_type=jnp.float32
            ).reshape(seq_length, group_span)
            * score_scale
        )
        d_query_acc = lax.dynamic_update_slice_in_dim(
            d_query_acc, d_query, group_index * group_span, 1
        )
        d_kv_acc = lax.dynamic_update_slice_in_dim(d_kv_acc, d_key, group_index * group_span, 1)
        d_kv_acc = lax.dynamic_update_slice_in_dim(
            d_kv_acc, d_value, model_width + group_index * group_span, 1
        )
        return (d_query_acc, d_kv_acc)

    back_state = (
        jnp.zeros((local_rows, model_width), jnp.float32),
        jnp.zeros((seq_length, 2 * model_width), jnp.float32),
    )
    d_query_rot, d_kv_term = lax.fori_loop(0, group_count, backward_group, back_state)
    d_kv_own = lax.psum_scatter(
        d_kv_term.astype(jnp.bfloat16), "ctx", scatter_dimension=0, tiled=True
    ).astype(jnp.float32)
    d_key_rot = d_kv_own[:, :model_width]
    d_value_low = d_kv_own[:, model_width:].astype(jnp.bfloat16)
    unused_query, pull_query = jax.vjp(query_side, q_raw, gain_query)
    d_q_raw, grad_gq = pull_query(d_query_rot.reshape(local_rows, head_count, head_size))
    unused_key, pull_key = jax.vjp(query_side, k_raw, gain_key)
    d_k_raw, grad_gk = pull_key(d_key_rot.reshape(local_rows, head_count, head_size))
    d_q_low = d_q_raw.astype(jnp.bfloat16)
    d_k_low = d_k_raw.astype(jnp.bfloat16)
    d_tokens = (
        d_mid
        + times_transpose(d_q_low, q_back)
        + times_transpose(d_k_low, k_back)
        + times_transpose(d_value_low, v_back)
    )
    qkv_rows = jnp.concatenate([d_q_low, d_k_low, d_value_low], axis=1)
    column_part = token_rows
    qkv_grads = lax.psum_scatter(
        transpose_times(column_part, qkv_rows), ("ctx", "fsdp"), scatter_dimension=0, tiled=True
    )
    grad_out, sum_gq, sum_gk, sum_ga, sum_gm = (
        lax.psum_scatter(out_term, ("ctx", "fsdp"), scatter_dimension=0, tiled=True),
        lax.psum_scatter(grad_gq, ("ctx", "fsdp"), scatter_dimension=0, tiled=True),
        lax.psum_scatter(grad_gk, ("ctx", "fsdp"), scatter_dimension=0, tiled=True),
        lax.psum_scatter(grad_ga, ("ctx", "fsdp"), scatter_dimension=0, tiled=True),
        lax.psum_scatter(grad_gm, ("ctx", "fsdp"), scatter_dimension=0, tiled=True),
    )
    return (
        output[None],
        d_tokens.astype(jnp.bfloat16)[None],
        qkv_grads[:, :model_width],
        qkv_grads[:, model_width : 2 * model_width],
        qkv_grads[:, 2 * model_width :],
        grad_out,
        gate_up_grads[:, :hidden_width],
        gate_up_grads[:, hidden_width:],
        grad_down,
        sum_gq,
        sum_gk,
        sum_ga,
        sum_gm,
    )


def solution(mesh):
    in_specs = (
        P("fsdp", "ctx", None),
        P("fsdp", None),
        P("fsdp", None),
        P("fsdp", None),
        P("fsdp", None),
        P("fsdp", None),
        P("fsdp", None),
        P("fsdp", None),
        P("fsdp", None),
        P(),
        P(),
        P(),
        P(),
        P("fsdp", "ctx", None),
    )
    out_specs = (
        P("fsdp", "ctx", None),
        P("fsdp", "ctx", None),
        P(("ctx", "fsdp"), None),
        P(("ctx", "fsdp"), None),
        P(("ctx", "fsdp"), None),
        P(("ctx", "fsdp"), None),
        P(("ctx", "fsdp"), None),
        P(("ctx", "fsdp"), None),
        P(("ctx", "fsdp"), None),
        P(("ctx", "fsdp")),
        P(("ctx", "fsdp")),
        P(("ctx", "fsdp")),
        P(("ctx", "fsdp")),
    )
    return jax.shard_map(shards, mesh=mesh, in_specs=in_specs, out_specs=out_specs, check_vma=False)
```

profile of v0, /device:TPU:11, one launch (start us, length us, event | category | flops | bytes accessed | tf_op | source)
XLA Modules:
  0.0 4243.5 jit_solution(9477879786665022247)
XLA Ops:
  10.7 55.1 %all-gather.10.cloned.1.call-done = bf16[2048,2048]{1,0:T(8,128)(2,1)} async-done(((bf16[256,2048]{1,0:T(8,128)(2,1)}), bf16[2048,2048]{1,0:T(8,128)(2,1)}) %all-gather.10.cloned.1.call-update) | async-done | bytes 8388624 | tf_op jit(solution)/shard_map/all_gather | solution.py:107
  71.6 50.6 %all-gather.16.cloned.1.call-done = bf16[2048,2048]{1,0:T(8,128)(2,1)} async-done(((bf16[256,2048]{1,0:T(8,128)(2,1)}), bf16[2048,2048]{1,0:T(8,128)(2,1)}) %all-gather.16.cloned.1.call-update) | async-done | bytes 8388624 | tf_op jit(solution)/shard_map/all_gather | solution.py:106
  127.7 50.8 %all-gather.14.cloned.1.call-done = bf16[2048,2048]{1,0:T(8,128)(2,1)} async-done(((bf16[256,2048]{1,0:T(8,128)(2,1)}), bf16[2048,2048]{1,0:T(8,128)(2,1)}) %all-gather.14.cloned.1.call-update) | async-done | bytes 8388624 | tf_op jit(solution)/shard_map/all_gather | solution.py:105
  191.4 32.8 all-gather.12.cloned.1.call-done
  227.1 43.8 %all-gather.18.cloned.1.call-done = bf16[512,2048]{1,0:T(8,128)(2,1)} async-done(((bf16[128,2048]{1,0:T(8,128)(2,1)}), bf16[512,2048]{1,0:T(8,128)(2,1)}) %all-gather.18.cloned.1.call-update) | async-done | bytes 2097168 | tf_op jit(solution)/shard_map/all_gather | solution.py:117
  274.8 14.5 while.36
  289.3 38.8 all-gather.20.cloned.1.call-done
  334.0 156.7 %all-gather.22.cloned.1.call-done = bf16[2048,8192]{1,0:T(8,128)(2,1)} async-done(((bf16[256,8192]{1,0:T(8,128)(2,1)}), bf16[2048,8192]{1,0:T(8,128)(2,1)}) %all-gather.22.cloned.1.call-update) | async-done | bytes 33554448 | tf_op jit(solution)/shard_map/all_gather | solution.py:169
  490.7 18.7 fusion.85
  509.4 144.0 %all-gather.24.cloned.1.call-done = bf16[2048,8192]{1,0:T(8,128)(2,1)} async-done(((bf16[256,8192]{1,0:T(8,128)(2,1)}), bf16[2048,8192]{1,0:T(8,128)(2,1)}) %all-gather.24.cloned.1.call-update) | async-done | bytes 33554448 | tf_op jit(solution)/shard_map/all_gather | solution.py:170
  653.5 21.9 multiply_convert_fusion.2
  675.4 140.8 %all-gather.26.cloned.1.call-done = bf16[8192,2048]{1,0:T(8,128)(2,1)} async-done(((bf16[1024,2048]{1,0:T(8,128)(2,1)}), bf16[8192,2048]{1,0:T(8,128)(2,1)}) %all-gather.26.cloned.1.call-update) | async-done | bytes 33554448 | tf_op jit(solution)/shard_map/all_gather | solution.py:171
  816.2 14.0 multiply_reduce_fusion.5
  832.3 19.8 multiply_convert_fusion.1
  852.1 17.5 convolution_add_fusion.1
  869.6 18.7 multiply_reduce_fusion.1
  891.2 7.3 convolution_convert_fusion
  901.8 30.9 while.37
  932.7 6.4 copy.90
  940.7 46.1 %fusion.18 = f32[2048,16384]{1,0:T(8,128)} fusion(bf16[128,2048]{1,0:T(8,128)(2,1)S(1)} %fusion.44, bf16[128,8192]{1,0:T(8,128)(2,1)} %get-tuple-element.637, bf16[128,8192]{1,0:T(8,128)(2,1)S(1)} %copy-done.9), kind=kOutput, calls=%fused_computation.43 | convolution fusion | flops 8598323200 | bytes 138936320 | tf_op jit(solution)/shard_map/dot_general | solution.py:54
  988.5 27.2 reduce-scatter.7.cloned.1.call-done
  1021.6 21.8 convolution_bitcast_fusion
  1043.3 49.5 %copy.100 = f32[2048,6144]{1,0:T(8,128)} copy(f32[2048,6144]{0,1:T(8,128)} %convolution_bitcast_fusion) | data formatting | bytes 100663296
  1094.1 8.4 fusion.87
  1104.1 26.7 fusion.86
  1131.5 41.3 all-reduce.9
  1175.2 7.2 convolution_add_fusion.4
  1182.4 6.8 convolution_add_fusion.3
  1192.8 1708.9 %all-reduce.12.cloned.1.call-done = f32[2048,16384]{1,0:T(8,128)} async-done(((f32[2048,16384]{1,0:T(8,128)}), f32[2048,16384]{1,0:T(8,128)}) %all-reduce.12.cloned.1.call-update) | async-done | bytes 134217744
  2906.6 432.6 %reduce-scatter.13.cloned.1.call-done = f32[64,6144]{1,0:T(8,128)} async-done(((f32[2048,6144]{1,0:T(8,128)}), f32[64,6144]{1,0:T(8,128)}) %reduce-scatter.13.cloned.1.call-update) | async-done | bytes 1572880
  3341.8 185.5 %reduce-scatter.9.cloned.1.call-done = f32[64,2048]{1,0:T(8,128)} async-done(((f32[2048,2048]{1,0:T(8,128)}), f32[64,2048]{1,0:T(8,128)}) %reduce-scatter.9.cloned.1.call-update) | async-done | bytes 524304 | tf_op jit(solution)/shard_map/reduce_scatter | solution.py:283
  3527.2 709.2 %reduce-scatter.11.cloned.1.call-done = f32[256,2048]{1,0:T(8,128)} async-done(((f32[8192,2048]{1,0:T(8,128)}), f32[256,2048]{1,0:T(8,128)}) %reduce-scatter.11.cloned.1.call-update) | async-done | bytes 2097168 | tf_op jit(solution)/shard_map/reduce_scatter | solution.py:199
  (262 shorter events, 118.8 us)
Async XLA Ops:
  7.2 58.7 %all-gather.10.cloned.1.call-start = ((), (), s32[]{:S(2)}) async-start(), calls=%async_computation.4 | async-start | bytes 9437184 | tf_op jit(solution)/shard_map/all_gather | solution.py:107
  7.9 114.3 %all-gather.16.cloned.1.call-start = ((), (), s32[]{:S(2)}) async-start(), calls=%async_computation.7 | async-start | bytes 9437184 | tf_op jit(solution)/shard_map/all_gather | solution.py:106
  8.7 169.9 %all-gather.14.cloned.1.call-start = ((), (), s32[]{:S(2)}) async-start(), calls=%async_computation.6 | async-start | bytes 9437184 | tf_op jit(solution)/shard_map/all_gather | solution.py:105
  9.4 214.8 %all-gather.12.cloned.1.call-start = ((), (), s32[]{:S(2)}) async-start(), calls=%async_computation.5 | async-start | bytes 2621440 | tf_op jit(solution)/shard_map/all_gather | solution.py:118
  10.7 173.6 %copy-start.18 = (f32[128,128]{1,0:T(8,128)}, f32[128,128]{1,0:T(8,128)S(1)}, u32[]{:S(2)}) copy-start(f32[128,128]{1,0:T(8,128)S(1)} %get-tuple-element.663) | copy-start | bytes 196612
  10.7 174.3 %copy-start.20 = (f32[128,128]{1,0:T(8,128)}, f32[128,128]{1,0:T(8,128)S(1)}, u32[]{:S(2)}) copy-start(f32[128,128]{1,0:T(8,128)S(1)} %get-tuple-element.662) | copy-start | bytes 196612
  10.7 111.5 %copy-start = (bf16[1,128,2048]{2,1,0:T(8,128)(2,1)S(1)}, bf16[1,128,2048]{2,1,0:T(8,128)(2,1)}, u32[]{:S(2)}) copy-start(bf16[1,128,2048]{2,1,0:T(8,128)(2,1)} %param.18) | copy-start | bytes 1572868
  71.5 55.4 %copy-start.24 = (f32[2048]{0:T(1024)S(1)}, f32[2048]{0:T(1024)}, u32[]{:S(2)}) copy-start(f32[2048]{0:T(1024)} %param.28) | copy-start | bytes 24580
  71.5 199.3 %all-gather.18.cloned.1.call-start = ((), (), s32[]{:S(2)}) async-start(), calls=%async_computation.8 | async-start | bytes 2621440 | tf_op jit(solution)/shard_map/all_gather | solution.py:117
  126.9 58.1 %copy-start.1 = (f32[128,2048]{1,0:T(8,128)}, f32[128,2048]{1,0:T(8,128)S(1)}, u32[]{:S(2)}) copy-start(f32[128,2048]{1,0:T(8,128)S(1)} %get-tuple-element.665) | copy-start | bytes 3145732
  127.0 58.1 %copy-start.30 = (f32[128]{0:T(128)}, f32[128]{0:T(128)S(1)}, u32[]{:S(2)}) copy-start(f32[128]{0:T(128)S(1)} %fusion.71) | copy-start | bytes 1540
  127.7 55.6 %copy-start.22 = (f32[2048]{0:T(1024)S(1)}, f32[2048]{0:T(1024)}, u32[]{:S(2)}) copy-start(f32[2048]{0:T(1024)} %param.27) | copy-start | bytes 24580
  187.5 140.5 %all-gather.20.cloned.1.call-start = ((), (), s32[]{:S(2)}) async-start(), calls=%async_computation.9 | async-start | bytes 9437184 | tf_op jit(solution)/shard_map/all_gather | solution.py:108
  188.1 302.7 %all-gather.22.cloned.1.call-start = ((), (), s32[]{:S(2)}) async-start(), calls=%async_computation.10 | async-start | bytes 37748736 | tf_op jit(solution)/shard_map/all_gather | solution.py:169
  188.8 464.6 %all-gather.24.cloned.1.call-start = ((), (), s32[]{:S(2)}) async-start(), calls=%async_computation.11 | async-start | bytes 37748736 | tf_op jit(solution)/shard_map/all_gather | solution.py:170
  189.6 626.6 %all-gather.26.cloned.1.call-start = ((), (), s32[]{:S(2)}) async-start(), calls=%async_computation.12 | async-start | bytes 37748736 | tf_op jit(solution)/shard_map/all_gather | solution.py:171
  190.3 825.3 %reduce-scatter.7.cloned.1.call-start = ((), (), s32[]{:S(2)}) async-start(), calls=%async_computation.13 | async-start | bytes 5242880 | tf_op jit(solution)/shard_map/reduce_scatter | solution.py:260
  289.2 43.5 %copy-start.11 = (bf16[128,2048]{0,1:T(8,128)(2,1)}, bf16[128,2048]{0,1:T(8,128)(2,1)S(1)}, u32[]{:S(2)}) copy-start(bf16[128,2048]{0,1:T(8,128)(2,1)S(1)} %get-tuple-element.397) | copy-start | bytes 1572868
  328.0 5.7 copy-start.27
  816.2 14.0 copy-start.15
  816.2 14.0 copy-start.26
  852.1 17.5 copy-start.6
  891.2 7.3 copy-start.13
  939.1 1962.6 %all-reduce.12.cloned.1.call-start = ((), (), s32[]{:S(2)}) async-start(), calls=%async_computation.17 | async-start | bytes 268435456
  986.8 30.4 copy-start.19
  986.8 2352.4 %reduce-scatter.13.cloned.1.call-start = ((), (), s32[]{:S(2)}) async-start(), calls=%async_computation.16 | async-start | bytes 51904512
  1092.9 2434.4 %reduce-scatter.9.cloned.1.call-start = ((), (), s32[]{:S(2)}) async-start(), calls=%async_computation.14 | async-start | bytes 17301504 | tf_op jit(solution)/shard_map/reduce_scatter | solution.py:283
  1102.5 3133.9 %reduce-scatter.11.cloned.1.call-start = ((), (), s32[]{:S(2)}) async-start(), calls=%async_computation.15 | async-start | bytes 69206016 | tf_op jit(solution)/shard_map/reduce_scatter | solution.py:199
  1130.8 44.4 %copy-start.10 = (f32[128,2048]{1,0:T(8,128)S(1)}, f32[128,2048]{1,0:T(8,128)}, u32[]{:S(2)}) copy-start(f32[128,2048]{1,0:T(8,128)} %get-tuple-element.674) | copy-start | bytes 3145732
  1175.2 14.0 slice-start
  1182.4 6.8 slice-start.1
  1182.4 6.8 copy-start.17
  (22 other events, 28.9 us)
Sparse Core Ops, SparseCore 0:
  9.9 55.9 all-gather.9
  67.8 54.3 all-gather.15
  124.1 54.3 all-gather.13
  180.5 43.6 all-gather.11
  226.2 44.6 all-gather.17
  272.6 55.3 all-gather.19
  329.9 160.7 all-gather.21
  492.6 160.7 all-gather.23
  655.3 160.7 all-gather.25
  939.2 76.3 reduce-scatter.6
  1023.2 1878.4 all-reduce.11
  2909.1 430.0 reduce-scatter.12
  3342.2 185.0 reduce-scatter.8
  3530.1 706.2 reduce-scatter.10
where the time goes:
time: 4260 us; the launch traced here: 4240 us
  waiting for transfers between devices  3780 us (89%)
  matrix products  270 us (6%)
  local copies, waits for them, and re-layouts  117 us (3%)
    unnamed x16, waiting for transfers between devices  2150 us
    reduce_scatter x1, waiting for transfers between devices, shards(): lax.psum_scatter(transpose_times(column_part, d_mlp_low), ('ctx', 'fsdp')...  709 us
    reduce_scatter x1, waiting for transfers between devices, shards(): lax.psum_scatter(out_term, ('ctx', 'fsdp'), scatter_dimension=0, tiled=True)  185 us
    all_gather x1, waiting for transfers between devices, shards(): lax.all_gather(w_gate, 'fsdp', axis=0, tiled=True)  157 us
    all_gather x1, waiting for transfers between devices, shards(): lax.all_gather(w_up, 'fsdp', axis=0, tiled=True)  144 us
    all_gather x1, waiting for transfers between devices, shards(): lax.all_gather(w_down, 'fsdp', axis=0, tiled=True)  141 us
    dot_general x4, matrix products, transpose_times(): lax.dot_general(left, right, (((0,), (0,)), ((), ())), preferred_element_...  103 us
  transfers between devices with their start and end apart: 14, of which 14 were waited for; matrix products, arithmetic and copies ran while one was open for 6% of the time, Pallas kernels for 0%

commit v1 on v0

v1 whole, which is shorter than its diff:
```python
import jax
import jax.numpy as jnp
from jax import lax
from jax.sharding import PartitionSpec as P

HD = 128


EPSILON = 1e-06
ROPE_BASE = 500000.0
NEGATIVE = -1e30


def norm_scale(values, gain_vec):
    return (
        values * lax.rsqrt(jnp.mean(values * values, axis=-1, keepdims=True) + EPSILON) * gain_vec
    )


def turn_half(values, cosine, sine):
    half_size = values.shape[-1] // 2
    turned = jnp.concatenate([-values[..., half_size:], values[..., :half_size]], axis=-1)
    return values * cosine + turned * sine


def angle_tables(positions, head_size):
    half_size = head_size // 2
    frequency = jnp.power(ROPE_BASE, -(jnp.arange(half_size).astype(jnp.float32) * 2.0 / head_size))
    angles = positions.astype(jnp.float32)[:, None] * frequency[None, :]
    angles = jnp.concatenate([angles, angles], axis=-1)
    return (jnp.cos(angles)[:, None, :], jnp.sin(angles)[:, None, :])


def row_positions(row_ids, pair_row, block_rows, ctx_count):
    rank_of = row_ids // (2 * block_rows)
    second = row_ids // block_rows % 2
    offset = row_ids % block_rows
    rank_match = (rank_of[:, None] == jnp.arange(ctx_count, dtype=jnp.int32)[None, :]).astype(
        jnp.int32
    )
    chosen = jnp.sum(rank_match * pair_row[None, :], axis=1)
    block_index = jnp.where(second == 0, chosen, 2 * ctx_count - 1 - chosen)
    return block_index * block_rows + offset


def times_transpose(left, right):
    return lax.dot_general(
        left, right, (((1,), (1,)), ((), ())), preferred_element_type=jnp.float32
    )


def transpose_times(left, right):
    return lax.dot_general(
        left, right, (((0,), (0,)), ((), ())), preferred_element_type=jnp.float32
    )


def activate(gate_in, up_in):
    return jax.nn.silu(gate_in) * up_in


def spread_rows(values, outer, inner):
    rows, width = values.shape
    return (
        values.reshape(outer, inner, rows // (outer * inner), width)
        .transpose(1, 0, 2, 3)
        .reshape(rows, width)
    )


def shards(
    tokens,
    block_pairs,
    w_query,
    w_key,
    w_value,
    w_out,
    w_gate,
    w_up,
    w_down,
    gain_query,
    gain_key,
    gain_attn,
    gain_mlp,
    cotangent,
):
    bf16 = jnp.bfloat16
    f32 = jnp.float32
    local_rows = tokens.shape[1]
    block_rows = local_rows // 2
    width = w_query.shape[1]
    hidden_width = w_gate.shape[1]
    ctx_count = lax.axis_size("ctx")
    fsdp_count = lax.axis_size("fsdp")
    ctx_index = lax.axis_index("ctx")
    seq = local_rows * ctx_count
    cols = width // ctx_count
    heads = cols // HD
    strip = hidden_width // (ctx_count * fsdp_count)
    hid = strip * fsdp_count
    scale = HD ** (-0.5)

    def ctx_cols(w):
        return lax.dynamic_slice_in_dim(w, ctx_index * cols, cols, 1)

    def ctx_strips(w):
        parts = w.reshape(w.shape[0], fsdp_count, ctx_count, strip)
        return lax.dynamic_index_in_dim(parts, ctx_index, 2, keepdims=False).reshape(w.shape[0], hid)

    token_rows = tokens[0]
    x_all = lax.all_gather(token_rows, "ctx", axis=0, tiled=True)
    qkv_w = lax.all_gather(
        jnp.concatenate([ctx_cols(w_query), ctx_cols(w_key), ctx_cols(w_value)], axis=1),
        "fsdp", axis=0, tiled=True,
    )
    out_w = lax.dynamic_slice_in_dim(
        lax.all_gather(w_out, "fsdp", axis=0, tiled=True), ctx_index * cols, cols, 0
    )
    gate_w = lax.all_gather(ctx_strips(w_gate), "fsdp", axis=0, tiled=True)
    up_w = lax.all_gather(ctx_strips(w_up), "fsdp", axis=0, tiled=True)
    down_w = lax.all_gather(
        lax.dynamic_slice_in_dim(w_down, ctx_index * strip, strip, 0), "fsdp", axis=0, tiled=True
    )

    pos = row_positions(jnp.arange(seq, dtype=jnp.int32), block_pairs[0], block_rows, ctx_count)
    cosine, sine = angle_tables(pos, HD)
    mask = pos[None, :] <= pos[:, None]
    gain_q = lax.dynamic_slice_in_dim(gain_query, ctx_index * cols, cols)
    gain_k = lax.dynamic_slice_in_dim(gain_key, ctx_index * cols, cols)

    qkv = jnp.dot(x_all, qkv_w, preferred_element_type=f32)
    q_raw, k_raw, v_raw = qkv[:, :cols], qkv[:, cols : 2 * cols], qkv[:, 2 * cols :]
    squares = jnp.stack([jnp.sum(q_raw * q_raw, axis=1), jnp.sum(k_raw * k_raw, axis=1)])
    squares = lax.psum(squares, "ctx")
    scales = lax.rsqrt(squares / width + EPSILON)
    c_q, c_k = scales[0][:, None], scales[1][:, None]

    def rope(v):
        return turn_half(v.reshape(seq, heads, HD), cosine, sine)

    def rope_back(w):
        w = w.reshape(seq, heads, HD)
        u = w * sine
        half = HD // 2
        turned = jnp.concatenate([u[..., half:], -u[..., :half]], axis=-1)
        return (w * cosine + turned).reshape(seq, cols)

    queries = rope(q_raw * c_q * gain_q).astype(bf16)
    keys = rope(k_raw * c_k * gain_k).astype(bf16)
    values = v_raw.astype(bf16).reshape(seq, heads, HD)
    scores = jnp.einsum("qhd,khd->hqk", queries, keys, preferred_element_type=f32) * scale
    scores = jnp.where(mask[None], scores, NEGATIVE)
    exponent = jnp.exp(scores - jnp.max(scores, axis=-1, keepdims=True))
    probs = exponent / jnp.sum(exponent, axis=-1, keepdims=True)
    prob_low = probs.astype(bf16)
    attended = (
        jnp.einsum("hqk,khd->qhd", prob_low, values, preferred_element_type=f32)
        .reshape(seq, cols)
        .astype(bf16)
    )
    branch = lax.psum_scatter(
        jnp.dot(attended, out_w, preferred_element_type=f32).astype(bf16),
        "ctx", scatter_dimension=0, tiled=True,
    ).astype(f32)
    mid = token_rows.astype(f32) + norm_scale(branch, gain_attn)
    mid_all = lax.all_gather(mid.astype(bf16), "ctx", axis=0, tiled=True)
    gate_act = jnp.dot(mid_all, gate_w, preferred_element_type=f32)
    up_act = jnp.dot(mid_all, up_w, preferred_element_type=f32)
    hidden = activate(gate_act, up_act).astype(bf16)
    mlp_out = lax.psum_scatter(
        jnp.dot(hidden, down_w, preferred_element_type=f32).astype(bf16),
        "ctx", scatter_dimension=0, tiled=True,
    ).astype(f32)
    output = (mid + norm_scale(mlp_out, gain_mlp)).astype(bf16)

    d_output = cotangent[0].astype(f32)
    unused_mlp, pull_mlp = jax.vjp(norm_scale, mlp_out, gain_mlp)
    d_mlp, grad_gm = pull_mlp(d_output)
    d_mlp_all = lax.all_gather(d_mlp.astype(bf16), "ctx", axis=0, tiled=True)
    d_hidden = times_transpose(d_mlp_all, down_w)
    unused_act, pull_act = jax.vjp(activate, gate_act, up_act)
    d_gate, d_up = pull_act(d_hidden)
    d_gate = d_gate.astype(bf16)
    d_up = d_up.astype(bf16)
    d_mid_part = times_transpose(d_gate, gate_w) + times_transpose(d_up, up_w)
    d_mid = d_output + lax.psum_scatter(
        d_mid_part.astype(bf16), "ctx", scatter_dimension=0, tiled=True
    ).astype(f32)

    down_sum = lax.psum_scatter(
        transpose_times(hidden, d_mlp_all).astype(bf16), "fsdp", scatter_dimension=0, tiled=True
    )
    moves = [
        (z * fsdp_count + f, f * ctx_count + z)
        for z in range(ctx_count)
        for f in range(fsdp_count)
    ]
    grad_down = lax.ppermute(down_sum, ("ctx", "fsdp"), moves).astype(f32)

    def column_grad(left, right):
        part = transpose_times(left, right).astype(bf16)
        mine = lax.psum_scatter(
            spread_rows(part, ctx_count, fsdp_count), "fsdp", scatter_dimension=0, tiled=True
        )
        mine = mine.reshape(ctx_count, mine.shape[0] // ctx_count, mine.shape[1])
        return lax.all_to_all(mine, "ctx", 0, 0, tiled=True)

    gate_up = column_grad(mid_all, jnp.concatenate([d_gate, d_up], axis=1))
    rows = gate_up.shape[1]

    def from_strips(part):
        return (
            part.reshape(ctx_count, rows, fsdp_count, strip)
            .transpose(1, 2, 0, 3)
            .reshape(rows, hidden_width)
            .astype(f32)
        )

    unused_branch, pull_branch = jax.vjp(norm_scale, branch, gain_attn)
    d_branch, grad_ga = pull_branch(d_mid)
    d_branch_all = lax.all_gather(d_branch.astype(bf16), "ctx", axis=0, tiled=True)
    d_attended = times_transpose(d_branch_all, out_w).astype(bf16).reshape(seq, heads, HD)
    grad_out = lax.psum_scatter(
        transpose_times(attended, d_branch_all).astype(bf16),
        "fsdp", scatter_dimension=0, tiled=True,
    ).astype(f32)

    d_values = jnp.einsum("hqk,qhd->khd", prob_low, d_attended, preferred_element_type=f32)
    d_values = d_values.astype(bf16).reshape(seq, cols)
    d_probs = jnp.einsum("qhd,khd->hqk", d_attended, values, preferred_element_type=f32)
    delta = jnp.sum(probs * d_probs, axis=-1, keepdims=True)
    d_scores = (probs * (d_probs - delta)).astype(bf16)
    d_queries = jnp.einsum("hqk,khd->qhd", d_scores, keys, preferred_element_type=f32) * scale
    d_keys = jnp.einsum("hqk,qhd->khd", d_scores, queries, preferred_element_type=f32) * scale
    dy_q = rope_back(d_queries)
    dy_k = rope_back(d_keys)
    dots = jnp.stack([
        jnp.sum(q_raw * gain_q * dy_q, axis=1), jnp.sum(k_raw * gain_k * dy_k, axis=1)
    ])
    dots = lax.psum(dots, "ctx") / width
    d_q = c_q * gain_q * dy_q - q_raw * (c_q * c_q * c_q * dots[0][:, None])
    d_k = c_k * gain_k * dy_k - k_raw * (c_k * c_k * c_k * dots[1][:, None])
    d_qkv = jnp.concatenate([d_q.astype(bf16), d_k.astype(bf16), d_values], axis=1)
    d_tokens = d_mid + lax.psum_scatter(
        times_transpose(d_qkv, qkv_w).astype(bf16), "ctx", scatter_dimension=0, tiled=True
    ).astype(f32)
    qkv_grad = column_grad(x_all, d_qkv).transpose(1, 0, 2)
    sum_gqk = lax.psum_scatter(
        jnp.stack([jnp.sum(dy_q * q_raw * c_q, axis=0), jnp.sum(dy_k * k_raw * c_k, axis=0)]),
        "fsdp", scatter_dimension=1, tiled=True,
    )
    sum_gam = lax.psum_scatter(
        jnp.stack([grad_ga, grad_gm]), ("ctx", "fsdp"), scatter_dimension=1, tiled=True
    )

    def whole(part):
        return part.reshape(part.shape[0], width).astype(f32)

    return (
        output[None],
        d_tokens.astype(bf16)[None],
        whole(qkv_grad[:, :, :cols]),
        whole(qkv_grad[:, :, cols : 2 * cols]),
        whole(qkv_grad[:, :, 2 * cols :]),
        grad_out,
        from_strips(gate_up[:, :, :hid]),
        from_strips(gate_up[:, :, hid:]),
        grad_down,
        sum_gqk[0],
        sum_gqk[1],
        sum_gam[0],
        sum_gam[1],
    )


def solution(mesh):
    in_specs = (
        P("fsdp", "ctx", None),
        P("fsdp", None),
        P("fsdp", None),
        P("fsdp", None),
        P("fsdp", None),
        P("fsdp", None),
        P("fsdp", None),
        P("fsdp", None),
        P("fsdp", None),
        P(),
        P(),
        P(),
        P(),
        P("fsdp", "ctx", None),
    )
    out_specs = (
        P("fsdp", "ctx", None),
        P("fsdp", "ctx", None),
        P(("ctx", "fsdp"), None),
        P(("ctx", "fsdp"), None),
        P(("ctx", "fsdp"), None),
        P(("ctx", "fsdp"), None),
        P(("ctx", "fsdp"), None),
        P(("ctx", "fsdp"), None),
        P(("ctx", "fsdp"), None),
        P(("ctx", "fsdp")),
        P(("ctx", "fsdp")),
        P(("ctx", "fsdp")),
        P(("ctx", "fsdp")),
    )
    return jax.shard_map(shards, mesh=mesh, in_specs=in_specs, out_specs=out_specs, check_vma=False)
```

time: 4260 us -> 1280 us (0.30)
  waiting for transfers between devices: 3780 us -> 958 us
  matrix products: 270 us -> 132 us
    unnamed x16 -> x21, waiting for transfers between devices: 2150 us -> 187 us
    reduce_scatter x3 -> x8, waiting for transfers between devices: 922 us -> 377 us  [the longest x2 105 us: column_grad(): lax.psum_scatter(spread_rows(part, ctx_count, fsdp_count), 'fsdp', scatte...]
    all_gather x8, waiting for transfers between devices: 675 us -> 364 us  [the longest x1 49 us: shards(): lax.all_gather(jnp.concatenate([ctx_cols(w_query), ctx_cols(w_key), ctx_c...]
    dot_general x4, matrix products: 103 us -> 35.1 us  [transpose_times(): lax.dot_general(left, right, (((0,), (0,)), ((), ())), preferred_element_...]
    unnamed x91 -> x68, local copies, waits for them, and re-layouts: 68.3 us -> 25.1 us
    dot_general x35 -> x10, matrix products: 85.6 us -> 51 us  [the longest x1 12.5 us: shards(): up_act = jnp.dot(mid_all, up_w, preferred_element_type=f32)]
  transfers between devices with their start and end apart: 14 -> 21, of which waited for: 14 -> 19; matrix products, arithmetic and copies ran while one was open for 6% -> 11% of each run, Pallas kernels for 0% -> 0%
where the time goes in v1:
time: 1280 us; the launch traced here: 1270 us
  waiting for transfers between devices  958 us (75%)
  matrix products  132 us (10%)
  local copies, waits for them, and re-layouts  78.4 us (6%)
  blocking collectives  38.1 us (3%)
  other arithmetic  35.5 us (3%)
  between operations  15 us (1%)
    unnamed x21, waiting for transfers between devices  187 us
    reduce_scatter x2, waiting for transfers between devices, column_grad(): lax.psum_scatter(spread_rows(part, ctx_count, fsdp_count), 'fsdp', scatte...  105 us
    reduce_scatter x1, waiting for transfers between devices, shards(): lax.psum_scatter(transpose_times(hidden, d_mlp_all).astype(bf16), 'fsdp',...  70.1 us
    all_gather x1, waiting for transfers between devices, shards(): lax.all_gather(jnp.concatenate([ctx_cols(w_query), ctx_cols(w_key), ctx_c...  49 us
    all_gather x1, waiting for transfers between devices, shards(): up_w = lax.all_gather(ctx_strips(w_up), 'fsdp', axis=0, tiled=True)  49 us
    all_gather x1, waiting for transfers between devices, shards(): mid_all = lax.all_gather(mid.astype(bf16), 'ctx', axis=0, tiled=True)  45.8 us
    all_gather x1, waiting for transfers between devices, shards(): lax.all_gather(d_branch.astype(bf16), 'ctx', axis=0, tiled=True)  45.7 us
    all_gather x1, waiting for transfers between devices, shards(): gate_w = lax.all_gather(ctx_strips(w_gate), 'fsdp', axis=0, tiled=True)  45.6 us
  transfers between devices with their start and end apart: 21, of which 19 were waited for; matrix products, arithmetic and copies ran while one was open for 11% of the time, Pallas kernels for 0%

profile of v1, /device:TPU:11, one launch (start us, length us, event | category | flops | bytes accessed | tf_op | source)
XLA Modules:
  0.0 1266.9 jit_solution(4619035155710057180)
XLA Ops:
  15.6 39.3 %all-gather.27.cloned.1.call-done = bf16[1,512,2048]{2,1,0:T(8,128)(2,1)} async-done(((bf16[1,128,2048]{2,1,0:T(8,128)(2,1)}), bf16[1,512,2048]{2,1,0:T(8,128)(2,1)}) %all-gather.27.cloned.1.call-update) | async-done | bytes 2097168 | tf_op jit(solution)/shard_map/all_gather | solution.py:111
  54.9 49.0 %all-gather.11.cloned.1.call-done = bf16[2048,1536]{1,0:T(8,128)(2,1)} async-done(((bf16[256,1536]{1,0:T(8,128)(2,1)}), bf16[2048,1536]{1,0:T(8,128)(2,1)}) %all-gather.11.cloned.1.call-update) | async-done | bytes 6291472 | tf_op jit(solution)/shard_map/all_gather | solution.py:112
  129.7 30.5 %all-gather.13.cloned.1.call-done = bf16[2048,2048]{1,0:T(8,128)(2,1)} async-done(((bf16[256,2048]{1,0:T(8,128)(2,1)}), bf16[2048,2048]{1,0:T(8,128)(2,1)}) %all-gather.13.cloned.1.call-update) | async-done | bytes 8388624 | tf_op jit(solution)/shard_map/all_gather | solution.py:117
  173.4 32.4 %reduce-scatter.15.cloned.1.call-done = bf16[128,2048]{1,0:T(8,128)(2,1)} async-done(((bf16[512,2048]{1,0:T(8,128)(2,1)}), bf16[128,2048]{1,0:T(8,128)(2,1)}) %reduce-scatter.15.cloned.1.call-update) | async-done | bytes 524304 | tf_op jit(solution)/shard_map/reduce_scatter | solution.py:161
  220.8 45.6 %all-gather.17.cloned.1.call-done = bf16[2048,2048]{0,1:T(8,128)(2,1)} async-done(((bf16[256,2048]{0,1:T(8,128)(2,1)}), bf16[2048,2048]{0,1:T(8,128)(2,1)}) %all-gather.17.cloned.1.call-update) | async-done | bytes 8388624 | tf_op jit(solution)/shard_map/all_gather | solution.py:119
  266.4 45.8 %all-gather.15.cloned.1.call-done = bf16[512,2048]{1,0:T(8,128)(2,1)} async-done(((bf16[128,2048]{1,0:T(8,128)(2,1)}), bf16[512,2048]{1,0:T(8,128)(2,1)}) %all-gather.15.cloned.1.call-update) | async-done | bytes 2097168 | tf_op jit(solution)/shard_map/all_gather | solution.py:166
  312.1 10.6 fusion.91
  322.7 49.0 %all-gather.19.cloned.1.call-done = bf16[2048,2048]{0,1:T(8,128)(2,1)} async-done(((bf16[256,2048]{0,1:T(8,128)(2,1)}), bf16[2048,2048]{0,1:T(8,128)(2,1)}) %all-gather.19.cloned.1.call-update) | async-done | bytes 8388624 | tf_op jit(solution)/shard_map/all_gather | solution.py:120
  371.7 12.5 multiply_convert_fusion.2
  384.3 44.5 %all-gather.21.cloned.1.call-done = bf16[2048,2048]{1,0:T(8,128)(2,1)} async-done(((bf16[256,2048]{1,0:T(8,128)(2,1)}), bf16[2048,2048]{1,0:T(8,128)(2,1)}) %all-gather.21.cloned.1.call-update) | async-done | bytes 8388624 | tf_op jit(solution)/shard_map/all_gather | solution.py:121
  428.8 9.8 convolution_convert_fusion.5
  438.7 41.2 %reduce-scatter.17.cloned.1.call-done = bf16[128,2048]{1,0:T(8,128)(2,1)} async-done(((bf16[512,2048]{1,0:T(8,128)(2,1)}), bf16[128,2048]{1,0:T(8,128)(2,1)}) %reduce-scatter.17.cloned.1.call-update) | async-done | bytes 524304 | tf_op jit(solution)/shard_map/reduce_scatter | solution.py:170
  485.6 45.5 %all-gather.23.cloned.1.call-done = bf16[512,2048]{1,0:T(8,128)(2,1)} async-done(((bf16[128,2048]{1,0:T(8,128)(2,1)}), bf16[512,2048]{1,0:T(8,128)(2,1)}) %all-gather.23.cloned.1.call-update) | async-done | bytes 2097168 | tf_op jit(solution)/shard_map/all_gather | solution.py:179
  531.1 12.0 multiply_convert_fusion.1
  543.2 8.5 fusion.92
  551.7 9.2 add_convert_fusion
  561.0 42.2 %reduce-scatter.19.cloned.1.call-done = bf16[128,2048]{1,0:T(8,128)(2,1)} async-done(((bf16[512,2048]{1,0:T(8,128)(2,1)}), bf16[128,2048]{1,0:T(8,128)(2,1)}) %reduce-scatter.19.cloned.1.call-update) | async-done | bytes 524304 | tf_op jit(solution)/shard_map/reduce_scatter | solution.py:186
  608.6 45.7 %all-gather.25.cloned.1.call-done = bf16[512,2048]{1,0:T(8,128)(2,1)} async-done(((bf16[128,2048]{1,0:T(8,128)(2,1)}), bf16[512,2048]{1,0:T(8,128)(2,1)}) %all-gather.25.cloned.1.call-update) | async-done | bytes 2097168 | tf_op jit(solution)/shard_map/all_gather | solution.py:221
  667.8 8.7 psum.15
  686.7 8.6 copy.92
  703.0 15.2 %convolution_convert_fusion = bf16[2048,4096]{1,0:T(8,128)(2,1)} fusion(bf16[512,2048]{1,0:T(8,128)(2,1)S(1)} %copy-done.23, bf16[512,2048]{1,0:T(8,128)(2,1)} %copy-done.27, bf16[512,2048]{1,0:T(8,128)(2,1)} %copy-done.28), kind=kOutput, calls=%fused_computation.1 | convolution fusion | flops 8606711808 | bytes 23068672 | tf_op jit(solution)/shard_map/dot_general | solution.py:53
  718.2 14.2 %copy.97 = bf16[4,8,64,4096]{3,2,0,1:T(8,128)(2,1)} copy(bf16[4,8,64,4096]{3,2,1,0:T(8,128)(2,1)} %bitcast.165) | data formatting | bytes 33554432 | tf_op jit(solution)/shard_map/reshape | solution.py:65
  734.0 8.5 convolution_convert_fusion.1
  749.4 7.5 convolution_convert_fusion.4
  756.9 7.5 reduce-scatter.23.cloned.1.call-done
  764.4 22.0 %all_to_all.10 = bf16[4,64,1536]{2,1,0:T(8,128)(2,1)} all-to-all(bf16[4,64,1536]{2,1,0:T(8,128)(2,1)} %bitcast.182), channel_id=1, replica_groups=mesh['ctx'=4,'fsdp'=8] {'ctx'}, dimensions={0} | all-to-all | bytes 1572864 | tf_op jit(solution)/shard_map/all_to_all | solution.py:206
  786.4 97.3 %reduce-scatter.27.cloned.1.call-done = bf16[256,4096]{1,0:T(8,128)(2,1)} async-done(((bf16[2048,4096]{1,0:T(8,128)(2,1)}), bf16[256,4096]{1,0:T(8,128)(2,1)}) %reduce-scatter.27.cloned.1.call-update) | async-done | bytes 2097168 | tf_op jit(solution)/shard_map/reduce_scatter | solution.py:202
  888.3 70.1 %reduce-scatter.29.cloned.1.call-done = bf16[256,2048]{1,0:T(8,128)(2,1)} async-done(((bf16[2048,2048]{1,0:T(8,128)(2,1)}), bf16[256,2048]{1,0:T(8,128)(2,1)}) %reduce-scatter.29.cloned.1.call-update) | async-done | bytes 1048592 | tf_op jit(solution)/shard_map/reduce_scatter | solution.py:190
  961.7 135.3 %reduce-scatter.33.cloned.1.call-done = f32[64,2]{1,0:T(8,128)} async-done(((f32[2048,2]{1,0:T(8,128)}), f32[64,2]{1,0:T(8,128)}) %reduce-scatter.33.cloned.1.call-update) | async-done | bytes 528
  1099.1 49.8 %reduce-scatter.31.cloned.1.call-done = f32[64,2]{1,0:T(8,128)} async-done(((f32[512,2]{1,0:T(8,128)}), f32[64,2]{1,0:T(8,128)}) %reduce-scatter.31.cloned.1.call-update) | async-done | bytes 528
  1150.9 43.7 %reduce-scatter.25.cloned.1.call-done = bf16[64,2048]{1,0:T(8,128)(2,1)} async-done(((bf16[512,2048]{1,0:T(8,128)(2,1)}), bf16[64,2048]{1,0:T(8,128)(2,1)}) %reduce-scatter.25.cloned.1.call-update) | async-done | bytes 262160 | tf_op jit(solution)/shard_map/reduce_scatter | solution.py:223
  1196.4 42.7 %reduce-scatter.21.cloned.1.call-done = bf16[128,2048]{1,0:T(8,128)(2,1)} async-done(((bf16[512,2048]{1,0:T(8,128)(2,1)}), bf16[128,2048]{1,0:T(8,128)(2,1)}) %reduce-scatter.21.cloned.1.call-update) | async-done | bytes 524304 | tf_op jit(solution)/shard_map/reduce_scatter | solution.py:244
  (187 shorter events, 147.6 us)
Async XLA Ops:
  7.2 5.6 copy-start.21
  7.2 47.7 %all-gather.27.cloned.1.call-start = ((), (), s32[]{:S(2)}) async-start(), calls=%async_computation.28 | async-start | bytes 2621440 | tf_op jit(solution)/shard_map/all_gather | solution.py:111
  7.9 95.9 %all-gather.11.cloned.1.call-start = ((), (), s32[]{:S(2)}) async-start(), calls=%async_computation.12 | async-start | bytes 7077888 | tf_op jit(solution)/shard_map/all_gather | solution.py:112
  10.5 149.7 %all-gather.13.cloned.1.call-start = ((), (), s32[]{:S(2)}) async-start(), calls=%async_computation.13 | async-start | bytes 9437184 | tf_op jit(solution)/shard_map/all_gather | solution.py:117
  11.2 194.6 %reduce-scatter.15.cloned.1.call-start = ((), (), s32[]{:S(2)}) async-start(), calls=%async_computation.14 | async-start | bytes 2621440 | tf_op jit(solution)/shard_map/reduce_scatter | solution.py:161
  164.6 101.8 %all-gather.17.cloned.1.call-start = ((), (), s32[]{:S(2)}) async-start(), calls=%async_computation.16 | async-start | bytes 9437184 | tf_op jit(solution)/shard_map/all_gather | solution.py:119
  164.6 42.4 %copy-start.19 = (f32[2048]{0:T(1024)S(1)}, f32[2048]{0:T(1024)}, u32[]{:S(2)}) copy-start(f32[2048]{0:T(1024)} %param.25) | copy-start | bytes 24580
  173.4 138.8 %all-gather.15.cloned.1.call-start = ((), (), s32[]{:S(2)}) async-start(), calls=%async_computation.15 | async-start | bytes 2621440 | tf_op jit(solution)/shard_map/all_gather | solution.py:166
  209.3 162.4 %all-gather.19.cloned.1.call-start = ((), (), s32[]{:S(2)}) async-start(), calls=%async_computation.17 | async-start | bytes 9437184 | tf_op jit(solution)/shard_map/all_gather | solution.py:120
  218.0 210.8 %all-gather.21.cloned.1.call-start = ((), (), s32[]{:S(2)}) async-start(), calls=%async_computation.18 | async-start | bytes 9437184 | tf_op jit(solution)/shard_map/all_gather | solution.py:121
  220.5 259.4 %reduce-scatter.17.cloned.1.call-start = ((), (), s32[]{:S(2)}) async-start(), calls=%async_computation.19 | async-start | bytes 2621440 | tf_op jit(solution)/shard_map/reduce_scatter | solution.py:170
  428.8 52.3 %copy-start.20 = (f32[2048]{0:T(1024)S(1)}, f32[2048]{0:T(1024)}, u32[]{:S(2)}) copy-start(f32[2048]{0:T(1024)} %param.26) | copy-start | bytes 24580
  438.7 92.5 %all-gather.23.cloned.1.call-start = ((), (), s32[]{:S(2)}) async-start(), calls=%async_computation.20 | async-start | bytes 2621440 | tf_op jit(solution)/shard_map/all_gather | solution.py:179
  485.2 118.0 %reduce-scatter.19.cloned.1.call-start = ((), (), s32[]{:S(2)}) async-start(), calls=%async_computation.21 | async-start | bytes 2621440 | tf_op jit(solution)/shard_map/reduce_scatter | solution.py:186
  543.2 8.5 copy-start.28
  543.2 8.5 copy-start.27
  560.9 93.4 %all-gather.25.cloned.1.call-start = ((), (), s32[]{:S(2)}) async-start(), calls=%async_computation.22 | async-start | bytes 2621440 | tf_op jit(solution)/shard_map/all_gather | solution.py:221
  608.4 155.9 %reduce-scatter.23.cloned.1.call-start = ((), (), s32[]{:S(2)}) async-start(), calls=%async_computation.24 | async-start | bytes 7077888 | tf_op jit(solution)/shard_map/reduce_scatter | solution.py:202
  701.4 182.3 %reduce-scatter.27.cloned.1.call-start = ((), (), s32[]{:S(2)}) async-start(), calls=%async_computation.26 | async-start | bytes 18874368 | tf_op jit(solution)/shard_map/reduce_scatter | solution.py:202
  732.4 225.9 %reduce-scatter.29.cloned.1.call-start = ((), (), s32[]{:S(2)}) async-start(), calls=%async_computation.27 | async-start | bytes 9437184 | tf_op jit(solution)/shard_map/reduce_scatter | solution.py:190
  742.5 354.5 %reduce-scatter.33.cloned.1.call-start = ((), (), s32[]{:S(2)}) async-start(), calls=%async_computation.30 | async-start | bytes 1081344
  743.9 404.9 %reduce-scatter.31.cloned.1.call-start = ((), (), s32[]{:S(2)}) async-start(), calls=%async_computation.29 | async-start | bytes 294912
  744.9 4.4 copy-start.15
  744.9 4.4 copy-start.17
  744.9 449.7 %reduce-scatter.25.cloned.1.call-start = ((), (), s32[]{:S(2)}) async-start(), calls=%async_computation.25 | async-start | bytes 2359296 | tf_op jit(solution)/shard_map/reduce_scatter | solution.py:223
  749.3 489.7 %reduce-scatter.21.cloned.1.call-start = ((), (), s32[]{:S(2)}) async-start(), calls=%async_computation.23 | async-start | bytes 2621440 | tf_op jit(solution)/shard_map/reduce_scatter | solution.py:244
  756.9 482.2 %copy-start.2 = (bf16[1,128,2048]{2,1,0:T(8,128)(2,1)S(1)}, bf16[1,128,2048]{2,1,0:T(8,128)(2,1)}, u32[]{:S(2)}) copy-start(bf16[1,128,2048]{2,1,0:T(8,128)(2,1)} %param.27) | copy-start | bytes 1572868
  756.9 482.2 %copy-start.5 = (bf16[128,2048]{1,0:T(8,128)(2,1)S(1)}, bf16[128,2048]{1,0:T(8,128)(2,1)}, u32[]{:S(2)}) copy-start(bf16[128,2048]{1,0:T(8,128)(2,1)} %reduce-scatter.19.cloned.1.call-done) | copy-start | bytes 1572868
  883.7 363.0 %all-to-all-start.1 = ((bf16[4,64,4096]{2,1,0:T(8,128)(2,1)}), bf16[4,64,4096]{2,1,0:T(8,128)(2,1)S(1)}, u32[]{:S(2)}, u32[]{:S(2)}) async-start(bf16[4,64,4096]{2,1,0:T(8,128)(2,1)} %bitcast.180), calls=%async_computation.8 | async-start | bytes 4194304 | tf_op jit(solution)/shard_map/all_to_all | solution.py:206
  958.4 282.8 %collective-permute-start = (bf16[256,2048]{1,0:T(8,128)(2,1)}, bf16[256,2048]{1,0:T(8,128)(2,1)}, u32[]{:S(2)}, u32[]{:S(2)}) collective-permute-start(bf16[256,2048]{1,0:T(8,128)(2,1)} %reduce-scatter.29.cloned.1.call-done), channel_id=1, source_target_pairs={{0,0},{1,4},{2,8},{3,12},{4,16},{5,20},{6,24},{7,28},{8,1},{9,5},{... | collective-permute-start | bytes 3145736 | tf_op jit(solution)/shard_map/ppermute | solution.py:198
  1239.0 4.9 copy-start.7
  1249.4 6.0 copy-start.4
  (18 other events, 35.4 us)
Sparse Core Ops, SparseCore 0:
  9.6 45.2 all-gather.26
  57.3 46.5 all-gather.10
  105.8 54.3 all-gather.12
  164.7 41.0 reduce-scatter.14
  208.2 58.0 all-gather.16
  268.5 43.6 all-gather.14
  314.7 56.9 all-gather.18
  374.4 54.3 all-gather.20
  438.8 41.0 reduce-scatter.16
  485.3 45.7 all-gather.22
  561.0 42.0 reduce-scatter.18
  608.5 45.7 all-gather.24
  701.5 62.7 reduce-scatter.22
  767.8 115.8 reduce-scatter.26
  887.0 71.2 reduce-scatter.28
  961.1 135.8 reduce-scatter.32
  1100.4 48.3 reduce-scatter.30
  1152.9 41.6 reduce-scatter.24
  1197.5 41.5 reduce-scatter.20

commit v2 on v1

--- a/solution.py
+++ b/solution.py
@@ -1,6 +1,10 @@
+import math
+
 import jax
 import jax.numpy as jnp
 from jax import lax
+from jax.experimental import pallas as pl
+from jax.experimental.pallas import tpu as pltpu
 from jax.sharding import PartitionSpec as P
 
 HD = 128
@@ -68,7 +72,7 @@
     )
 
 
-def shards(
+def shards_general(
     tokens,
     block_pairs,
     w_query,
@@ -273,6 +277,1315 @@
     )
 
 
+MESH = pl.DeviceIdType.MESH
+BF16 = jnp.bfloat16
+F32 = jnp.float32
+LINE = 4
+PLANE = 4
+
+
+def dot(left, right):
+    return lax.dot_general(left, right, (((1,), (0,)), ((), ())), preferred_element_type=F32)
+
+
+def dot_rt(left, right):
+    return lax.dot_general(left, right, (((1,), (1,)), ((), ())), preferred_element_type=F32)
+
+
+def dot_lt(left, right):
+    return lax.dot_general(left, right, (((0,), (0,)), ((), ())), preferred_element_type=F32)
+
+
+def exact(left, right, dims):
+    return lax.dot_general(
+        left, right, (dims, ((), ())), precision=lax.Precision.HIGHEST, preferred_element_type=F32
+    )
+
+
+def remote(src, dst, send, recv, device):
+    return pltpu.make_async_remote_copy(
+        src_ref=src, dst_ref=dst, send_sem=send, recv_sem=recv, device_id=device, device_id_type=MESH
+    )
+
+
+def at128(i, step=128):
+    return pl.ds(i if isinstance(i, int) else pl.multiple_of(i, step), step)
+
+
+class Place:
+    def __init__(self):
+        z = lax.axis_index("ctx")
+        f = lax.axis_index("fsdp")
+        self.z, self.f = z, f
+        self.p, self.k = f // 2, f % 2
+        self.p_x = self.p + 1 - 2 * (self.p % 2)
+        self.p_y = (self.p + 2) % PLANE
+        self.p_d = PLANE - 1 - self.p
+        self.partner = (z, 2 * self.p + 1 - self.k)
+        self.x = (z, 2 * self.p_x + self.k)
+        self.y = (z, 2 * self.p_y + self.k)
+        self.d = (z, 2 * self.p_d + self.k)
+        self.ends = z // 3 + (3 - z) // 3
+
+    def line(self, c):
+        return (c, self.f)
+
+    def order(self, s):
+        z, e, t = self.z, self.ends, s // 3
+        end = z + s * (1 - 2 * (z // 3))
+        mid = (1 - t) * (z + (3 * s * s - 5 * s) // 2) + t * 3 * (2 - z)
+        return e * end + (1 - e) * mid
+
+    def cross(self, c):
+        return (c, 2 * self.p + 1 - self.k)
+
+    def barrier(self, more=(), senders=()):
+        sem = pltpu.get_barrier_semaphore()
+
+        def greet(peer):
+            pl.semaphore_signal(sem, inc=1, device_id=peer, device_id_type=MESH)
+
+        peers = [self.partner, self.x, self.y] + list(more)
+        peers += [self.line((self.z + step) % LINE) for step in range(1, LINE)]
+        for peer in peers:
+            greet(peer)
+        count = len(peers)
+        for here, peer in senders:
+            pl.when(here)(lambda peer=peer: greet(peer))
+            count = count + here.astype(jnp.int32)
+        pl.semaphore_wait(sem, count)
+
+
+class Gather:
+    def __init__(self, place, buf, z_send, z_recv, c_send, c_recv):
+        self.pl, self.buf = place, buf
+        self.sems = z_send, z_recv, c_send, c_recv
+
+    def to_line(self, c, target, way):
+        z_send, z_recv, _, _ = self.sems
+        part = self.buf.at[c, self.pl.k]
+        return remote(part, part, z_send.at[way, c], z_recv.at[c], self.pl.line(target))
+
+    def to_core(self, c):
+        _, _, c_send, c_recv = self.sems
+        part = self.buf.at[c, self.pl.k]
+        return remote(part, part, c_send.at[c], c_recv.at[c], self.pl.partner)
+
+    def from_core(self, c):
+        _, _, c_send, c_recv = self.sems
+        part = self.buf.at[c, 1 - self.pl.k]
+        return remote(part, part, c_send.at[c], c_recv.at[c], self.pl.partner)
+
+    def start(self):
+        z = self.pl.z
+        pl.when(z < LINE - 1)(lambda: self.to_line(z, z + 1, 0).start())
+        pl.when(z > 0)(lambda: self.to_line(z, z - 1, 1).start())
+        self.to_core(z).start()
+
+    def arrive(self, c):
+        z = self.pl.z
+        self.to_line(c, z, 0).wait_recv()
+        pl.when(jnp.logical_and(c < z, z < LINE - 1))(lambda: self.to_line(c, z + 1, 0).start())
+        pl.when(jnp.logical_and(c > z, z > 0))(lambda: self.to_line(c, z - 1, 1).start())
+        self.to_core(c).start()
+
+    def arrive_first(self):
+        self.arrive(self.pl.order(1))
+        pl.when(self.pl.ends == 0)(lambda: self.arrive(self.pl.order(2)))
+
+    def arrive_second(self):
+        pl.when(self.pl.ends == 1)(lambda: self.arrive(self.pl.order(2)))
+
+    def arrive_third(self):
+        self.arrive(self.pl.order(3))
+
+    def ready(self, c):
+        self.from_core(c).wait_recv()
+
+    def finish(self):
+        z = self.pl.z
+
+        def body(c, carry):
+            pl.when(jnp.logical_and(c <= z, z < LINE - 1))(
+                lambda: self.to_line(c, z, 0).wait_send()
+            )
+            pl.when(jnp.logical_and(c >= z, z > 0))(lambda: self.to_line(c, z, 1).wait_send())
+            self.to_core(c).wait_send()
+            return carry
+
+        lax.fori_loop(0, LINE, body, 0)
+
+
+class RowSum:
+    def __init__(self, place, term, pair_out, pair_in, keep, mine, line_out, line_in, sems):
+        self.pl, self.term = place, term
+        self.pair_out, self.pair_in, self.keep, self.mine = pair_out, pair_in, keep, mine
+        self.line_out, self.line_in = line_out, line_in
+        self.p_send, self.p_recv, self.l_send, self.l_recv = sems
+
+    def pair(self, c):
+        return remote(
+            self.pair_out.at[c], self.pair_in.at[c], self.p_send.at[c], self.p_recv.at[c], self.pl.partner
+        )
+
+    def line(self, c, source):
+        return remote(
+            self.line_out.at[c], self.line_in.at[source], self.l_send.at[c], self.l_recv.at[source],
+            self.pl.line(c),
+        )
+
+    def give(self, c, s):
+        k = self.pl.k
+        self.pair_out[c] = self.term[1 - k].astype(BF16)
+        self.pair(c).start()
+        self.keep[s % 2] = self.term[k]
+
+    def pass_on(self, c, s):
+        z = self.pl.z
+        self.pair(c).wait_recv()
+
+        @pl.when(c != z)
+        def _():
+            self.line_out[c] = (self.keep[s % 2] + self.pair_in[c].astype(F32)).astype(BF16)
+            self.line(c, z).start()
+
+        @pl.when(c == z)
+        def _():
+            self.mine[...] = self.keep[s % 2] + self.pair_in[c].astype(F32)
+
+    def total(self):
+        z = self.pl.z
+        for step in range(1, LINE):
+            self.line((z + step) % LINE, (z + step) % LINE).wait_recv()
+        result = self.mine[...]
+        for step in range(1, LINE):
+            result = result + self.line_in[(z + step) % LINE].astype(F32)
+        return result
+
+    def finish(self):
+        z = self.pl.z
+
+        def body(c, carry):
+            self.pair(c).wait_send()
+            pl.when(c != z)(lambda: self.line(c, z).wait_send())
+            return carry
+
+        lax.fori_loop(0, LINE, body, 0)
+
+
+class Ring:
+    def __init__(self, place, buf, rows, send, recv):
+        self.pl, self.buf, self.rows = place, buf, rows
+        self.send, self.recv = send, recv
+
+    def block(self, p):
+        return self.buf.at[at128(p * self.rows, self.rows)]
+
+    def half(self, p, i):
+        size = self.rows // 2
+        return self.buf.at[at128(p * self.rows + i * size, size)]
+
+    def own(self, way):
+        part = self.block(self.pl.p)
+        return remote(part, part, self.send.at[way], self.recv.at[way], (self.pl.x, self.pl.y)[way])
+
+    def far(self, i):
+        part = self.half((self.pl.p_x, self.pl.p_y)[i], i)
+        return remote(part, part, self.send.at[2 + i], self.recv.at[2 + i], (self.pl.y, self.pl.x)[i])
+
+    def start(self):
+        self.own(0).start()
+        self.own(1).start()
+
+    def forward(self):
+        for i in range(2):
+            part = self.block((self.pl.p_x, self.pl.p_y)[i])
+            remote(part, part, self.send.at[i], self.recv.at[i], (self.pl.x, self.pl.y)[i]).wait_recv()
+            self.far(i).start()
+
+    def ready(self):
+        for i in range(2):
+            part = self.half(self.pl.p_d, i)
+            remote(part, part, self.send.at[2 + i], self.recv.at[2 + i], self.pl.x).wait_recv()
+
+    def finish(self):
+        for i in range(2):
+            self.own(i).wait_send()
+            self.far(i).wait_send()
+
+
+def scale_columns(totals, rows, which):
+    pick = (lax.broadcasted_iota(jnp.int32, (8, 128), 0) == which).astype(F32)
+    return exact(totals[:, rows], pick, ((0,), (0,)))
+
+
+def forward_kernel(
+    pairs, gains_qk, gain_attn, gain_mlp, tokens, cotangent,
+    w_query, w_key, w_value, w_out, w_gate, w_up, w_down,
+    o_out, o_dmlp, o_gm, o_branch, o_tot,
+    o_qkv, o_wo, o_g, o_u, o_dn, o_x, o_m, o_ga, o_ua, o_hid, o_raw, o_heads, o_probs, o_att, o_tab,
+    qkv, wo, wg, wu, wd, xs, ms, ga, ua, hid, raw, heads, probs, att, tab, posr, posc,
+    term, pair_out, pair_in, keep, mine, line_out, line_in,
+    sq_own, sq_pair, sq_both, sq_line, mid,
+    loc_sem, swap_send, swap_recv, ring_send, ring_recv, wo_send, wo_recv,
+    zs, zr, cs, cr, ps, pr, ls, lr, ts, tr, as_, ar, out_sem,
+):
+    place = Place()
+    z, f, p, k = place.z, place.f, place.p, place.k
+    rows = 128
+    width = 2048
+    cols = 256
+    seq = 512
+    place.barrier()
+
+    def own_rows(n):
+        return at128(n * (2 * p + k), n)
+
+    def strips(core):
+        return [1024 * (2 * q + core) + 256 * z for q in range(PLANE)]
+
+    local, swap = {}, {}
+
+    def split(name, w, buf, sources, first):
+        local[name], swap[name] = [], []
+        for i, (mine, theirs) in enumerate(sources):
+            dst = buf.at[own_rows(256), pl.ds(256 * i + first[1], 256)]
+            local[name].append(
+                pltpu.make_async_copy(w.at[:, at128(mine, 256)], dst, loc_sem.at[first[0] + i])
+            )
+            swap[name].append(
+                remote(
+                    w.at[:, at128(theirs, 256)], dst, swap_send.at[first[0] + i],
+                    swap_recv.at[first[0] + i], place.partner,
+                )
+            )
+
+    head_cols = [(256 * (2 * z + k), 256 * (2 * z + 1 - k))]
+    hid_cols = list(zip(strips(k), strips(1 - k)))
+    split("q", w_query, qkv, head_cols, (0, 0))
+    split("k", w_key, qkv, head_cols, (1, 256))
+    split("v", w_value, qkv, head_cols, (2, 512))
+    split("g", w_gate, wg, hid_cols, (3, 0))
+    split("u", w_up, wu, hid_cols, (7, 0))
+
+    def begin(*names):
+        for name in names:
+            for a, b in zip(local[name], swap[name]):
+                b.start()
+                a.start()
+
+    def settle(*names):
+        for name in names:
+            for a, b in zip(local[name], swap[name]):
+                a.wait()
+                b.wait_recv()
+
+    begin("q", "k", "v")
+    xs[z, k] = tokens[...]
+    gather_x = Gather(place, xs, zs.at[0], zr.at[0], cs.at[0], cr.at[0])
+    gather_x.start()
+    down_copy = pltpu.make_async_copy(
+        w_down.at[at128(256 * z, 256)], wd.at[at128(256 * p, 256)], loc_sem.at[11]
+    )
+    down_copy.start()
+    begin("g", "u")
+    ring_qkv = Ring(place, qkv, 512, ring_send.at[0], ring_recv.at[0])
+    ring_g = Ring(place, wg, 512, ring_send.at[1], ring_recv.at[1])
+    ring_u = Ring(place, wu, 512, ring_send.at[2], ring_recv.at[2])
+    ring_d = Ring(place, wd, 256, ring_send.at[3], ring_recv.at[3])
+    settle("q", "k", "v")
+    ring_qkv.start()
+
+    dx, dy = (p % 2 + z % 2) % 2, (p // 2 + z // 2) % 2
+    top, low = wo.at[pl.ds(0, 128)], wo.at[pl.ds(128, 128)]
+    wo_copy = pltpu.make_async_copy(w_out, wo, loc_sem.at[12])
+
+    def wo_send_to(i, part, device):
+        return remote(part, part, wo_send.at[i], wo_recv.at[i], device)
+
+    is_source = jnp.logical_and(dx == 0, dy == 0)
+    is_x = jnp.logical_and(dx == 1, dy == 0)
+    is_y = jnp.logical_and(dx == 0, dy == 1)
+    is_d = jnp.logical_and(dx == 1, dy == 1)
+
+    @pl.when(is_source)
+    def _():
+        wo_copy.start()
+
+    def positions(shape, axis):
+        i = lax.broadcasted_iota(jnp.int32, shape, axis)
+        block = i // 64
+        pos = jnp.zeros(shape, jnp.int32)
+        for r in range(LINE):
+            b = pairs[0, r]
+            pos = pos + jnp.where(block == 2 * r, b * 64, 0)
+            pos = pos + jnp.where(block == 2 * r + 1, (2 * LINE - 1 - b) * 64, 0)
+        return (pos + i % 64).astype(F32)
+
+    posr[k] = positions((8, seq), 1)
+    col = positions((seq, 128), 0)
+    posc[k] = col
+    lane = lax.broadcasted_iota(jnp.int32, (seq, 128), 1)
+    freq = jnp.exp((lane % 64).astype(F32) * (-2.0 / HD * math.log(ROPE_BASE)))
+    angle = col * freq
+    tab[0, k] = jnp.cos(angle)
+    sine = jnp.sin(angle)
+    tab[1, k] = jnp.where(lane < 64, -sine, sine)
+    tables = [
+        remote(r, r, ts.at[i], tr.at[i], place.partner)
+        for i, r in enumerate([posr.at[k], posc.at[k], tab.at[0, k], tab.at[1, k]])
+    ]
+    for t in tables:
+        t.start()
+
+    gather_x.arrive_first()
+    ring_qkv.forward()
+    settle("g")
+    ring_g.start()
+
+    @pl.when(is_source)
+    def _():
+        wo_copy.wait()
+        wo_send_to(0, top, place.x).start()
+        wo_send_to(1, low, place.y).start()
+
+    gather_x.arrive_second()
+    ring_qkv.ready()
+
+    def project(c):
+        gather_x.ready(c)
+        chunk = xs[c].reshape(2 * rows, width)
+        there = at128(c * rows)
+        sums = jnp.zeros((8, 2 * rows), F32)
+        pick = lax.broadcasted_iota(jnp.int32, (8, cols), 0)
+        for i in range(2):
+            part = dot(chunk, qkv[:, i * cols : (i + 1) * cols])
+            raw[i, :, there] = part.reshape(2, rows, cols)
+            sums = sums + exact((pick == i).astype(F32), part * part, ((1,), (1,)))
+        part = dot(chunk, qkv[:, 2 * cols :])
+        heads[2, :, there] = part.astype(BF16).reshape(2, rows, cols)
+        sq_own[c] = sums
+
+    def project_step(s, carry):
+        project(place.order(s))
+        return carry
+
+    lax.fori_loop(0, 2, project_step, 0)
+    pl.when(is_x)(lambda: wo_send_to(0, top, place.x).wait_recv())
+    pl.when(is_x)(lambda: wo_send_to(0, top, place.y).start())
+    pl.when(is_y)(lambda: wo_send_to(1, low, place.x).wait_recv())
+    pl.when(is_y)(lambda: wo_send_to(1, low, place.x).start())
+    gather_x.arrive_third()
+    lax.fori_loop(2, 4, project_step, 0)
+
+    pair_sq = remote(sq_own, sq_pair, as_.at[0], ar.at[0], place.partner)
+    pair_sq.start()
+    settle("u")
+    pair_sq.wait_recv()
+    sq_both[...] = sq_own[...] + sq_pair[...]
+
+    def line_sq(step, source):
+        return remote(
+            sq_both, sq_line.at[source], as_.at[step], ar.at[1 + source],
+            place.line((z + step) % LINE),
+        )
+
+    for step in range(1, LINE):
+        line_sq(step, z).start()
+    for t in tables:
+        t.wait_recv()
+    for step in range(1, LINE):
+        line_sq(step, (z + step) % LINE).wait_recv()
+    sq_line[z] = sq_both[...]
+    total = (sq_line[0] + sq_line[1]) + (sq_line[2] + sq_line[3])
+    scales = lax.rsqrt(total / width + EPSILON)
+    o_tot[...] = scales
+
+    def rotate(c, carry):
+        there = at128(c * rows)
+        now = o_tot[c]
+        for i in range(2):
+            pick = (lax.broadcasted_iota(jnp.int32, (8, 128), 0) == i).astype(F32)
+            column = exact(now, pick, ((0,), (0,)))
+            for s in range(2):
+                for h in range(2):
+                    lanes = slice(128 * h, 128 * h + 128)
+                    v = raw[i, s, there, lanes] * column[128 * s : 128 * s + 128]
+                    v = v * gains_qk[i : i + 1, lanes]
+                    v = v * tab[0, s, there] + pltpu.roll(v, 64, 1) * tab[1, s, there]
+                    heads[i, s, there, lanes] = v.astype(BF16)
+        return carry
+
+    lax.fori_loop(0, LINE, rotate, 0)
+
+    def attend(s, carry):
+        mask = posr[s, 0:1, :] <= posc[s][:, 0:1]
+        for h in range(2):
+            lanes = slice(128 * h, 128 * h + 128)
+            scores = dot_rt(heads[0, s, :, lanes], heads[1, s, :, lanes]) * (HD ** -0.5)
+            scores = jnp.where(mask, scores, NEGATIVE)
+            e = jnp.exp(scores - jnp.max(scores, axis=1, keepdims=True))
+            low_p = (e / jnp.sum(e, axis=1, keepdims=True)).astype(BF16)
+            probs[s, h] = low_p
+            att[s, :, lanes] = dot(low_p, heads[2, s, :, lanes]).astype(BF16)
+        return carry
+
+    lax.fori_loop(0, 2, attend, 0)
+
+    ring_g.forward()
+    ring_u.start()
+
+    @pl.when(is_d)
+    def _():
+        wo_send_to(0, top, place.x).wait_recv()
+        wo_send_to(0, top, place.x).start()
+        wo_send_to(1, low, place.x).wait_recv()
+        wo_send_to(1, low, place.y).start()
+
+    pl.when(is_x)(lambda: wo_send_to(1, low, place.x).wait_recv())
+    pl.when(is_y)(lambda: wo_send_to(0, top, place.x).wait_recv())
+
+    sums = RowSum(place, term, pair_out, pair_in, keep, mine, line_out, line_in, (ps, pr, ls, lr))
+
+    def tiles(c, left, weight):
+        def body(t, carry):
+            lanes = at128(t * 512, 512)
+            term[:, :, lanes] = dot(left, weight[:, lanes]).reshape(2, rows, 512)
+            return carry
+
+        lax.fori_loop(0, 4, body, 0)
+
+    def branch_step(s, carry):
+        c = place.order(3 - s)
+        there = at128(c * rows)
+        tiles(c, att[:, there].reshape(2 * rows, cols), wo)
+        sums.give(c, s)
+        pl.when(s > 0)(lambda: sums.pass_on(place.order(4 - s), s + 1))
+        return carry
+
+    lax.fori_loop(0, 4, branch_step, 0)
+    sums.pass_on(z, 3)
+    ring_u.forward()
+    down_copy.wait()
+    ring_d.start()
+    branch = sums.total()
+    sums.finish()
+    o_branch[...] = branch
+
+    def mean_sq(v):
+        return jnp.sum(v * v, axis=1, keepdims=True) / width
+
+    mid[...] = tokens[...].astype(F32) + branch * lax.rsqrt(mean_sq(branch) + EPSILON) * gain_attn[...]
+    ms[z, k] = mid[...].astype(BF16)
+    gather_m = Gather(place, ms, zs.at[1], zr.at[1], cs.at[1], cr.at[1])
+    gather_m.start()
+
+    ring_g.ready()
+    ring_u.ready()
+
+    def expand(s, carry):
+        c = place.order(s)
+        gather_m.ready(c)
+        chunk = ms[c].reshape(2 * rows, width)
+
+        def body(t, inner):
+            lanes = at128(t * 256, 256)
+            g = dot(chunk, wg[:, lanes])
+            u = dot(chunk, wu[:, lanes])
+            ga[c, :, lanes] = g.astype(BF16)
+            ua[c, :, lanes] = u.astype(BF16)
+            hid[c, :, lanes] = (g / (1.0 + jnp.exp(-g)) * u).astype(BF16)
+            return inner
+
+        lax.fori_loop(0, 4, body, 0)
+        return carry
+
+    def contract(s, carry):
+        c = place.order(s)
+        tiles(c, hid[c], wd)
+        sums.give(c, s)
+        pl.when(s > 0)(lambda: sums.pass_on(place.order(s - 1), s + 1))
+        return carry
+
+    lax.fori_loop(0, 1, expand, 0)
+    gather_m.arrive_first()
+    lax.fori_loop(1, 2, expand, 0)
+    ring_d.forward()
+    gather_m.arrive_second()
+    lax.fori_loop(2, 3, expand, 0)
+    ring_d.ready()
+    lax.fori_loop(0, 3, contract, 0)
+    gather_m.arrive_third()
+    lax.fori_loop(3, 4, expand, 0)
+    lax.fori_loop(3, 4, contract, 0)
+    sums.pass_on(place.order(3), 3)
+
+    saves = [
+        (qkv, o_qkv), (wo, o_wo), (wg, o_g), (wu, o_u), (wd, o_dn), (xs, o_x), (ms, o_m), (ga, o_ga),
+        (ua, o_ua), (hid, o_hid), (raw, o_raw), (heads, o_heads), (probs, o_probs), (att, o_att),
+        (tab, o_tab),
+    ]
+    copies = [pltpu.make_async_copy(a, b, out_sem.at[i]) for i, (a, b) in enumerate(saves)]
+    for copy in copies:
+        copy.start()
+
+    mlp = sums.total()
+    sums.finish()
+    c_m = lax.rsqrt(mean_sq(mlp) + EPSILON)
+    gain = gain_mlp[...]
+    o_out[...] = (mid[...] + mlp * c_m * gain).astype(BF16)
+    dy = cotangent[...].astype(F32)
+    gdy = gain * dy
+    inner = jnp.sum(mlp * gdy, axis=1, keepdims=True) / width
+    o_dmlp[...] = (c_m * gdy - mlp * (c_m * c_m * c_m * inner)).astype(BF16)
+    o_gm[...] = jnp.sum(dy * mlp * c_m, axis=0, keepdims=True)
+
+    gather_x.finish()
+    gather_m.finish()
+    for ring in (ring_qkv, ring_g, ring_u, ring_d):
+        ring.finish()
+    for group in swap.values():
+        for copy in group:
+            copy.wait_send()
+    for t in tables:
+        t.wait_send()
+    pair_sq.wait_send()
+    for step in range(1, LINE):
+        line_sq(step, z).wait_send()
+
+    @pl.when(is_source)
+    def _():
+        wo_send_to(0, top, place.x).wait_send()
+        wo_send_to(1, low, place.y).wait_send()
+
+    pl.when(is_x)(lambda: wo_send_to(0, top, place.y).wait_send())
+    pl.when(is_y)(lambda: wo_send_to(1, low, place.x).wait_send())
+
+    @pl.when(is_d)
+    def _():
+        wo_send_to(0, top, place.x).wait_send()
+        wo_send_to(1, low, place.y).wait_send()
+
+    for copy in copies:
+        copy.wait()
+
+
+def any_spec():
+    return pl.BlockSpec(memory_space=pl.ANY)
+
+
+def vmem_spec():
+    return pl.BlockSpec(memory_space=pltpu.VMEM)
+
+
+def run_forward(pairs, gains_qk, gain_attn, gain_mlp, tokens, cotangent, weights):
+    shape = jax.ShapeDtypeStruct
+    dma = pltpu.SemaphoreType.DMA
+    kept = [
+        shape((2048, 768), BF16),
+        shape((256, 2048), BF16),
+        shape((2048, 1024), BF16),
+        shape((2048, 1024), BF16),
+        shape((1024, 2048), BF16),
+        shape((4, 2, 128, 2048), BF16),
+        shape((4, 2, 128, 2048), BF16),
+        shape((4, 256, 1024), BF16),
+        shape((4, 256, 1024), BF16),
+        shape((4, 256, 1024), BF16),
+        shape((2, 2, 512, 256), F32),
+        shape((3, 2, 512, 256), BF16),
+        shape((2, 2, 512, 512), BF16),
+        shape((2, 512, 256), BF16),
+        shape((2, 2, 512, 128), F32),
+    ]
+    return pl.pallas_call(
+        forward_kernel,
+        name="forward",
+        out_shape=[
+            shape((128, 2048), BF16),
+            shape((128, 2048), BF16),
+            shape((1, 2048), F32),
+            shape((128, 2048), F32),
+            shape((4, 8, 256), F32),
+        ]
+        + kept,
+        in_specs=[pl.BlockSpec(memory_space=pltpu.SMEM)] + [vmem_spec()] * 5 + [any_spec()] * 7,
+        out_specs=[vmem_spec()] * 5 + [any_spec()] * len(kept),
+        scratch_shapes=[pltpu.VMEM(k.shape, k.dtype) for k in kept]
+        + [
+            pltpu.VMEM((2, 8, 512), F32),
+            pltpu.VMEM((2, 512, 128), F32),
+            pltpu.VMEM((2, 128, 2048), F32),
+            pltpu.VMEM((4, 128, 2048), BF16),
+            pltpu.VMEM((4, 128, 2048), BF16),
+            pltpu.VMEM((2, 128, 2048), F32),
+            pltpu.VMEM((128, 2048), F32),
+            pltpu.VMEM((4, 128, 2048), BF16),
+            pltpu.VMEM((4, 128, 2048), BF16),
+            pltpu.VMEM((4, 8, 256), F32),
+            pltpu.VMEM((4, 8, 256), F32),
+            pltpu.VMEM((4, 8, 256), F32),
+            pltpu.VMEM((4, 4, 8, 256), F32),
+            pltpu.VMEM((128, 2048), F32),
+            dma((13,)),
+            dma((11,)),
+            dma((11,)),
+            dma((4, 4)),
+            dma((4, 4)),
+            dma((2,)),
+            dma((2,)),
+            dma((2, 2, 4)),
+            dma((2, 4)),
+            dma((2, 4)),
+            dma((2, 4)),
+            dma((4,)),
+            dma((4,)),
+            dma((4,)),
+            dma((4,)),
+            dma((4,)),
+            dma((4,)),
+            dma((4,)),
+            dma((5,)),
+            dma((len(kept),)),
+        ],
+        compiler_params=pltpu.CompilerParams(
+            collective_id=0, has_side_effects=True, vmem_limit_bytes=64 * 1024 * 1024
+        ),
+    )(pairs, gains_qk, gain_attn, gain_mlp, tokens, cotangent, *weights)
+
+
+def backward_kernel(
+    gains_qk, gain_attn, d_mlp, cotangent, branch, scales, gm_part,
+    h_qkv, h_wo, h_g, h_u, h_dn, h_x, h_m, h_ga, h_ua, h_hid, h_raw, h_heads, h_probs, h_att, h_tab,
+    o_tok, o_gains, o_down, o_out, o_gu, o_qkv,
+    st_dn, rc_dn, st_gu, rc_gu, st_qkv, rc_qkv, st_out, rc_out,
+    wd, wg, wu, ga, ua, hid, dm, dg, du, ms, db, raw, tab, datt, dy,
+    term, pair_out, pair_in, keep, mine, line_out, line_in,
+    sq_own, sq_pair, sq_both, sq_line, gn_own, gn_in, d_mid, stage, stage_d,
+    ld, zs, zr, cs, cr, ps, pr, ls, lr, as_, ar, gs, gr, in_send, in_recv, st_sem, sum_sem,
+    fin_send, fin_recv, fin_loc, al_send, al_recv, al_loc,
+):
+    place = Place()
+    z, f, p, k = place.z, place.f, place.p, place.k
+    rows, width, cols = 128, 2048, 256
+
+    down_to = ((p - z + LINE) % LINE, 4 * k + z)
+    down_from = (f % 4, 2 * ((z + f % 4) % LINE) + f // 4)
+    down_moves = jnp.logical_or(down_to[0] != z, down_to[1] != f)
+    out_to = (z, 4 * k + p)
+    out_from = (z, 2 * (f % 4) + f // 4)
+    out_moves = out_to[1] != f
+    place.barrier(
+        [place.d] + [place.cross((z + step) % LINE) for step in range(1, LINE)],
+        [(down_moves, down_from), (out_moves, out_from)],
+    )
+
+    loads = {}
+
+    def load(name, src, dst):
+        loads[name] = pltpu.make_async_copy(src, dst, ld.at[len(loads)])
+        loads[name].start()
+
+    dm[at128(z * 256 + k * rows)] = d_mlp[...]
+
+    class Rows:
+        def __init__(self, ref):
+            self.ref = ref
+
+        @property
+        def at(self):
+            ref = self.ref
+
+            class At:
+                def __getitem__(self, key):
+                    c, core = key
+                    return ref.at[at128(c * 256 + core * rows)]
+
+            return At()
+
+    gather_d = Gather(place, Rows(dm), zs.at[0], zr.at[0], cs.at[0], cr.at[0])
+    gather_d.start()
+    load("wd", h_dn, wd)
+    load("ga", h_ga, ga)
+    load("ua", h_ua, ua)
+    load("wg", h_g, wg)
+    load("wu", h_u, wu)
+    load("hid", h_hid, hid)
+    load("ms", h_m, ms)
+    load("raw", h_raw, raw)
+    load("tab", h_tab, tab)
+
+    sums = RowSum(place, term, pair_out, pair_in, keep, mine, line_out, line_in, (ps, pr, ls, lr))
+
+    def chunk_rows(c):
+        return at128(c * 256, 256)
+
+    def ffn(s, carry):
+        c = place.order(s)
+        gather_d.ready(c)
+        here = chunk_rows(c)
+        grad = dm[here]
+
+        def act(t, inner):
+            lanes = at128(t * 256, 256)
+            dh = dot_rt(grad, wd[lanes])
+            g = ga[here, lanes].astype(F32)
+            u = ua[here, lanes].astype(F32)
+            sig = 1.0 / (1.0 + jnp.exp(-g))
+            dg[here, lanes] = (dh * u * sig * (1.0 + g * (1.0 - sig))).astype(BF16)
+            du[here, lanes] = (dh * g * sig).astype(BF16)
+            return inner
+
+        lax.fori_loop(0, 4, act, 0)
+        left_g, left_u = dg[here], du[here]
+
+        def back(t, inner):
+            lanes = at128(t * 512, 512)
+            part = dot_rt(left_g, wg[lanes]) + dot_rt(left_u, wu[lanes])
+            term[:, :, lanes] = part.reshape(2, rows, 512)
+            return inner
+
+        lax.fori_loop(0, 4, back, 0)
+        sums.give(c, s)
+        pl.when(s > 0)(lambda: sums.pass_on(place.order(s - 1), s + 1))
+        return carry
+
+    for name in ("wd", "ga", "ua", "wg", "wu"):
+        loads[name].wait()
+    lax.fori_loop(0, 1, ffn, 0)
+    gather_d.arrive_first()
+    lax.fori_loop(1, 2, ffn, 0)
+    gather_d.arrive_second()
+    lax.fori_loop(2, 3, ffn, 0)
+    gather_d.arrive_third()
+    lax.fori_loop(3, 4, ffn, 0)
+    sums.pass_on(place.order(3), 3)
+    load("x", h_x, wd)
+    load("qkv", h_qkv, wg.at[:, pl.ds(0, 768)])
+    load("probs", h_probs, wu.at[:, pl.ds(0, 512)])
+    load("qk", h_heads.at[pl.ds(0, 2048)], wu.at[:, pl.ds(512, 256)])
+    load("v", h_heads.at[pl.ds(2048, 1024)], wu.at[pl.ds(0, 1024), pl.ds(768, 256)])
+    load("att", h_att, wu.at[pl.ds(1024, 1024), pl.ds(768, 256)])
+
+    chips = [place.p_x, place.p_y, place.p_d, p]
+    near = [place.x, place.y, place.d]
+
+    def send_part(kind, i, src, dst):
+        return remote(src.at[i], dst.at[i], in_send.at[kind, i], in_recv.at[kind, i], near[i])
+
+    loads["hid"].wait()
+    order = (2, 0, 1, 3)
+    for n, i in enumerate(order):
+        strip = hid[:, at128(((chips[i] - z + LINE) % LINE) * 256, 256)]
+
+        def down(t, carry, strip=strip):
+            lanes = at128(t * 512, 512)
+            stage_d[:, lanes] = dot_lt(strip, dm[:, lanes]).astype(BF16)
+            return carry
+
+        lax.fori_loop(0, 4, down, 0)
+        copy = pltpu.make_async_copy(stage_d, st_dn.at[i], st_sem.at[0])
+        copy.start()
+        copy.wait()
+        if i < 3:
+            send_part(0, i, st_dn, rc_dn).start()
+
+    load("wo", h_wo, stage_d)
+    loads["ms"].wait()
+
+    def feature_rows(ref, chip):
+        return jnp.concatenate([ref[:, at128(512 * c + 128 * chip)] for c in range(LINE)], axis=1)
+
+    for n, i in enumerate(order):
+        left = feature_rows(ms, chips[i])
+        for m, right in enumerate((dg, du)):
+
+            def both(t, carry, left=left, right=right, m=m):
+                lanes = at128(t * 256, 256)
+                stage[m, :, lanes] = dot_lt(left, right[:, lanes]).astype(BF16)
+                return carry
+
+            lax.fori_loop(0, 4, both, 0)
+            copy = pltpu.make_async_copy(stage.at[m], st_gu.at[i, m], st_sem.at[1 + m])
+            copy.start()
+        for m in range(2):
+            pltpu.make_async_copy(stage.at[m], st_gu.at[i, m], st_sem.at[1 + m]).wait()
+        if i < 3:
+            send_part(1, i, st_gu, rc_gu).start()
+
+    gather_d.finish()
+
+    def mean_of(v):
+        return jnp.sum(v, axis=1, keepdims=True) / width
+
+    d_mid[...] = cotangent[...].astype(F32) + sums.total()
+    sums.finish()
+    b = branch[...]
+    c_b = lax.rsqrt(mean_of(b * b) + EPSILON)
+    gdy = gain_attn[...] * d_mid[...]
+    db[at128(z * 256 + k * rows)] = (
+        c_b * gdy - b * (c_b * c_b * c_b * mean_of(b * gdy))
+    ).astype(BF16)
+    gather_b = Gather(place, Rows(db), zs.at[1], zr.at[1], cs.at[1], cr.at[1])
+    gather_b.start()
+    gn_own[...] = jnp.zeros((8, width), F32)
+    gn_own[2:3, :] = jnp.sum(d_mid[...] * b * c_b, axis=0, keepdims=True)
+    gn_own[3:4, :] = gm_part[...]
+
+    for name in ("wo", "raw", "tab", "x", "qkv", "probs", "qk", "v", "att"):
+        loads[name].wait()
+
+    def attended_step(s, carry):
+        c = place.order(s)
+        gather_b.ready(c)
+        part = dot_rt(db[chunk_rows(c)], stage_d[...]).astype(BF16)
+        datt[:, at128(c * rows)] = part.reshape(2, rows, cols)
+        return carry
+
+    gather_b.arrive_first()
+    lax.fori_loop(0, 2, attended_step, 0)
+
+    for i in range(3):
+        send_part(0, i, st_dn, rc_dn).wait_recv()
+    parts = [rc_dn.at[0], rc_dn.at[1], rc_dn.at[2], st_dn.at[3]]
+    gather_b.arrive_second()
+    copies = [
+        pltpu.make_async_copy(src, ms.at[pl.ds(256 * i, 256)], sum_sem.at[i])
+        for i, src in enumerate(parts)
+    ]
+    for copy in copies:
+        copy.start()
+    for copy in copies:
+        copy.wait()
+
+    def add_down(t, carry):
+        lanes = at128(t * 512, 512)
+        acc = ms[0:256, lanes].astype(F32)
+        for i in range(1, 4):
+            acc = acc + ms[256 * i : 256 * i + 256, lanes].astype(F32)
+        dm[0:256, lanes] = acc.astype(BF16)
+        return carry
+
+    lax.fori_loop(0, 4, add_down, 0)
+    down_done = dm.at[pl.ds(0, 256)]
+    fin_down = remote(down_done, o_down, fin_send.at[0], fin_recv.at[0], down_to)
+    keep_down = pltpu.make_async_copy(down_done, o_down, fin_loc.at[0])
+    pl.when(down_moves)(lambda: fin_down.start())
+    pl.when(jnp.logical_not(down_moves))(lambda: keep_down.start())
+
+    lax.fori_loop(2, 3, attended_step, 0)
+    gather_b.arrive_third()
+    lax.fori_loop(3, 4, attended_step, 0)
+
+    def attend(s, carry):
+        there = at128(s * 512, 512)
+        for h in range(2):
+            lanes = slice(128 * h, 128 * h + 128)
+            more = slice(512 + 128 * h, 640 + 128 * h)
+            vals = slice(768 + 128 * h, 896 + 128 * h)
+            low_p = wu[at128((2 * s + h) * 512, 512), 0:512]
+            grad = datt[s, :, lanes]
+            q = wu[there, more]
+            key = wu[at128(1024 + s * 512, 512), more]
+            value = wu[there, vals]
+            d_value = dot_lt(low_p, grad).astype(BF16)
+            d_probs = dot_rt(grad, value)
+            pr32 = low_p.astype(F32)
+            delta = jnp.sum(pr32 * d_probs, axis=1, keepdims=True)
+            d_scores = (pr32 * (d_probs - delta)).astype(BF16)
+            d_q = dot(d_scores, key) * (HD ** -0.5)
+            d_k = dot_lt(d_scores, q) * (HD ** -0.5)
+            for i, d in enumerate((d_q, d_k)):
+                dy[i, s, :, lanes] = d * tab[0, s] - pltpu.roll(d, 64, 1) * tab[1, s]
+            for c in range(LINE):
+                ga[c * 256 + s * rows : c * 256 + s * rows + rows, vals.start - 256 : vals.stop - 256] = (
+                    d_value[c * rows : c * rows + rows]
+                )
+        return carry
+
+    for s in range(2):
+        attend(s, 0)
+
+    def dots_step(c, carry):
+        there = at128(c * rows)
+        pick = lax.broadcasted_iota(jnp.int32, (8, cols), 0)
+        acc = jnp.zeros((8, 2 * rows), F32)
+        for i in range(2):
+            part = (raw[i, :, there] * dy[i, :, there]).reshape(2 * rows, cols) * gains_qk[i : i + 1]
+            acc = acc + exact((pick == i).astype(F32), part, ((1,), (1,)))
+        sq_own[c] = acc
+        return carry
+
+    lax.fori_loop(0, LINE, dots_step, 0)
+    pair_sq = remote(sq_own, sq_pair, as_.at[0], ar.at[0], place.partner)
+    pair_sq.start()
+    pair_sq.wait_recv()
+    sq_both[...] = sq_own[...] + sq_pair[...]
+
+    def line_sq(step, source):
+        return remote(
+            sq_both, sq_line.at[source], as_.at[step], ar.at[1 + source], place.line((z + step) % LINE)
+        )
+
+    for step in range(1, LINE):
+        line_sq(step, z).start()
+    for step in range(1, LINE):
+        line_sq(step, (z + step) % LINE).wait_recv()
+    sq_line[z] = sq_both[...]
+
+    def normalise(c, gains):
+        there = at128(c * rows)
+        means = ((sq_line[0, c] + sq_line[1, c]) + (sq_line[2, c] + sq_line[3, c])) / width
+        now = scales[c]
+        result = []
+        for i in range(2):
+            pick = (lax.broadcasted_iota(jnp.int32, (8, 128), 0) == i).astype(F32)
+            scale = exact(now, pick, ((0,), (0,)))
+            mean = exact(means, pick, ((0,), (0,)))
+            gain_sum = []
+            for h in range(2):
+                lanes = slice(128 * h, 128 * h + 128)
+                v = raw[i, :, there, lanes].reshape(2 * rows, 128)
+                d = dy[i, :, there, lanes].reshape(2 * rows, 128)
+                gain_sum.append(jnp.sum(d * v * scale, axis=0, keepdims=True))
+                d = scale * gains_qk[i : i + 1, lanes] * d - v * (scale * scale * scale * mean)
+                ga[chunk_rows(c), 256 * i + 128 * h : 256 * i + 128 * h + 128] = d.astype(BF16)
+            result.append(gains[i] + jnp.concatenate(gain_sum, axis=1))
+        return tuple(result)
+
+    start = (jnp.zeros((1, cols), F32), jnp.zeros((1, cols), F32))
+    gain_q, gain_k = lax.fori_loop(0, LINE, normalise, start)
+    own_cols = at128(cols * (2 * z + k), cols)
+    gn_own[0:1, own_cols] = gain_q
+    gn_own[1:2, own_cols] = gain_k
+
+    def token_step(s, carry):
+        c = place.order(3 - s)
+        left = ga[chunk_rows(c), 0:768]
+
+        def body(t, inner):
+            lanes = at128(t * 512, 512)
+            term[:, :, lanes] = dot_rt(left, wg[lanes, 0:768]).reshape(2, rows, 512)
+            return inner
+
+        lax.fori_loop(0, 4, body, 0)
+        sums.give(c, s)
+        pl.when(s > 0)(lambda: sums.pass_on(place.order(4 - s), s + 1))
+        return carry
+
+    lax.fori_loop(0, 4, token_step, 0)
+    sums.pass_on(z, 3)
+
+    for n, i in enumerate(order):
+        left = feature_rows(wd, chips[i])
+
+        def three(t, carry, left=left):
+            lanes = at128(t * 256, 256)
+            stage[0, :, lanes] = dot_lt(left, ga[:, lanes]).astype(BF16)
+            return carry
+
+        lax.fori_loop(0, 3, three, 0)
+        part = stage.at[0, :, pl.ds(0, 768)]
+        copy = pltpu.make_async_copy(part, st_qkv.at[i], st_sem.at[3])
+        copy.start()
+        copy.wait()
+        if i < 3:
+            send_part(2, i, st_qkv, rc_qkv).start()
+
+    for s in range(2):
+        for c in range(LINE):
+            dg[c * 256 + s * rows : c * 256 + s * rows + rows, 0:256] = (
+                wu[1024 + s * 512 + c * rows : 1024 + s * 512 + c * rows + rows, 768:1024]
+            )
+
+    def outer(t, carry):
+        lanes = at128(t * 512, 512)
+        stage_d[:, lanes] = dot_lt(dg[:, 0:256], db[:, lanes]).astype(BF16)
+        return carry
+
+    lax.fori_loop(0, 4, outer, 0)
+    copy = pltpu.make_async_copy(stage_d, st_out, st_sem.at[0])
+    copy.start()
+    copy.wait()
+
+    def out_part(i):
+        return remote(
+            st_out.at[at128(64 * chips[i], 64)], rc_out.at[i], in_send.at[3, i], in_recv.at[3, i], near[i]
+        )
+
+    for i in range(3):
+        out_part(i).start()
+
+    def share(step, peer):
+        return remote(gn_own, gn_in.at[step], gs.at[step], gr.at[step], peer)
+
+    for step, peer in enumerate((place.partner, place.x, place.y)):
+        copy = share(step, peer)
+        copy.start()
+        copy.wait()
+        gn_own[...] = gn_own[...] + gn_in[step]
+
+    def line_gain(step, source):
+        return remote(
+            gn_own, gn_in.at[3 + source], gs.at[2 + step], gr.at[3 + source],
+            place.line((z + step) % LINE),
+        )
+
+    for step in range(1, LINE):
+        line_gain(step, z).start()
+
+    def to_owner(kind, src, dst):
+        def go(c, core, device, there):
+            return remote(
+                src(c, core), there, al_send.at[kind, c, core], al_recv.at[kind, z, k], device
+            )
+
+        def each(action):
+            for step in range(1, LINE):
+                c = (z + step) % LINE
+                action(go(c, k, place.line(c), dst.at[z, k]))
+                action(go(c, 1 - k, place.cross(c), dst.at[z, k]))
+            action(go(z, 1 - k, place.partner, dst.at[z, k]))
+
+        here = pltpu.make_async_copy(src(z, k), dst.at[z, k], al_loc.at[kind])
+        each(lambda copy: copy.start())
+        here.start()
+
+        def wait():
+            here.wait()
+            each(lambda copy: copy.wait_send())
+            for step in range(LINE):
+                c = (z + step) % LINE
+                for core in (0, 1):
+                    got = remote(
+                        src(c, k), dst.at[c, core], al_send.at[kind, c, core], al_recv.at[kind, c, core],
+                        place.partner,
+                    )
+                    if step == 0:
+                        pl.when(k != core)(lambda got=got: got.wait_recv())
+                    else:
+                        got.wait_recv()
+
+        return wait
+
+    for i in range(3):
+        send_part(1, i, st_gu, rc_gu).wait_recv()
+    waits = []
+    for m, (a, b2) in enumerate(((hid, ua), (dg, du))):
+        slots = [a.at[pl.ds(0, 512)], a.at[pl.ds(512, 512)], b2.at[pl.ds(0, 512)], b2.at[pl.ds(512, 512)]]
+        sources = [rc_gu.at[0, m], rc_gu.at[1, m], rc_gu.at[2, m], st_gu.at[3, m]]
+        copies = [
+            pltpu.make_async_copy(src, dst, sum_sem.at[4 + 4 * m + i])
+            for i, (src, dst) in enumerate(zip(sources, slots))
+        ]
+        for copy in copies:
+            copy.start()
+        for copy in copies:
+            copy.wait()
+
+        def add_up(t, carry, a=a, b2=b2):
+            there = at128(t * 128)
+            acc = a[there].astype(F32) + a[at128(512 + t * 128)].astype(F32)
+            acc = acc + b2[there].astype(F32) + b2[at128(512 + t * 128)].astype(F32)
+            a[there] = acc.astype(BF16)
+            return carry
+
+        lax.fori_loop(0, 4, add_up, 0)
+        waits.append(
+            to_owner(
+                m, lambda c, core, a=a: a.at[at128(c * 128 + core * 64, 64)], o_gu.at[m]
+            )
+        )
+
+    o_tok[...] = (d_mid[...] + sums.total()).astype(BF16)
+    sums.finish()
+
+    for i in range(3):
+        send_part(2, i, st_qkv, rc_qkv).wait_recv()
+    lanes = pl.ds(0, 768)
+    slots = [ua.at[pl.ds(0, 512), lanes], ua.at[pl.ds(512, 512), lanes],
+             du.at[pl.ds(0, 512), lanes], du.at[pl.ds(512, 512), lanes]]
+    sources = [rc_qkv.at[0], rc_qkv.at[1], rc_qkv.at[2], st_qkv.at[3]]
+    copies = [
+        pltpu.make_async_copy(src, dst, sum_sem.at[12 + i])
+        for i, (src, dst) in enumerate(zip(sources, slots))
+    ]
+    for copy in copies:
+        copy.start()
+    for copy in copies:
+        copy.wait()
+
+    def add_qkv(t, carry):
+        there, then = at128(t * 128), at128(512 + t * 128)
+        acc = ua[there, 0:768].astype(F32) + ua[then, 0:768].astype(F32)
+        acc = acc + du[there, 0:768].astype(F32) + du[then, 0:768].astype(F32)
+        ua[there, 0:768] = acc.astype(BF16)
+        return carry
+
+    lax.fori_loop(0, 4, add_qkv, 0)
+    waits.append(
+        to_owner(2, lambda c, core: ua.at[at128(c * 128 + core * 64, 64), lanes], o_qkv)
+    )
+
+    for i in range(3):
+        out_part(i).wait_recv()
+    sources = [rc_out.at[0], rc_out.at[1], rc_out.at[2], st_out.at[at128(64 * p, 64)]]
+    copies = [
+        pltpu.make_async_copy(src, ms.at[pl.ds(64 * i, 64)], sum_sem.at[16 + i])
+        for i, src in enumerate(sources)
+    ]
+    for copy in copies:
+        copy.start()
+    for copy in copies:
+        copy.wait()
+    acc = ms[0:64].astype(F32) + ms[64:128].astype(F32)
+    acc = acc + ms[128:192].astype(F32) + ms[192:256].astype(F32)
+    ms[256:320] = acc.astype(BF16)
+    out_done = ms.at[pl.ds(256, 64)]
+    fin_out = remote(out_done, o_out, fin_send.at[1], fin_recv.at[1], out_to)
+    keep_out = pltpu.make_async_copy(out_done, o_out, fin_loc.at[1])
+    pl.when(out_moves)(lambda: fin_out.start())
+    pl.when(jnp.logical_not(out_moves))(lambda: keep_out.start())
+
+    for step in range(1, LINE):
+        line_gain(step, (z + step) % LINE).wait_recv()
+    for step in range(1, LINE):
+        line_gain(step, z).wait_send()
+    total = gn_own[...]
+    for step in range(1, LINE):
+        total = total + gn_in[3 + (z + step) % LINE]
+    o_gains[...] = total
+
+    gather_b.finish()
+    pair_sq.wait_send()
+    for step in range(1, LINE):
+        line_sq(step, z).wait_send()
+    for i in range(3):
+        send_part(0, i, st_dn, rc_dn).wait_send()
+        send_part(1, i, st_gu, rc_gu).wait_send()
+        send_part(2, i, st_qkv, rc_qkv).wait_send()
+        out_part(i).wait_send()
+    for wait in waits:
+        wait()
+    pl.when(down_moves)(lambda: fin_down.wait())
+    pl.when(jnp.logical_not(down_moves))(lambda: keep_down.wait())
+    pl.when(out_moves)(lambda: fin_out.wait())
+    pl.when(jnp.logical_not(out_moves))(lambda: keep_out.wait())
+
+
+def run_backward(gains_qk, gain_attn, d_mlp, cotangent, branch, scales, gm_part, kept):
+    shape = jax.ShapeDtypeStruct
+    dma = pltpu.SemaphoreType.DMA
+    flat = [(2048, 768), (256, 2048), (2048, 1024), (2048, 1024), (1024, 2048), (1024, 2048), (1024, 2048),
+            (1024, 1024), (1024, 1024), (1024, 1024), None, (3072, 256), (2048, 512), (1024, 256), None]
+    kept = [a if s is None else a.reshape(s) for a, s in zip(kept, flat)]
+    results = [
+        shape((256, 2048), BF16),
+        shape((64, 2048), BF16),
+        shape((2, 4, 2, 64, 1024), BF16),
+        shape((4, 2, 64, 768), BF16),
+    ]
+    transit = [
+        shape((4, 256, 2048), BF16),
+        shape((3, 256, 2048), BF16),
+        shape((4, 2, 512, 1024), BF16),
+        shape((3, 2, 512, 1024), BF16),
+        shape((4, 512, 768), BF16),
+        shape((3, 512, 768), BF16),
+        shape((256, 2048), BF16),
+        shape((3, 64, 2048), BF16),
+    ]
+    wide, square = pltpu.VMEM((1024, 2048), BF16), pltpu.VMEM((1024, 1024), BF16)
+    tall = pltpu.VMEM((2048, 1024), BF16)
+    rows = pltpu.VMEM((4, 128, 2048), BF16)
+    small = pltpu.VMEM((4, 8, 256), F32)
+    return pl.pallas_call(
+        backward_kernel,
+        name="backward",
+        out_shape=[shape((128, 2048), BF16), shape((8, 2048), F32)] + results + transit,
+        in_specs=[vmem_spec()] * 7 + [any_spec()] * len(kept),
+        out_specs=[vmem_spec()] * 2 + [any_spec()] * (len(results) + len(transit)),
+        scratch_shapes=[
+            wide, tall, tall, square, square, square, wide, square, square, wide, wide,
+            pltpu.VMEM((2, 2, 512, 256), F32),
+            pltpu.VMEM((2, 2, 512, 128), F32),
+            pltpu.VMEM((2, 512, 256), BF16),
+            pltpu.VMEM((2, 2, 512, 256), F32),
+            pltpu.VMEM((2, 128, 2048), F32),
+            rows,
+            rows,
+            pltpu.VMEM((2, 128, 2048), F32),
+            pltpu.VMEM((128, 2048), F32),
+            rows,
+            rows,
+            small,
+            small,
+            small,
+            pltpu.VMEM((4, 4, 8, 256), F32),
+            pltpu.VMEM((8, 2048), F32),
+            pltpu.VMEM((7, 8, 2048), F32),
+            pltpu.VMEM((128, 2048), F32),
+            pltpu.VMEM((2, 512, 1024), BF16),
+            pltpu.VMEM((256, 2048), BF16),
+            dma((16,)),
+            dma((2, 2, 4)), dma((2, 4)), dma((2, 4)), dma((2, 4)),
+            dma((4,)), dma((4,)), dma((4,)), dma((4,)),
+            dma((4,)), dma((5,)),
+            dma((6,)), dma((7,)),
+            dma((4, 3)), dma((4, 3)),
+            dma((4,)), dma((20,)),
+            dma((2,)), dma((2,)), dma((2,)),
+            dma((3, 4, 2)), dma((3, 4, 2)), dma((3,)),
+        ],
+        compiler_params=pltpu.CompilerParams(
+            collective_id=1, has_side_effects=True, vmem_limit_bytes=64 * 1024 * 1024
+        ),
+    )(gains_qk, gain_attn, d_mlp, cotangent, branch, scales, gm_part, *kept)[:6]
+
+
+def shards_kernels(tokens, block_pairs, w_query, w_key, w_value, w_out, w_gate, w_up, w_down,
+                   gain_query, gain_key, gain_attn, gain_mlp, cotangent):
+    z = lax.axis_index("ctx")
+    f = lax.axis_index("fsdp")
+    start = 256 * (2 * z + f % 2)
+    gains_qk = jnp.stack([
+        lax.dynamic_slice_in_dim(gain_query, start, 256), lax.dynamic_slice_in_dim(gain_key, start, 256)
+    ])
+    out, d_mlp, gm_part, branch, scales, *kept = run_forward(
+        block_pairs, gains_qk, gain_attn[None], gain_mlp[None], tokens[0], cotangent[0],
+        (w_query, w_key, w_value, w_out, w_gate, w_up, w_down),
+    )
+    d_tokens, gains, down, out_rows, gate_up, qkv = run_backward(
+        gains_qk, gain_attn[None], d_mlp, cotangent[0], branch, scales, gm_part, kept
+    )
+    gate_up = gate_up.reshape(2, 4, 2, 64, 4, 256).transpose(0, 3, 4, 2, 1, 5).reshape(2, 64, 8192)
+    qkv = qkv.reshape(4, 2, 64, 3, 256).transpose(3, 2, 0, 1, 4).reshape(3, 64, 2048)
+    gains = lax.dynamic_slice_in_dim(gains, 64 * (8 * z + f), 64, 1)
+    return (
+        out[None],
+        d_tokens[None],
+        qkv[0].astype(F32),
+        qkv[1].astype(F32),
+        qkv[2].astype(F32),
+        out_rows.astype(F32),
+        gate_up[0].astype(F32),
+        gate_up[1].astype(F32),
+        down.astype(F32),
+        gains[0],
+        gains[1],
+        gains[2],
+        gains[3],
+    )
+
+
+def shards(*arrays):
+    tokens, w_query, w_down = arrays[0], arrays[2], arrays[8]
+    here = (lax.axis_size("ctx"), lax.axis_size("fsdp"), tokens.shape, w_query.shape, w_down.shape)
+    if here == (LINE, 2 * PLANE, (1, 128, 2048), (256, 2048), (1024, 2048)):
+        return shards_kernels(*arrays)
+    return shards_general(*arrays)
+
+
 def solution(mesh):
     in_specs = (
         P("fsdp", "ctx", None),

time: 1280 us -> 666 us (0.52)
  the two profiles are of different devices: /device:TPU:11 before, /device:TPU:27 now
where the time goes in v2:
time: 666 us; the launch traced here: 658 us
  Pallas kernels  626 us (94%)
  local copies, waits for them, and re-layouts  27 us (4%)
    pallas_call x1, Pallas kernels, run_backward(): pl.pallas_call(backward_kernel, name='backward', out_shape=[shape((128, 2...  346 us
    pallas_call x1, Pallas kernels, run_forward(): pl.pallas_call(forward_kernel, name='forward', out_shape=[shape((128, 204...  280 us

profile of v2, /device:TPU:27, one launch (start us, length us, event | category | flops | bytes accessed | tf_op | source)
XLA Modules:
  0.0 658.1 jit_solution(7652186544556779483)
XLA Ops:
  0.7 0.8 dynamic_slice.9
  1.4 0.8 dynamic_slice.10
  2.2 0.6 pad_maximum_fusion.gains_qk
  2.8 279.6 %forward.1 = (bf16[128,2048]{1,0:T(8,128)(2,1)}, bf16[128,2048]{1,0:T(8,128)(2,1)}, f32[1,2048]{1,0:T(1,128)}, f32[128,2048]{1,0:T(8,128)}, f32[4,8,256]{2,1,0:T...) custom-call(s32[1,4]{1,0:T(1,128)} %pairs.1, ...), custom_call_target="tpu_custom_call" | custom-call | tf_op jit(solution)/shard_map/forward/pallas_call | solution.py:901
  282.3 346.1 %backward.1 = (bf16[128,2048]{1,0:T(8,128)(2,1)}, f32[8,2048]{1,0:T(8,128)}, bf16[256,2048]{1,0:T(8,128)(2,1)}, bf16[64,2048]{1,0:T(8,128)(2,1)}, bf16[2,4,2,64,...) custom-call(f32[2,256]{1,0:T(2,128)} %pad_maximum_fusion.gains_qk, ...), custom_call_target="tpu_custom_call" | custom-call | tf_op jit(solution)/shard_map/backward/pallas_call | solution.py:1502
  628.5 1.2 copy.55
  629.7 0.8 constant_dynamic-slice_fusion
  630.5 0.5 slice_bitcast_fusion
  631.0 1.8 convert_element_type.42
  632.8 0.2 slice_convert_fusion.2
  632.9 0.4 copy.47
  633.3 1.2 reshape.90
  634.6 0.4 copy.46
  635.0 1.2 reshape.89
  636.2 0.4 copy.45
  636.6 1.2 reshape.88
  637.8 3.3 reshape.87
  641.1 0.0 copy-start
  641.2 0.4 copy.54
  641.5 0.8 copy-done
  642.4 1.6 convert_element_type.47
  643.9 0.4 slice_convert_fusion
  644.3 2.7 copy.50
  647.0 3.3 reshape.92
  650.3 2.7 copy.49
  653.0 0.0 copy-start.1
  653.0 0.0 copy-start.2
  653.0 3.4 reshape.91
  656.4 0.0 copy-done.1
  656.4 0.8 copy.58
  657.2 0.0 copy-done.2
  657.2 0.8 copy.59
Async XLA Ops:
  641.1 1.2 copy-start
  653.0 3.4 copy-start.1
  653.0 4.2 copy-start.2

commit v3 on v2

--- a/solution.py
+++ b/solution.py
@@ -394,10 +394,10 @@
         pl.when(self.pl.ends == 0)(lambda: self.arrive(self.pl.order(2)))
 
     def arrive_second(self):
-        pl.when(self.pl.ends == 1)(lambda: self.arrive(self.pl.order(2)))
+        self.arrive(self.pl.order(3 - self.pl.ends))
 
     def arrive_third(self):
-        self.arrive(self.pl.order(3))
+        pl.when(self.pl.ends == 1)(lambda: self.arrive(self.pl.order(3)))
 
     def ready(self, c):
         self.from_core(c).wait_recv()
@@ -417,49 +417,72 @@
 
 
 class RowSum:
-    def __init__(self, place, term, pair_out, pair_in, keep, mine, line_out, line_in, sems):
-        self.pl, self.term = place, term
-        self.pair_out, self.pair_in, self.keep, self.mine = pair_out, pair_in, keep, mine
-        self.line_out, self.line_in = line_out, line_in
+    def __init__(self, place, h, buffers, sems):
+        self.pl, self.h = place, h
+        self.term, self.pair_out, self.pair_in, self.keep, self.mine, self.line_out, self.line_in = buffers
         self.p_send, self.p_recv, self.l_send, self.l_recv = sems
 
     def pair(self, c):
+        h = self.h
         return remote(
-            self.pair_out.at[c], self.pair_in.at[c], self.p_send.at[c], self.p_recv.at[c], self.pl.partner
+            self.pair_out.at[h, c], self.pair_in.at[h, c], self.p_send.at[h, c], self.p_recv.at[h, c],
+            self.pl.partner,
         )
 
-    def line(self, c, source):
+    def line(self, c, slot, target):
+        h = self.h
         return remote(
-            self.line_out.at[c], self.line_in.at[source], self.l_send.at[c], self.l_recv.at[source],
-            self.pl.line(c),
+            self.line_out.at[h, c], self.line_in.at[h, slot], self.l_send.at[h, c],
+            self.l_recv.at[h, slot], self.pl.line(target),
         )
 
+    def mate(self):
+        return self.pl.z + 1 - 2 * (self.pl.z % 2)
+
     def give(self, c, s):
-        k = self.pl.k
-        self.pair_out[c] = self.term[1 - k].astype(BF16)
+        h, k = self.h, self.pl.k
+        self.pair_out[h, c] = self.term[1 - k].astype(BF16)
         self.pair(c).start()
-        self.keep[s % 2] = self.term[k]
+        self.keep[h, s % 2] = self.term[k]
 
     def pass_on(self, c, s):
-        z = self.pl.z
+        h, z = self.h, self.pl.z
+        near = c // 2 == z // 2
+        end = self.pl.ends == 1
         self.pair(c).wait_recv()
+
+        @pl.when(c == z)
+        def _():
+            self.mine[h] = self.keep[h, s % 2] + self.pair_in[h, c].astype(F32)
 
         @pl.when(c != z)
         def _():
-            self.line_out[c] = (self.keep[s % 2] + self.pair_in[c].astype(F32)).astype(BF16)
-            self.line(c, z).start()
-
-        @pl.when(c == z)
+            self.line_out[h, c] = (self.keep[h, s % 2] + self.pair_in[h, c].astype(F32)).astype(BF16)
+
+        pl.when(jnp.logical_and(c != z, near))(lambda: self.line(c, z, c).start())
+        pl.when(jnp.logical_and(jnp.logical_not(near), end))(
+            lambda: self.line(c, 2 * c - 3 * (1 - z // 2), self.mate()).start()
+        )
+
+    def relay(self, far):
+        h, z = self.h, self.pl.z
+
+        @pl.when(self.pl.ends == 0)
         def _():
-            self.mine[...] = self.keep[s % 2] + self.pair_in[c].astype(F32)
+            c = 3 * (2 - z) if far else 3 - z
+            slot = 2 * c - 3 * (2 - z)
+            self.line(c, slot, z).wait_recv()
+            self.line_out[h, c] = (
+                self.line_out[h, c].astype(F32) + self.line_in[h, slot].astype(F32)
+            ).astype(BF16)
+            self.line(c, z, c).start()
 
     def total(self):
-        z = self.pl.z
-        for step in range(1, LINE):
-            self.line((z + step) % LINE, (z + step) % LINE).wait_recv()
-        result = self.mine[...]
-        for step in range(1, LINE):
-            result = result + self.line_in[(z + step) % LINE].astype(F32)
+        h, z = self.h, self.pl.z
+        result = self.mine[h]
+        for source in (self.mate(), 2 - z // 2):
+            self.line(source, source, source).wait_recv()
+            result = result + self.line_in[h, source].astype(F32)
         return result
 
     def finish(self):
@@ -467,7 +490,7 @@
 
         def body(c, carry):
             self.pair(c).wait_send()
-            pl.when(c != z)(lambda: self.line(c, z).wait_send())
+            pl.when(c != z)(lambda: self.line(c, z, c).wait_send())
             return carry
 
         lax.fori_loop(0, LINE, body, 0)
@@ -580,37 +603,48 @@
                 a.wait()
                 b.wait_recv()
 
+    dx, dy = (p % 2 + z % 2) % 2, (p // 2 + z // 2) % 2
+    top, low = wo.at[pl.ds(0, 128)], wo.at[pl.ds(128, 128)]
+    wo_copy = pltpu.make_async_copy(w_out, wo, loc_sem.at[12])
+
+    def wo_first(i, device):
+        rows_i = pl.ds(128 * i, 128)
+        return remote(w_out.at[rows_i], wo.at[rows_i], wo_send.at[i], wo_recv.at[i], device)
+
+    def wo_send_to(i, part, device):
+        return remote(part, part, wo_send.at[i], wo_recv.at[i], device)
+
+    is_source = jnp.logical_and(dx == 0, dy == 0)
+    is_x = jnp.logical_and(dx == 1, dy == 0)
+    is_y = jnp.logical_and(dx == 0, dy == 1)
+    is_d = jnp.logical_and(dx == 1, dy == 1)
+
+    @pl.when(is_source)
+    def _():
+        wo_copy.start()
+        wo_first(0, place.x).start()
+        wo_first(1, place.y).start()
+
     begin("q", "k", "v")
     xs[z, k] = tokens[...]
     gather_x = Gather(place, xs, zs.at[0], zr.at[0], cs.at[0], cr.at[0])
     gather_x.start()
-    down_copy = pltpu.make_async_copy(
-        w_down.at[at128(256 * z, 256)], wd.at[at128(256 * p, 256)], loc_sem.at[11]
-    )
-    down_copy.start()
+    down_copies = [
+        pltpu.make_async_copy(
+            w_down.at[at128(256 * z, 256), pl.ds(1024 * h, 1024)], wd.at[h, at128(256 * p, 256)],
+            loc_sem.at[(11, 13)[h]],
+        )
+        for h in range(2)
+    ]
+    for copy in down_copies:
+        copy.start()
     begin("g", "u")
     ring_qkv = Ring(place, qkv, 512, ring_send.at[0], ring_recv.at[0])
     ring_g = Ring(place, wg, 512, ring_send.at[1], ring_recv.at[1])
     ring_u = Ring(place, wu, 512, ring_send.at[2], ring_recv.at[2])
-    ring_d = Ring(place, wd, 256, ring_send.at[3], ring_recv.at[3])
+    ring_d = [Ring(place, wd.at[h], 256, ring_send.at[3 + h], ring_recv.at[3 + h]) for h in range(2)]
     settle("q", "k", "v")
     ring_qkv.start()
-
-    dx, dy = (p % 2 + z % 2) % 2, (p // 2 + z // 2) % 2
-    top, low = wo.at[pl.ds(0, 128)], wo.at[pl.ds(128, 128)]
-    wo_copy = pltpu.make_async_copy(w_out, wo, loc_sem.at[12])
-
-    def wo_send_to(i, part, device):
-        return remote(part, part, wo_send.at[i], wo_recv.at[i], device)
-
-    is_source = jnp.logical_and(dx == 0, dy == 0)
-    is_x = jnp.logical_and(dx == 1, dy == 0)
-    is_y = jnp.logical_and(dx == 0, dy == 1)
-    is_d = jnp.logical_and(dx == 1, dy == 1)
-
-    @pl.when(is_source)
-    def _():
-        wo_copy.start()
 
     def positions(shape, axis):
         i = lax.broadcasted_iota(jnp.int32, shape, axis)
@@ -639,17 +673,22 @@
         t.start()
 
     gather_x.arrive_first()
+    pl.when(is_x)(lambda: wo_send_to(0, top, place.x).wait_recv())
+    pl.when(is_x)(lambda: wo_send_to(0, top, place.y).start())
+    pl.when(is_y)(lambda: wo_send_to(1, low, place.x).wait_recv())
+    pl.when(is_y)(lambda: wo_send_to(1, low, place.x).start())
     ring_qkv.forward()
-    settle("g")
+    settle("g", "u")
+    gather_x.arrive_second()
+
+    @pl.when(is_d)
+    def _():
+        wo_send_to(0, top, place.x).wait_recv()
+        wo_send_to(0, top, place.x).start()
+        wo_send_to(1, low, place.x).wait_recv()
+        wo_send_to(1, low, place.y).start()
+
     ring_g.start()
-
-    @pl.when(is_source)
-    def _():
-        wo_copy.wait()
-        wo_send_to(0, top, place.x).start()
-        wo_send_to(1, low, place.y).start()
-
-    gather_x.arrive_second()
     ring_qkv.ready()
 
     def project(c):
@@ -670,17 +709,13 @@
         project(place.order(s))
         return carry
 
-    lax.fori_loop(0, 2, project_step, 0)
-    pl.when(is_x)(lambda: wo_send_to(0, top, place.x).wait_recv())
-    pl.when(is_x)(lambda: wo_send_to(0, top, place.y).start())
-    pl.when(is_y)(lambda: wo_send_to(1, low, place.x).wait_recv())
-    pl.when(is_y)(lambda: wo_send_to(1, low, place.x).start())
+    lax.fori_loop(0, 3, project_step, 0)
     gather_x.arrive_third()
-    lax.fori_loop(2, 4, project_step, 0)
+    lax.fori_loop(3, 4, project_step, 0)
 
     pair_sq = remote(sq_own, sq_pair, as_.at[0], ar.at[0], place.partner)
     pair_sq.start()
-    settle("u")
+    ring_u.start()
     pair_sq.wait_recv()
     sq_both[...] = sq_own[...] + sq_pair[...]
 
@@ -732,44 +767,38 @@
 
     lax.fori_loop(0, 2, attend, 0)
 
-    ring_g.forward()
-    ring_u.start()
-
-    @pl.when(is_d)
-    def _():
-        wo_send_to(0, top, place.x).wait_recv()
-        wo_send_to(0, top, place.x).start()
-        wo_send_to(1, low, place.x).wait_recv()
-        wo_send_to(1, low, place.y).start()
-
+    pl.when(is_source)(lambda: wo_copy.wait())
     pl.when(is_x)(lambda: wo_send_to(1, low, place.x).wait_recv())
     pl.when(is_y)(lambda: wo_send_to(0, top, place.x).wait_recv())
 
-    sums = RowSum(place, term, pair_out, pair_in, keep, mine, line_out, line_in, (ps, pr, ls, lr))
-
-    def tiles(c, left, weight):
-        def body(t, carry):
-            lanes = at128(t * 512, 512)
-            term[:, :, lanes] = dot(left, weight[:, lanes]).reshape(2, rows, 512)
-            return carry
-
-        lax.fori_loop(0, 4, body, 0)
+    ring_g.forward()
+    buffers = (term, pair_out, pair_in, keep, mine, line_out, line_in)
+    sums = [RowSum(place, h, buffers, (ps, pr, ls, lr)) for h in range(2)]
 
     def branch_step(s, carry):
         c = place.order(3 - s)
-        there = at128(c * rows)
-        tiles(c, att[:, there].reshape(2 * rows, cols), wo)
-        sums.give(c, s)
-        pl.when(s > 0)(lambda: sums.pass_on(place.order(4 - s), s + 1))
+        left = att[:, at128(c * rows)].reshape(2 * rows, cols)
+        for h in range(2):
+            term[...] = dot(left, wo[:, 1024 * h : 1024 * h + 1024]).reshape(2, rows, 1024)
+            sums[h].give(c, s)
+        for h in range(2):
+            pl.when(s > 0)(lambda h=h: sums[h].pass_on(place.order(4 - s), s + 1))
         return carry
 
     lax.fori_loop(0, 4, branch_step, 0)
-    sums.pass_on(z, 3)
+    for h in range(2):
+        sums[h].pass_on(z, 3)
+    for h in range(2):
+        sums[h].relay(True)
     ring_u.forward()
-    down_copy.wait()
-    ring_d.start()
-    branch = sums.total()
-    sums.finish()
+    for h in range(2):
+        sums[h].relay(False)
+    for copy in down_copies:
+        copy.wait()
+    ring_d[0].start()
+    branch = jnp.concatenate([sums[h].total() for h in range(2)], axis=1)
+    for h in range(2):
+        sums[h].finish()
     o_branch[...] = branch
 
     def mean_sq(v):
@@ -780,6 +809,8 @@
     gather_m = Gather(place, ms, zs.at[1], zr.at[1], cs.at[1], cr.at[1])
     gather_m.start()
 
+    ring_d[0].forward()
+    ring_d[1].start()
     ring_g.ready()
     ring_u.ready()
 
@@ -800,28 +831,41 @@
         lax.fori_loop(0, 4, body, 0)
         return carry
 
-    def contract(s, carry):
-        c = place.order(s)
-        tiles(c, hid[c], wd)
-        sums.give(c, s)
-        pl.when(s > 0)(lambda: sums.pass_on(place.order(s - 1), s + 1))
-        return carry
+    def contract(h):
+        def step(s, carry):
+            c = place.order(s)
+            term[...] = dot(hid[c], wd[h]).reshape(2, rows, 1024)
+            sums[h].give(c, s)
+            pl.when(s > 0)(lambda: sums[h].pass_on(place.order(s - 1), s + 1))
+            return carry
+
+        return step
 
     lax.fori_loop(0, 1, expand, 0)
     gather_m.arrive_first()
     lax.fori_loop(1, 2, expand, 0)
-    ring_d.forward()
+    ring_d[0].ready()
+    lax.fori_loop(0, 2, contract(0), 0)
     gather_m.arrive_second()
+    ring_d[1].forward()
     lax.fori_loop(2, 3, expand, 0)
-    ring_d.ready()
-    lax.fori_loop(0, 3, contract, 0)
+    lax.fori_loop(2, 3, contract(0), 0)
+    ring_d[1].ready()
+    lax.fori_loop(0, 3, contract(1), 0)
     gather_m.arrive_third()
     lax.fori_loop(3, 4, expand, 0)
-    lax.fori_loop(3, 4, contract, 0)
-    sums.pass_on(place.order(3), 3)
+    for h in range(2):
+        lax.fori_loop(3, 4, contract(h), 0)
+    for h in range(2):
+        sums[h].relay(False)
+    for h in range(2):
+        sums[h].pass_on(place.order(3), 3)
+    for h in range(2):
+        sums[h].relay(True)
 
     saves = [
-        (qkv, o_qkv), (wo, o_wo), (wg, o_g), (wu, o_u), (wd, o_dn), (xs, o_x), (ms, o_m), (ga, o_ga),
+        (qkv, o_qkv), (wo, o_wo), (wg, o_g), (wu, o_u), (wd.at[0], o_dn.at[:, pl.ds(0, 1024)]),
+        (wd.at[1], o_dn.at[:, pl.ds(1024, 1024)]), (xs, o_x), (ms, o_m), (ga, o_ga),
         (ua, o_ua), (hid, o_hid), (raw, o_raw), (heads, o_heads), (probs, o_probs), (att, o_att),
         (tab, o_tab),
     ]
@@ -829,8 +873,9 @@
     for copy in copies:
         copy.start()
 
-    mlp = sums.total()
-    sums.finish()
+    mlp = jnp.concatenate([sums[h].total() for h in range(2)], axis=1)
+    for h in range(2):
+        sums[h].finish()
     c_m = lax.rsqrt(mean_sq(mlp) + EPSILON)
     gain = gain_mlp[...]
     o_out[...] = (mid[...] + mlp * c_m * gain).astype(BF16)
@@ -842,7 +887,7 @@
 
     gather_x.finish()
     gather_m.finish()
-    for ring in (ring_qkv, ring_g, ring_u, ring_d):
+    for ring in (ring_qkv, ring_g, ring_u, *ring_d):
         ring.finish()
     for group in swap.values():
         for copy in group:
@@ -855,8 +900,8 @@
 
     @pl.when(is_source)
     def _():
-        wo_send_to(0, top, place.x).wait_send()
-        wo_send_to(1, low, place.y).wait_send()
+        wo_first(0, place.x).wait_send()
+        wo_first(1, place.y).wait_send()
 
     pl.when(is_x)(lambda: wo_send_to(0, top, place.y).wait_send())
     pl.when(is_y)(lambda: wo_send_to(1, low, place.x).wait_send())
@@ -911,42 +956,42 @@
         + kept,
         in_specs=[pl.BlockSpec(memory_space=pltpu.SMEM)] + [vmem_spec()] * 5 + [any_spec()] * 7,
         out_specs=[vmem_spec()] * 5 + [any_spec()] * len(kept),
-        scratch_shapes=[pltpu.VMEM(k.shape, k.dtype) for k in kept]
+        scratch_shapes=[pltpu.VMEM((2, 1024, 1024) if i == 4 else k.shape, k.dtype) for i, k in enumerate(kept)]
         + [
             pltpu.VMEM((2, 8, 512), F32),
             pltpu.VMEM((2, 512, 128), F32),
-            pltpu.VMEM((2, 128, 2048), F32),
-            pltpu.VMEM((4, 128, 2048), BF16),
-            pltpu.VMEM((4, 128, 2048), BF16),
-            pltpu.VMEM((2, 128, 2048), F32),
-            pltpu.VMEM((128, 2048), F32),
-            pltpu.VMEM((4, 128, 2048), BF16),
-            pltpu.VMEM((4, 128, 2048), BF16),
+            pltpu.VMEM((2, 128, 1024), F32),
+            pltpu.VMEM((2, 4, 128, 1024), BF16),
+            pltpu.VMEM((2, 4, 128, 1024), BF16),
+            pltpu.VMEM((2, 2, 128, 1024), F32),
+            pltpu.VMEM((2, 128, 1024), F32),
+            pltpu.VMEM((2, 4, 128, 1024), BF16),
+            pltpu.VMEM((2, 4, 128, 1024), BF16),
             pltpu.VMEM((4, 8, 256), F32),
             pltpu.VMEM((4, 8, 256), F32),
             pltpu.VMEM((4, 8, 256), F32),
             pltpu.VMEM((4, 4, 8, 256), F32),
             pltpu.VMEM((128, 2048), F32),
-            dma((13,)),
+            dma((14,)),
             dma((11,)),
             dma((11,)),
-            dma((4, 4)),
-            dma((4, 4)),
+            dma((5, 4)),
+            dma((5, 4)),
             dma((2,)),
             dma((2,)),
             dma((2, 2, 4)),
             dma((2, 4)),
             dma((2, 4)),
             dma((2, 4)),
-            dma((4,)),
-            dma((4,)),
-            dma((4,)),
-            dma((4,)),
+            dma((2, 4)),
+            dma((2, 4)),
+            dma((2, 4)),
+            dma((2, 4)),
             dma((4,)),
             dma((4,)),
             dma((4,)),
             dma((5,)),
-            dma((len(kept),)),
+            dma((len(kept) + 1,)),
         ],
         compiler_params=pltpu.CompilerParams(
             collective_id=0, has_side_effects=True, vmem_limit_bytes=64 * 1024 * 1024
@@ -957,20 +1002,23 @@
 def backward_kernel(
     gains_qk, gain_attn, d_mlp, cotangent, branch, scales, gm_part,
     h_qkv, h_wo, h_g, h_u, h_dn, h_x, h_m, h_ga, h_ua, h_hid, h_raw, h_heads, h_probs, h_att, h_tab,
-    o_tok, o_gains, o_down, o_out, o_gu, o_qkv,
-    st_dn, rc_dn, st_gu, rc_gu, st_qkv, rc_qkv, st_out, rc_out,
+    o_tok, o_down, o_out, o_gu, o_qkv,
+    st_g, rc_g, st_u, rc_u, st_dn, rc_dn, st_qkv, rc_qkv, st_out, rc_out,
     wd, wg, wu, ga, ua, hid, dm, dg, du, ms, db, raw, tab, datt, dy,
     term, pair_out, pair_in, keep, mine, line_out, line_in,
-    sq_own, sq_pair, sq_both, sq_line, gn_own, gn_in, d_mid, stage, stage_d,
-    ld, zs, zr, cs, cr, ps, pr, ls, lr, as_, ar, gs, gr, in_send, in_recv, st_sem, sum_sem,
+    sq_own, sq_pair, sq_both, sq_line, gn_own, d_mid, stage, stage_d, far_in,
+    ld, far_sem, zs, zr, cs, cr, ps, pr, ls, lr, as_, ar, in_send, in_recv, st_sem, sum_sem,
     fin_send, fin_recv, fin_loc, al_send, al_recv, al_loc,
 ):
     place = Place()
     z, f, p, k = place.z, place.f, place.p, place.k
     rows, width, cols = 128, 2048, 256
 
-    down_to = ((p - z + LINE) % LINE, 4 * k + z)
-    down_from = (f % 4, 2 * ((z + f % 4) % LINE) + f // 4)
+    def strip_of(chip, plane):
+        return (chip % 2 + plane // 2) % 2 + 2 * ((chip // 2 + plane % 2) % 2)
+
+    down_to = (strip_of(p, z), 4 * k + z)
+    down_from = (f % 4, 2 * strip_of(z, f % 4) + f // 4)
     down_moves = jnp.logical_or(down_to[0] != z, down_to[1] != f)
     out_to = (z, 4 * k + p)
     out_from = (z, 2 * (f % 4) + f // 4)
@@ -1015,12 +1063,13 @@
     load("raw", h_raw, raw)
     load("tab", h_tab, tab)
 
-    sums = RowSum(place, term, pair_out, pair_in, keep, mine, line_out, line_in, (ps, pr, ls, lr))
+    buffers = (term, pair_out, pair_in, keep, mine, line_out, line_in)
+    sums = [RowSum(place, h, buffers, (ps, pr, ls, lr)) for h in range(2)]
 
     def chunk_rows(c):
         return at128(c * 256, 256)
 
-    def ffn(s, carry):
+    def expand(s, carry):
         c = place.order(s)
         gather_d.ready(c)
         here = chunk_rows(c)
@@ -1037,29 +1086,37 @@
             return inner
 
         lax.fori_loop(0, 4, act, 0)
+        return carry
+
+    def contract(s, carry):
+        c = place.order(s)
+        here = chunk_rows(c)
         left_g, left_u = dg[here], du[here]
-
-        def back(t, inner):
-            lanes = at128(t * 512, 512)
-            part = dot_rt(left_g, wg[lanes]) + dot_rt(left_u, wu[lanes])
-            term[:, :, lanes] = part.reshape(2, rows, 512)
-            return inner
-
-        lax.fori_loop(0, 4, back, 0)
-        sums.give(c, s)
-        pl.when(s > 0)(lambda: sums.pass_on(place.order(s - 1), s + 1))
+        for h in range(2):
+            out = slice(1024 * h, 1024 * h + 1024)
+            term[...] = (dot_rt(left_g, wg[out]) + dot_rt(left_u, wu[out])).reshape(2, rows, 1024)
+            sums[h].give(c, s)
+        for h in range(2):
+            pl.when(s > 0)(lambda h=h: sums[h].pass_on(place.order(s - 1), s + 1))
         return carry
 
-    for name in ("wd", "ga", "ua", "wg", "wu"):
+    for name in ("wd", "ga", "ua"):
         loads[name].wait()
-    lax.fori_loop(0, 1, ffn, 0)
+    lax.fori_loop(0, 1, expand, 0)
+    for name in ("wg", "wu"):
+        loads[name].wait()
     gather_d.arrive_first()
-    lax.fori_loop(1, 2, ffn, 0)
-    gather_d.arrive_second()
-    lax.fori_loop(2, 3, ffn, 0)
+    lax.fori_loop(0, 1, contract, 0)
+    for s in (1, 2):
+        if s == 2:
+            gather_d.arrive_second()
+        lax.fori_loop(s, s + 1, expand, 0)
+        lax.fori_loop(s, s + 1, contract, 0)
     gather_d.arrive_third()
-    lax.fori_loop(3, 4, ffn, 0)
-    sums.pass_on(place.order(3), 3)
+    lax.fori_loop(3, 4, expand, 0)
+    lax.fori_loop(3, 4, contract, 0)
+    for h in range(2):
+        sums[h].pass_on(place.order(3), 3)
     load("x", h_x, wd)
     load("qkv", h_qkv, wg.at[:, pl.ds(0, 768)])
     load("probs", h_probs, wu.at[:, pl.ds(0, 512)])
@@ -1069,57 +1126,86 @@
 
     chips = [place.p_x, place.p_y, place.p_d, p]
     near = [place.x, place.y, place.d]
-
-    def send_part(kind, i, src, dst):
-        return remote(src.at[i], dst.at[i], in_send.at[kind, i], in_recv.at[kind, i], near[i])
-
-    loads["hid"].wait()
-    order = (2, 0, 1, 3)
-    for n, i in enumerate(order):
-        strip = hid[:, at128(((chips[i] - z + LINE) % LINE) * 256, 256)]
-
-        def down(t, carry, strip=strip):
-            lanes = at128(t * 512, 512)
-            stage_d[:, lanes] = dot_lt(strip, dm[:, lanes]).astype(BF16)
-            return carry
-
-        lax.fori_loop(0, 4, down, 0)
-        copy = pltpu.make_async_copy(stage_d, st_dn.at[i], st_sem.at[0])
+    GATE, UP, DOWN, QKV, OUT = range(5)
+    kinds = {GATE: (st_g, rc_g), UP: (st_u, rc_u), DOWN: (st_dn, rc_dn), QKV: (st_qkv, rc_qkv)}
+
+    def half_of(kind, ref, i, half):
+        if kind == DOWN:
+            return ref.at[i, :, pl.ds(1024 * half, 1024)]
+        return ref.at[i, pl.ds(256 * half, 256)]
+
+    def far_part(kind, half):
+        st, rc = kinds[kind]
+        return remote(
+            half_of(kind, st, 2, half), half_of(kind, rc, 2, half), in_send.at[kind, 2 + half],
+            in_recv.at[kind, 2 + half], near[half],
+        )
+
+    def near_part(kind, i):
+        st, rc = kinds[kind]
+        return remote(st.at[i], rc.at[i], in_send.at[kind, i], in_recv.at[kind, i], near[i])
+
+    def put(kind, i, buf, sem):
+        wide = 896 if kind == QKV else 1024
+        if i < 2:
+            half = 1 - i
+            far_part(kind, half).wait_recv()
+            got = far_in.at[:, pl.ds(0, wide)]
+            copy = pltpu.make_async_copy(half_of(kind, kinds[kind][1], 2, half), got, far_sem)
+            copy.start()
+            copy.wait()
+            if kind == DOWN:
+                now = (slice(None), slice(1024 * half, 1024 * half + 1024))
+            else:
+                now = (slice(256 * half, 256 * half + 256), slice(0, wide))
+            buf[now] = (buf[now].astype(F32) + far_in[:, 0:wide].astype(F32)).astype(BF16)
+        src = buf.at[:, pl.ds(0, 896)] if kind == QKV else buf
+        copy = pltpu.make_async_copy(src, kinds[kind][0].at[i], st_sem.at[sem])
         copy.start()
         copy.wait()
-        if i < 3:
-            send_part(0, i, st_dn, rc_dn).start()
-
-    load("wo", h_wo, stage_d)
-    loads["ms"].wait()
+        if i == 2:
+            far_part(kind, 0).start()
+            far_part(kind, 1).start()
+        elif i < 2:
+            near_part(kind, i).start()
 
     def feature_rows(ref, chip):
-        return jnp.concatenate([ref[:, at128(512 * c + 128 * chip)] for c in range(LINE)], axis=1)
-
-    for n, i in enumerate(order):
+        return jnp.concatenate([ref[:, at128(512 * c + 128 * chip)] for c in range(LINE)], axis=1).T
+
+    def gate_up_part(i):
         left = feature_rows(ms, chips[i])
         for m, right in enumerate((dg, du)):
-
-            def both(t, carry, left=left, right=right, m=m):
-                lanes = at128(t * 256, 256)
-                stage[m, :, lanes] = dot_lt(left, right[:, lanes]).astype(BF16)
-                return carry
-
-            lax.fori_loop(0, 4, both, 0)
-            copy = pltpu.make_async_copy(stage.at[m], st_gu.at[i, m], st_sem.at[1 + m])
-            copy.start()
-        for m in range(2):
-            pltpu.make_async_copy(stage.at[m], st_gu.at[i, m], st_sem.at[1 + m]).wait()
-        if i < 3:
-            send_part(1, i, st_gu, rc_gu).start()
-
+            for t in range(2):
+                lanes = slice(512 * t, 512 * t + 512)
+                stage[m, :, lanes] = dot(left, right[:, lanes]).astype(BF16)
+            put(m, i, stage.at[m], m)
+
+    def down_part(i):
+        left = hid[:, at128(strip_of(chips[i], z) * 256, 256)].T
+        for t in range(4):
+            lanes = slice(512 * t, 512 * t + 512)
+            stage_d[:, lanes] = dot(left, dm[:, lanes]).astype(BF16)
+        put(DOWN, i, stage_d, 2)
+
+    loads["ms"].wait()
+    loads["hid"].wait()
+    gate_up_part(2)
+    for h in range(2):
+        sums[h].relay(False)
+    down_part(2)
+    gate_up_part(3)
+    for h in range(2):
+        sums[h].relay(True)
+    gate_up_part(0)
+    gate_up_part(1)
     gather_d.finish()
 
     def mean_of(v):
         return jnp.sum(v, axis=1, keepdims=True) / width
 
-    d_mid[...] = cotangent[...].astype(F32) + sums.total()
-    sums.finish()
+    d_mid[...] = cotangent[...].astype(F32) + jnp.concatenate([sums[h].total() for h in range(2)], axis=1)
+    for h in range(2):
+        sums[h].finish()
     b = branch[...]
     c_b = lax.rsqrt(mean_of(b * b) + EPSILON)
     gdy = gain_attn[...] * d_mid[...]
@@ -1132,6 +1218,11 @@
     gn_own[2:3, :] = jnp.sum(d_mid[...] * b * c_b, axis=0, keepdims=True)
     gn_own[3:4, :] = gm_part[...]
 
+    down_part(3)
+    down_part(0)
+    down_part(1)
+    load("wo", h_wo, stage_d)
+
     for name in ("wo", "raw", "tab", "x", "qkv", "probs", "qk", "v", "att"):
         loads[name].wait()
 
@@ -1144,36 +1235,83 @@
 
     gather_b.arrive_first()
     lax.fori_loop(0, 2, attended_step, 0)
-
-    for i in range(3):
-        send_part(0, i, st_dn, rc_dn).wait_recv()
-    parts = [rc_dn.at[0], rc_dn.at[1], rc_dn.at[2], st_dn.at[3]]
     gather_b.arrive_second()
-    copies = [
-        pltpu.make_async_copy(src, ms.at[pl.ds(256 * i, 256)], sum_sem.at[i])
-        for i, src in enumerate(parts)
-    ]
-    for copy in copies:
-        copy.start()
-    for copy in copies:
-        copy.wait()
-
-    def add_down(t, carry):
-        lanes = at128(t * 512, 512)
-        acc = ms[0:256, lanes].astype(F32)
-        for i in range(1, 4):
-            acc = acc + ms[256 * i : 256 * i + 256, lanes].astype(F32)
-        dm[0:256, lanes] = acc.astype(BF16)
-        return carry
-
-    lax.fori_loop(0, 4, add_down, 0)
-    down_done = dm.at[pl.ds(0, 256)]
-    fin_down = remote(down_done, o_down, fin_send.at[0], fin_recv.at[0], down_to)
-    keep_down = pltpu.make_async_copy(down_done, o_down, fin_loc.at[0])
-    pl.when(down_moves)(lambda: fin_down.start())
-    pl.when(jnp.logical_not(down_moves))(lambda: keep_down.start())
-
     lax.fori_loop(2, 3, attended_step, 0)
+
+    def fetch(kind, parts, first):
+        copies = [
+            pltpu.make_async_copy(src, dst, sum_sem.at[first + n]) for n, (src, dst) in enumerate(parts)
+        ]
+        for copy in copies:
+            copy.start()
+        for copy in copies:
+            copy.wait()
+
+    def to_owner(kind, src, dst):
+        def go(c, core, device):
+            return remote(
+                src(c, core), dst.at[z, k], al_send.at[kind, c, core], al_recv.at[kind, z, k], device
+            )
+
+        def each(action):
+            for step in range(1, LINE):
+                c = (z + step) % LINE
+                action(go(c, k, place.line(c)))
+                action(go(c, 1 - k, place.cross(c)))
+            action(go(z, 1 - k, place.partner))
+
+        here = pltpu.make_async_copy(src(z, k), dst.at[z, k], al_loc.at[kind])
+        each(lambda copy: copy.start())
+        here.start()
+
+        def wait():
+            here.wait()
+            each(lambda copy: copy.wait_send())
+            for step in range(LINE):
+                c = (z + step) % LINE
+                for core in (0, 1):
+                    got = remote(
+                        src(c, k), dst.at[c, core], al_send.at[kind, c, core], al_recv.at[kind, c, core],
+                        place.partner,
+                    )
+                    if step == 0:
+                        pl.when(k != core)(lambda got=got: got.wait_recv())
+                    else:
+                        got.wait_recv()
+
+        return wait
+
+    waits = []
+
+    def square_sum(kind, buf, other, lanes, dst):
+        st, rc = kinds[kind]
+        cut = pl.ds(0, lanes)
+        near_part(kind, 0).wait_recv()
+        near_part(kind, 1).wait_recv()
+        fetch(
+            kind,
+            [
+                (st.at[3], buf.at[pl.ds(0, 512), cut]),
+                (rc.at[0], buf.at[pl.ds(512, 512), cut]),
+                (rc.at[1], other.at[pl.ds(0, 512), cut]),
+            ],
+            3 * kind,
+        )
+
+        def add_up(t, carry):
+            there = at128(t * 128)
+            acc = buf[there, 0:lanes].astype(F32) + buf[at128(512 + t * 128), 0:lanes].astype(F32)
+            buf[there, 0:lanes] = (acc + other[there, 0:lanes].astype(F32)).astype(BF16)
+            return carry
+
+        lax.fori_loop(0, 4, add_up, 0)
+        waits.append(
+            to_owner(
+                min(kind, 2), lambda c, core: buf.at[at128(c * 128 + core * 64, 64), cut], dst
+            )
+        )
+
+    square_sum(GATE, hid, ua, 1024, o_gu.at[0])
     gather_b.arrive_third()
     lax.fori_loop(3, 4, attended_step, 0)
 
@@ -1229,6 +1367,7 @@
 
     for step in range(1, LINE):
         line_sq(step, z).start()
+    square_sum(UP, dg, du, 1024, o_gu.at[1])
     for step in range(1, LINE):
         line_sq(step, (z + step) % LINE).wait_recv()
     sq_line[z] = sq_both[...]
@@ -1262,45 +1401,38 @@
     def token_step(s, carry):
         c = place.order(3 - s)
         left = ga[chunk_rows(c), 0:768]
-
-        def body(t, inner):
-            lanes = at128(t * 512, 512)
-            term[:, :, lanes] = dot_rt(left, wg[lanes, 0:768]).reshape(2, rows, 512)
-            return inner
-
-        lax.fori_loop(0, 4, body, 0)
-        sums.give(c, s)
-        pl.when(s > 0)(lambda: sums.pass_on(place.order(4 - s), s + 1))
+        for h in range(2):
+            term[...] = dot_rt(left, wg[1024 * h : 1024 * h + 1024, 0:768]).reshape(2, rows, 1024)
+            sums[h].give(c, s)
+        for h in range(2):
+            pl.when(s > 0)(lambda h=h: sums[h].pass_on(place.order(4 - s), s + 1))
         return carry
 
     lax.fori_loop(0, 4, token_step, 0)
-    sums.pass_on(z, 3)
-
-    for n, i in enumerate(order):
-        left = feature_rows(wd, chips[i])
-
-        def three(t, carry, left=left):
-            lanes = at128(t * 256, 256)
-            stage[0, :, lanes] = dot_lt(left, ga[:, lanes]).astype(BF16)
-            return carry
-
-        lax.fori_loop(0, 3, three, 0)
-        part = stage.at[0, :, pl.ds(0, 768)]
-        copy = pltpu.make_async_copy(part, st_qkv.at[i], st_sem.at[3])
-        copy.start()
-        copy.wait()
-        if i < 3:
-            send_part(2, i, st_qkv, rc_qkv).start()
-
+    for h in range(2):
+        sums[h].pass_on(z, 3)
+
+    def qkv_part(i):
+        stage[0, :, 0:768] = dot(feature_rows(wd, chips[i]), ga[:, 0:768]).astype(BF16)
+        sides = jnp.concatenate([gn_own[:, at128(512 * c + 128 * chips[i])] for c in range(LINE)], axis=1)
+        lane = lax.broadcasted_iota(jnp.int32, (8, 128), 1)
+        column = (lax.broadcasted_iota(jnp.int32, (8, 128), 0) == lane).astype(F32)
+        stage[0, :, 768:896] = exact(sides, column, ((0,), (0,))).astype(BF16)
+        put(QKV, i, stage.at[0], 3)
+
+    qkv_part(2)
+    for h in range(2):
+        sums[h].relay(True)
+    qkv_part(3)
     for s in range(2):
         for c in range(LINE):
-            dg[c * 256 + s * rows : c * 256 + s * rows + rows, 0:256] = (
+            ua[c * 256 + s * rows : c * 256 + s * rows + rows, 0:256] = (
                 wu[1024 + s * 512 + c * rows : 1024 + s * 512 + c * rows + rows, 768:1024]
             )
 
     def outer(t, carry):
         lanes = at128(t * 512, 512)
-        stage_d[:, lanes] = dot_lt(dg[:, 0:256], db[:, lanes]).astype(BF16)
+        stage_d[:, lanes] = dot_lt(ua[:, 0:256], db[:, lanes]).astype(BF16)
         return carry
 
     lax.fori_loop(0, 4, outer, 0)
@@ -1310,122 +1442,48 @@
 
     def out_part(i):
         return remote(
-            st_out.at[at128(64 * chips[i], 64)], rc_out.at[i], in_send.at[3, i], in_recv.at[3, i], near[i]
+            st_out.at[at128(64 * chips[i], 64)], rc_out.at[i], in_send.at[OUT, i], in_recv.at[OUT, i], near[i]
         )
 
+    qkv_part(0)
+    qkv_part(1)
     for i in range(3):
         out_part(i).start()
 
-    def share(step, peer):
-        return remote(gn_own, gn_in.at[step], gs.at[step], gr.at[step], peer)
-
-    for step, peer in enumerate((place.partner, place.x, place.y)):
-        copy = share(step, peer)
-        copy.start()
-        copy.wait()
-        gn_own[...] = gn_own[...] + gn_in[step]
-
-    def line_gain(step, source):
-        return remote(
-            gn_own, gn_in.at[3 + source], gs.at[2 + step], gr.at[3 + source],
-            place.line((z + step) % LINE),
-        )
-
-    for step in range(1, LINE):
-        line_gain(step, z).start()
-
-    def to_owner(kind, src, dst):
-        def go(c, core, device, there):
-            return remote(
-                src(c, core), there, al_send.at[kind, c, core], al_recv.at[kind, z, k], device
-            )
-
-        def each(action):
-            for step in range(1, LINE):
-                c = (z + step) % LINE
-                action(go(c, k, place.line(c), dst.at[z, k]))
-                action(go(c, 1 - k, place.cross(c), dst.at[z, k]))
-            action(go(z, 1 - k, place.partner, dst.at[z, k]))
-
-        here = pltpu.make_async_copy(src(z, k), dst.at[z, k], al_loc.at[kind])
-        each(lambda copy: copy.start())
-        here.start()
-
-        def wait():
-            here.wait()
-            each(lambda copy: copy.wait_send())
-            for step in range(LINE):
-                c = (z + step) % LINE
-                for core in (0, 1):
-                    got = remote(
-                        src(c, k), dst.at[c, core], al_send.at[kind, c, core], al_recv.at[kind, c, core],
-                        place.partner,
-                    )
-                    if step == 0:
-                        pl.when(k != core)(lambda got=got: got.wait_recv())
-                    else:
-                        got.wait_recv()
-
-        return wait
-
-    for i in range(3):
-        send_part(1, i, st_gu, rc_gu).wait_recv()
-    waits = []
-    for m, (a, b2) in enumerate(((hid, ua), (dg, du))):
-        slots = [a.at[pl.ds(0, 512)], a.at[pl.ds(512, 512)], b2.at[pl.ds(0, 512)], b2.at[pl.ds(512, 512)]]
-        sources = [rc_gu.at[0, m], rc_gu.at[1, m], rc_gu.at[2, m], st_gu.at[3, m]]
-        copies = [
-            pltpu.make_async_copy(src, dst, sum_sem.at[4 + 4 * m + i])
-            for i, (src, dst) in enumerate(zip(sources, slots))
-        ]
-        for copy in copies:
-            copy.start()
-        for copy in copies:
-            copy.wait()
-
-        def add_up(t, carry, a=a, b2=b2):
-            there = at128(t * 128)
-            acc = a[there].astype(F32) + a[at128(512 + t * 128)].astype(F32)
-            acc = acc + b2[there].astype(F32) + b2[at128(512 + t * 128)].astype(F32)
-            a[there] = acc.astype(BF16)
-            return carry
-
-        lax.fori_loop(0, 4, add_up, 0)
-        waits.append(
-            to_owner(
-                m, lambda c, core, a=a: a.at[at128(c * 128 + core * 64, 64)], o_gu.at[m]
-            )
-        )
-
-    o_tok[...] = (d_mid[...] + sums.total()).astype(BF16)
-    sums.finish()
-
-    for i in range(3):
-        send_part(2, i, st_qkv, rc_qkv).wait_recv()
-    lanes = pl.ds(0, 768)
-    slots = [ua.at[pl.ds(0, 512), lanes], ua.at[pl.ds(512, 512), lanes],
-             du.at[pl.ds(0, 512), lanes], du.at[pl.ds(512, 512), lanes]]
-    sources = [rc_qkv.at[0], rc_qkv.at[1], rc_qkv.at[2], st_qkv.at[3]]
-    copies = [
-        pltpu.make_async_copy(src, dst, sum_sem.at[12 + i])
-        for i, (src, dst) in enumerate(zip(sources, slots))
-    ]
-    for copy in copies:
-        copy.start()
-    for copy in copies:
-        copy.wait()
-
-    def add_qkv(t, carry):
-        there, then = at128(t * 128), at128(512 + t * 128)
-        acc = ua[there, 0:768].astype(F32) + ua[then, 0:768].astype(F32)
-        acc = acc + du[there, 0:768].astype(F32) + du[then, 0:768].astype(F32)
-        ua[there, 0:768] = acc.astype(BF16)
+    for h in range(2):
+        sums[h].relay(False)
+
+    near_part(DOWN, 0).wait_recv()
+    near_part(DOWN, 1).wait_recv()
+    fetch(
+        DOWN,
+        [
+            (st_dn.at[3], ms.at[pl.ds(0, 256)]),
+            (rc_dn.at[0], ms.at[pl.ds(256, 256)]),
+            (rc_dn.at[1], ms.at[pl.ds(512, 256)]),
+        ],
+        3 * DOWN,
+    )
+
+    def add_down(t, carry):
+        lanes = at128(t * 512, 512)
+        acc = ms[0:256, lanes].astype(F32) + ms[256:512, lanes].astype(F32)
+        dm[0:256, lanes] = (acc + ms[512:768, lanes].astype(F32)).astype(BF16)
         return carry
 
-    lax.fori_loop(0, 4, add_qkv, 0)
-    waits.append(
-        to_owner(2, lambda c, core: ua.at[at128(c * 128 + core * 64, 64), lanes], o_qkv)
-    )
+    lax.fori_loop(0, 4, add_down, 0)
+    down_done = dm.at[pl.ds(0, 256)]
+    fin_down = remote(down_done, o_down, fin_send.at[0], fin_recv.at[0], down_to)
+    keep_down = pltpu.make_async_copy(down_done, o_down, fin_loc.at[0])
+    pl.when(down_moves)(lambda: fin_down.start())
+    pl.when(jnp.logical_not(down_moves))(lambda: keep_down.start())
+
+    for h in range(2):
+        out = slice(1024 * h, 1024 * h + 1024)
+        o_tok[:, out] = (d_mid[:, out] + sums[h].total()).astype(BF16)
+        sums[h].finish()
+
+    square_sum(QKV, ua, du, 896, o_qkv)
 
     for i in range(3):
         out_part(i).wait_recv()
@@ -1447,24 +1505,16 @@
     pl.when(out_moves)(lambda: fin_out.start())
     pl.when(jnp.logical_not(out_moves))(lambda: keep_out.start())
 
-    for step in range(1, LINE):
-        line_gain(step, (z + step) % LINE).wait_recv()
-    for step in range(1, LINE):
-        line_gain(step, z).wait_send()
-    total = gn_own[...]
-    for step in range(1, LINE):
-        total = total + gn_in[3 + (z + step) % LINE]
-    o_gains[...] = total
-
     gather_b.finish()
     pair_sq.wait_send()
     for step in range(1, LINE):
         line_sq(step, z).wait_send()
     for i in range(3):
-        send_part(0, i, st_dn, rc_dn).wait_send()
-        send_part(1, i, st_gu, rc_gu).wait_send()
-        send_part(2, i, st_qkv, rc_qkv).wait_send()
         out_part(i).wait_send()
+    for kind in kinds:
+        for i in range(2):
+            near_part(kind, i).wait_send()
+            far_part(kind, i).wait_send()
     for wait in waits:
         wait()
     pl.when(down_moves)(lambda: fin_down.wait())
@@ -1483,39 +1533,41 @@
         shape((256, 2048), BF16),
         shape((64, 2048), BF16),
         shape((2, 4, 2, 64, 1024), BF16),
-        shape((4, 2, 64, 768), BF16),
+        shape((4, 2, 64, 896), BF16),
     ]
     transit = [
+        shape((4, 512, 1024), BF16),
+        shape((3, 512, 1024), BF16),
+        shape((4, 512, 1024), BF16),
+        shape((3, 512, 1024), BF16),
         shape((4, 256, 2048), BF16),
         shape((3, 256, 2048), BF16),
-        shape((4, 2, 512, 1024), BF16),
-        shape((3, 2, 512, 1024), BF16),
-        shape((4, 512, 768), BF16),
-        shape((3, 512, 768), BF16),
+        shape((4, 512, 896), BF16),
+        shape((3, 512, 896), BF16),
         shape((256, 2048), BF16),
         shape((3, 64, 2048), BF16),
     ]
     wide, square = pltpu.VMEM((1024, 2048), BF16), pltpu.VMEM((1024, 1024), BF16)
     tall = pltpu.VMEM((2048, 1024), BF16)
-    rows = pltpu.VMEM((4, 128, 2048), BF16)
+    rows = pltpu.VMEM((2, 4, 128, 1024), BF16)
     small = pltpu.VMEM((4, 8, 256), F32)
     return pl.pallas_call(
         backward_kernel,
         name="backward",
-        out_shape=[shape((128, 2048), BF16), shape((8, 2048), F32)] + results + transit,
+        out_shape=[shape((128, 2048), BF16)] + results + transit,
         in_specs=[vmem_spec()] * 7 + [any_spec()] * len(kept),
-        out_specs=[vmem_spec()] * 2 + [any_spec()] * (len(results) + len(transit)),
+        out_specs=[vmem_spec()] + [any_spec()] * (len(results) + len(transit)),
         scratch_shapes=[
             wide, tall, tall, square, square, square, wide, square, square, wide, wide,
             pltpu.VMEM((2, 2, 512, 256), F32),
             pltpu.VMEM((2, 2, 512, 128), F32),
             pltpu.VMEM((2, 512, 256), BF16),
             pltpu.VMEM((2, 2, 512, 256), F32),
-            pltpu.VMEM((2, 128, 2048), F32),
+            pltpu.VMEM((2, 128, 1024), F32),
             rows,
             rows,
-            pltpu.VMEM((2, 128, 2048), F32),
-            pltpu.VMEM((128, 2048), F32),
+            pltpu.VMEM((2, 2, 128, 1024), F32),
+            pltpu.VMEM((2, 128, 1024), F32),
             rows,
             rows,
             small,
@@ -1523,16 +1575,16 @@
             small,
             pltpu.VMEM((4, 4, 8, 256), F32),
             pltpu.VMEM((8, 2048), F32),
-            pltpu.VMEM((7, 8, 2048), F32),
             pltpu.VMEM((128, 2048), F32),
             pltpu.VMEM((2, 512, 1024), BF16),
             pltpu.VMEM((256, 2048), BF16),
+            pltpu.VMEM((256, 1024), BF16),
             dma((16,)),
+            dma(()),
             dma((2, 2, 4)), dma((2, 4)), dma((2, 4)), dma((2, 4)),
-            dma((4,)), dma((4,)), dma((4,)), dma((4,)),
+            dma((2, 4)), dma((2, 4)), dma((2, 4)), dma((2, 4)),
             dma((4,)), dma((5,)),
-            dma((6,)), dma((7,)),
-            dma((4, 3)), dma((4, 3)),
+            dma((5, 4)), dma((5, 4)),
             dma((4,)), dma((20,)),
             dma((2,)), dma((2,)), dma((2,)),
             dma((3, 4, 2)), dma((3, 4, 2)), dma((3,)),
@@ -1540,7 +1592,81 @@
         compiler_params=pltpu.CompilerParams(
             collective_id=1, has_side_effects=True, vmem_limit_bytes=64 * 1024 * 1024
         ),
-    )(gains_qk, gain_attn, d_mlp, cotangent, branch, scales, gm_part, *kept)[:6]
+    )(gains_qk, gain_attn, d_mlp, cotangent, branch, scales, gm_part, *kept)[:5]
+
+
+def arrange_kernel(
+    gate_up, qkv, out_rows, down, o_q, o_k, o_v, o_out, o_gate, o_up, o_down, g_q, g_k, g_attn, g_mlp,
+    v_gu, v_qkv, v_out, v_down, w_gu, w_qkv, w_out, w_down, in_sem, out_sem,
+):
+    reads = [
+        pltpu.make_async_copy(src, dst, in_sem.at[i])
+        for i, (src, dst) in enumerate([(gate_up, v_gu), (down, v_down), (qkv, v_qkv), (out_rows, v_out)])
+    ]
+    for copy in reads:
+        copy.start()
+    writes = []
+
+    def write(src, dst):
+        copy = pltpu.make_async_copy(src, dst, out_sem.at[len(writes)])
+        copy.start()
+        writes.append(copy)
+
+    reads[0].wait()
+    for m, dst in enumerate((o_gate, o_up)):
+        for z in range(LINE):
+            for k in range(2):
+                for q in range(PLANE):
+                    at = 1024 * (2 * q + k) + 256 * z
+                    w_gu[m, :, at : at + 256] = v_gu[m, z, k, :, 256 * q : 256 * q + 256].astype(F32)
+        write(w_gu.at[m], dst)
+    reads[1].wait()
+    w_down[...] = v_down[...].astype(F32)
+    write(w_down, o_down)
+    reads[2].wait()
+    total = jnp.zeros((64, 128), F32)
+    for z in range(LINE):
+        for k in range(2):
+            at = 256 * (2 * z + k)
+            for m in range(3):
+                w_qkv[m, :, at : at + 256] = v_qkv[z, k, :, 256 * m : 256 * m + 256].astype(F32)
+            total = total + v_qkv[z, k, :, 768:896].astype(F32)
+    for m, dst in enumerate((o_q, o_k, o_v)):
+        write(w_qkv.at[m], dst)
+    lane = lax.broadcasted_iota(jnp.int32, (8, 128), 1)
+    pick = (lax.broadcasted_iota(jnp.int32, (8, 128), 0) == lane).astype(F32)
+    gains = exact(pick, total, ((1,), (1,)))
+    for i, ref in enumerate((g_q, g_k, g_attn, g_mlp)):
+        ref[...] = gains[i : i + 1]
+    reads[3].wait()
+    w_out[...] = v_out[...].astype(F32)
+    write(w_out, o_out)
+    for copy in writes:
+        copy.wait()
+
+
+def run_arrange(gate_up, qkv, out_rows, down):
+    shape = jax.ShapeDtypeStruct
+    arrays = (gate_up, qkv, out_rows, down)
+    square = shape((64, 2048), F32)
+    return pl.pallas_call(
+        arrange_kernel,
+        name="arrange",
+        out_shape=[square] * 4 + [shape((64, 8192), F32)] * 2 + [shape((256, 2048), F32)]
+        + [shape((1, 64), F32)] * 4,
+        in_specs=[any_spec()] * 4,
+        out_specs=[any_spec()] * 7 + [vmem_spec()] * 4,
+        scratch_shapes=[pltpu.VMEM(a.shape, a.dtype) for a in arrays]
+        + [
+            pltpu.VMEM((2, 64, 8192), F32),
+            pltpu.VMEM((3, 64, 2048), F32),
+            pltpu.VMEM((64, 2048), F32),
+            pltpu.VMEM((256, 2048), F32),
+            pltpu.SemaphoreType.DMA((4,)),
+            pltpu.SemaphoreType.DMA((7,)),
+        ],
+        compiler_params=pltpu.CompilerParams(vmem_limit_bytes=48 * 1024 * 1024),
+    )(*arrays)
 
 
 def shards_kernels(tokens, block_pairs, w_query, w_key, w_value, w_out, w_gate, w_up, w_down,
@@ -1555,27 +1681,11 @@
         block_pairs, gains_qk, gain_attn[None], gain_mlp[None], tokens[0], cotangent[0],
         (w_query, w_key, w_value, w_out, w_gate, w_up, w_down),
     )
-    d_tokens, gains, down, out_rows, gate_up, qkv = run_backward(
+    d_tokens, down, out_rows, gate_up, qkv = run_backward(
         gains_qk, gain_attn[None], d_mlp, cotangent[0], branch, scales, gm_part, kept
     )
-    gate_up = gate_up.reshape(2, 4, 2, 64, 4, 256).transpose(0, 3, 4, 2, 1, 5).reshape(2, 64, 8192)
-    qkv = qkv.reshape(4, 2, 64, 3, 256).transpose(3, 2, 0, 1, 4).reshape(3, 64, 2048)
-    gains = lax.dynamic_slice_in_dim(gains, 64 * (8 * z + f), 64, 1)
-    return (
-        out[None],
-        d_tokens[None],
-        qkv[0].astype(F32),
-        qkv[1].astype(F32),
-        qkv[2].astype(F32),
-        out_rows.astype(F32),
-        gate_up[0].astype(F32),
-        gate_up[1].astype(F32),
-        down.astype(F32),
-        gains[0],
-        gains[1],
-        gains[2],
-        gains[3],
-    )
+    grads = run_arrange(gate_up, qkv, out_rows, down)
+    return (out[None], d_tokens[None], *grads[:7], *[g[0] for g in grads[7:]])
 
 
 def shards(*arrays):

time: 666 us -> 479 us (0.72)
  the two profiles are of different devices: /device:TPU:27 before, /device:TPU:11 now
where the time goes in v3:
time: 479 us; the launch traced here: 471 us
  Pallas kernels  461 us (96%)
  local copies, waits for them, and re-layouts  8.06 us (2%)
    pallas_call x1, Pallas kernels, run_backward(): pl.pallas_call(backward_kernel, name='backward', out_shape=[shape((128, 2...  256 us
    pallas_call x1, Pallas kernels, run_forward(): pl.pallas_call(forward_kernel, name='forward', out_shape=[shape((128, 204...  201 us

profile of v3, /device:TPU:11, one launch (start us, length us, event | category | flops | bytes accessed | tf_op | source)
XLA Modules:
  0.0 470.8 jit_solution(6593353423938959026)
XLA Ops:
  0.7 0.8 dynamic_slice.6
  1.4 0.8 dynamic_slice.7
  2.2 0.6 pad_maximum_fusion.gains_qk
  2.8 200.6 %forward.1 = (bf16[128,2048]{1,0:T(8,128)(2,1)}, bf16[128,2048]{1,0:T(8,128)(2,1)}, f32[1,2048]{1,0:T(1,128)}, f32[128,2048]{1,0:T(8,128)}, f32[4,8,256]{2,1,0:T...) custom-call(s32[1,4]{1,0:T(1,128)} %pairs.1, ...), custom_call_target="tpu_custom_call" | custom-call | tf_op jit(solution)/shard_map/forward/pallas_call | solution.py:946
  203.4 255.9 %backward.1 = (bf16[128,2048]{1,0:T(8,128)(2,1)}, bf16[256,2048]{1,0:T(8,128)(2,1)}, bf16[64,2048]{1,0:T(8,128)(2,1)}, bf16[2,4,2,64,1024]{4,3,2,1,0:T(8,128)(2,...) custom-call(f32[2,256]{1,0:T(2,128)} %pad_maximum_fusion.gains_qk, ...), custom_call_target="tpu_custom_call" | custom-call | tf_op jit(solution)/shard_map/backward/pallas_call | solution.py:1554
  459.3 0.0 copy-start
  459.3 1.6 copy-done
  460.9 0.0 copy-start.1
  460.9 1.2 copy-done.1
  462.1 0.0 copy-start.2
  462.1 1.2 copy-done.2
  463.3 0.0 copy-start.3
  463.3 0.9 copy-done.3
  464.3 0.0 copy-start.4
  464.3 0.0 copy-start.5
  464.3 4.5 arrange.1
  468.8 0.0 copy-done.4
  468.8 0.8 copy.29
  469.6 0.0 copy-done.5
  469.6 0.8 copy.30
Async XLA Ops:
  459.3 1.6 copy-start
  460.9 1.2 copy-start.1
  462.1 1.2 copy-start.2
  463.3 0.9 copy-start.3
  464.3 4.5 copy-start.4
  464.3 5.3 %copy-start.5 = (bf16[128,2048]{1,0:T(8,128)(2,1)S(1)}, bf16[128,2048]{1,0:T(8,128)(2,1)}, u32[]{:S(2)}) copy-start(bf16[128,2048]{1,0:T(8,128)(2,1)} %get-tuple-element.69) | copy-start | bytes 1572868

commit v4 on v3

--- a/solution.py
+++ b/solution.py
@@ -543,13 +543,13 @@
 
 
 def forward_kernel(
-    pairs, gains_qk, gain_attn, gain_mlp, tokens, cotangent,
+    pairs, gain_query, gain_key, gain_attn, gain_mlp, tokens, cotangent,
     w_query, w_key, w_value, w_out, w_gate, w_up, w_down,
     o_out, o_dmlp, o_gm, o_branch, o_tot,
     o_qkv, o_wo, o_g, o_u, o_dn, o_x, o_m, o_ga, o_ua, o_hid, o_raw, o_heads, o_probs, o_att, o_tab,
     qkv, wo, wg, wu, wd, xs, ms, ga, ua, hid, raw, heads, probs, att, tab, posr, posc,
     term, pair_out, pair_in, keep, mine, line_out, line_in,
-    sq_own, sq_pair, sq_both, sq_line, mid,
+    sq_own, sq_pair, sq_both, sq_line, mid, gains_qk, branch_kept,
     loc_sem, swap_send, swap_recv, ring_send, ring_recv, wo_send, wo_recv,
     zs, zr, cs, cr, ps, pr, ls, lr, ts, tr, as_, ar, out_sem,
 ):
@@ -560,6 +560,9 @@
     cols = 256
     seq = 512
     place.barrier()
+
+    for i, ref in enumerate((gain_query, gain_key)):
+        gains_qk[i : i + 1, :] = ref[:, at128(256 * (2 * z + k), 256)]
 
     def own_rows(n):
         return at128(n * (2 * p + k), n)
@@ -799,7 +802,7 @@
     branch = jnp.concatenate([sums[h].total() for h in range(2)], axis=1)
     for h in range(2):
         sums[h].finish()
-    o_branch[...] = branch
+    branch_kept[...] = branch
 
     def mean_sq(v):
         return jnp.sum(v * v, axis=1, keepdims=True) / width
@@ -831,35 +834,41 @@
         lax.fori_loop(0, 4, body, 0)
         return carry
 
-    def contract(h):
+    def contract(h, first, last):
         def step(s, carry):
             c = place.order(s)
             term[...] = dot(hid[c], wd[h]).reshape(2, rows, 1024)
             sums[h].give(c, s)
-            pl.when(s > 0)(lambda: sums[h].pass_on(place.order(s - 1), s + 1))
+            pl.when(s > first)(lambda: sums[h].pass_on(place.order(s - 1), s + 1))
             return carry
 
-        return step
+        lax.fori_loop(first, last, step, 0)
+
+    def flush(h, last):
+        sums[h].pass_on(place.order(last - 1), last - 1)
 
     lax.fori_loop(0, 1, expand, 0)
     gather_m.arrive_first()
     lax.fori_loop(1, 2, expand, 0)
     ring_d[0].ready()
-    lax.fori_loop(0, 2, contract(0), 0)
+    contract(0, 0, 2)
     gather_m.arrive_second()
+    flush(0, 2)
     ring_d[1].forward()
     lax.fori_loop(2, 3, expand, 0)
-    lax.fori_loop(2, 3, contract(0), 0)
+    contract(0, 2, 3)
     ring_d[1].ready()
-    lax.fori_loop(0, 3, contract(1), 0)
+    flush(0, 3)
+    contract(1, 0, 3)
     gather_m.arrive_third()
+    flush(1, 3)
     lax.fori_loop(3, 4, expand, 0)
+    contract(0, 3, 4)
+    contract(1, 3, 4)
     for h in range(2):
-        lax.fori_loop(3, 4, contract(h), 0)
+        flush(h, 4)
     for h in range(2):
         sums[h].relay(False)
-    for h in range(2):
-        sums[h].pass_on(place.order(3), 3)
     for h in range(2):
         sums[h].relay(True)
 
@@ -867,7 +876,7 @@
         (qkv, o_qkv), (wo, o_wo), (wg, o_g), (wu, o_u), (wd.at[0], o_dn.at[:, pl.ds(0, 1024)]),
         (wd.at[1], o_dn.at[:, pl.ds(1024, 1024)]), (xs, o_x), (ms, o_m), (ga, o_ga),
         (ua, o_ua), (hid, o_hid), (raw, o_raw), (heads, o_heads), (probs, o_probs), (att, o_att),
-        (tab, o_tab),
+        (tab, o_tab), (branch_kept, o_branch),
     ]
     copies = [pltpu.make_async_copy(a, b, out_sem.at[i]) for i, (a, b) in enumerate(saves)]
     for copy in copies:
@@ -923,7 +932,7 @@
     return pl.BlockSpec(memory_space=pltpu.VMEM)
 
 
-def run_forward(pairs, gains_qk, gain_attn, gain_mlp, tokens, cotangent, weights):
+def run_forward(pairs, gain_query, gain_key, gain_attn, gain_mlp, tokens, cotangent, weights):
     shape = jax.ShapeDtypeStruct
     dma = pltpu.SemaphoreType.DMA
     kept = [
@@ -954,8 +963,8 @@
             shape((4, 8, 256), F32),
         ]
         + kept,
-        in_specs=[pl.BlockSpec(memory_space=pltpu.SMEM)] + [vmem_spec()] * 5 + [any_spec()] * 7,
-        out_specs=[vmem_spec()] * 5 + [any_spec()] * len(kept),
+        in_specs=[pl.BlockSpec(memory_space=pltpu.SMEM)] + [vmem_spec()] * 6 + [any_spec()] * 7,
+        out_specs=[vmem_spec()] * 3 + [any_spec(), vmem_spec()] + [any_spec()] * len(kept),
         scratch_shapes=[pltpu.VMEM((2, 1024, 1024) if i == 4 else k.shape, k.dtype) for i, k in enumerate(kept)]
         + [
             pltpu.VMEM((2, 8, 512), F32),
@@ -971,6 +980,8 @@
             pltpu.VMEM((4, 8, 256), F32),
             pltpu.VMEM((4, 8, 256), F32),
             pltpu.VMEM((4, 4, 8, 256), F32),
+            pltpu.VMEM((128, 2048), F32),
+            pltpu.VMEM((2, 256), F32),
             pltpu.VMEM((128, 2048), F32),
             dma((14,)),
             dma((11,)),
@@ -991,22 +1002,22 @@
             dma((4,)),
             dma((4,)),
             dma((5,)),
-            dma((len(kept) + 1,)),
+            dma((len(kept) + 2,)),
         ],
         compiler_params=pltpu.CompilerParams(
             collective_id=0, has_side_effects=True, vmem_limit_bytes=64 * 1024 * 1024
         ),
-    )(pairs, gains_qk, gain_attn, gain_mlp, tokens, cotangent, *weights)
+    )(pairs, gain_query, gain_key, gain_attn, gain_mlp, tokens, cotangent, *weights)
 
 
 def backward_kernel(
-    gains_qk, gain_attn, d_mlp, cotangent, branch, scales, gm_part,
+    gain_query, gain_key, gain_attn, d_mlp, h_cot, h_branch, scales, gm_part,
     h_qkv, h_wo, h_g, h_u, h_dn, h_x, h_m, h_ga, h_ua, h_hid, h_raw, h_heads, h_probs, h_att, h_tab,
     o_tok, o_down, o_out, o_gu, o_qkv,
     st_g, rc_g, st_u, rc_u, st_dn, rc_dn, st_qkv, rc_qkv, st_out, rc_out,
     wd, wg, wu, ga, ua, hid, dm, dg, du, ms, db, raw, tab, datt, dy,
     term, pair_out, pair_in, keep, mine, line_out, line_in,
-    sq_own, sq_pair, sq_both, sq_line, gn_own, d_mid, stage, stage_d, far_in,
+    sq_own, sq_pair, sq_both, sq_line, gn_own, d_mid, stage, stage_d, far_in, gains_qk, cotangent, branch,
     ld, far_sem, zs, zr, cs, cr, ps, pr, ls, lr, as_, ar, in_send, in_recv, st_sem, sum_sem,
     fin_send, fin_recv, fin_loc, al_send, al_recv, al_loc,
 ):
@@ -1028,6 +1039,8 @@
         [(down_moves, down_from), (out_moves, out_from)],
     )
 
+    for i, ref in enumerate((gain_query, gain_key)):
+        gains_qk[i : i + 1, :] = ref[:, at128(256 * (2 * z + k), 256)]
     loads = {}
 
     def load(name, src, dst):
@@ -1060,6 +1073,8 @@
     load("wu", h_u, wu)
     load("hid", h_hid, hid)
     load("ms", h_m, ms)
+    load("cot", h_cot, cotangent)
+    load("branch", h_branch, branch)
     load("raw", h_raw, raw)
     load("tab", h_tab, tab)
 
@@ -1203,6 +1218,8 @@
     def mean_of(v):
         return jnp.sum(v, axis=1, keepdims=True) / width
 
+    loads["cot"].wait()
+    loads["branch"].wait()
     d_mid[...] = cotangent[...].astype(F32) + jnp.concatenate([sums[h].total() for h in range(2)], axis=1)
     for h in range(2):
         sums[h].finish()
@@ -1523,7 +1540,7 @@
     pl.when(jnp.logical_not(out_moves))(lambda: keep_out.wait())
 
 
-def run_backward(gains_qk, gain_attn, d_mlp, cotangent, branch, scales, gm_part, kept):
+def run_backward(gain_query, gain_key, gain_attn, d_mlp, cotangent, branch, scales, gm_part, kept):
     shape = jax.ShapeDtypeStruct
     dma = pltpu.SemaphoreType.DMA
     flat = [(2048, 768), (256, 2048), (2048, 1024), (2048, 1024), (1024, 2048), (1024, 2048), (1024, 2048),
@@ -1555,7 +1572,7 @@
         backward_kernel,
         name="backward",
         out_shape=[shape((128, 2048), BF16)] + results + transit,
-        in_specs=[vmem_spec()] * 7 + [any_spec()] * len(kept),
+        in_specs=[vmem_spec()] * 4 + [any_spec()] * 2 + [vmem_spec()] * 2 + [any_spec()] * len(kept),
         out_specs=[vmem_spec()] + [any_spec()] * (len(results) + len(transit)),
         scratch_shapes=[
             wide, tall, tall, square, square, square, wide, square, square, wide, wide,
@@ -1579,7 +1596,10 @@
             pltpu.VMEM((2, 512, 1024), BF16),
             pltpu.VMEM((256, 2048), BF16),
             pltpu.VMEM((256, 1024), BF16),
-            dma((16,)),
+            pltpu.VMEM((2, 256), F32),
+            pltpu.VMEM((128, 2048), BF16),
+            pltpu.VMEM((128, 2048), F32),
+            dma((18,)),
             dma(()),
             dma((2, 2, 4)), dma((2, 4)), dma((2, 4)), dma((2, 4)),
             dma((2, 4)), dma((2, 4)), dma((2, 4)), dma((2, 4)),
@@ -1592,16 +1612,20 @@
         compiler_params=pltpu.CompilerParams(
             collective_id=1, has_side_effects=True, vmem_limit_bytes=64 * 1024 * 1024
         ),
-    )(gains_qk, gain_attn, d_mlp, cotangent, branch, scales, gm_part, *kept)[:5]
+    )(gain_query, gain_key, gain_attn, d_mlp, cotangent, branch, scales, gm_part, *kept)[:5]
 
 
 def arrange_kernel(
-    gate_up, qkv, out_rows, down, o_q, o_k, o_v, o_out, o_gate, o_up, o_down, g_q, g_k, g_attn, g_mlp,
-    v_gu, v_qkv, v_out, v_down, w_gu, w_qkv, w_out, w_down, in_sem, out_sem,
+    gate_up, qkv, out_rows, down, result, d_tokens,
+    o_result, o_tokens, o_q, o_k, o_v, o_out, o_gate, o_up, o_down, g_q, g_k, g_attn, g_mlp,
+    v_gu, v_qkv, v_out, v_down, v_result, v_tokens, w_gu, w_qkv, w_out, w_down, in_sem, out_sem,
 ):
     reads = [
         pltpu.make_async_copy(src, dst, in_sem.at[i])
-        for i, (src, dst) in enumerate([(gate_up, v_gu), (down, v_down), (qkv, v_qkv), (out_rows, v_out)])
+        for i, (src, dst) in enumerate([
+            (gate_up, v_gu), (down, v_down), (qkv, v_qkv), (out_rows, v_out), (result, v_result),
+            (d_tokens, v_tokens),
+        ])
     ]
     for copy in reads:
         copy.start()
@@ -1641,50 +1665,48 @@
     reads[3].wait()
     w_out[...] = v_out[...].astype(F32)
     write(w_out, o_out)
+    reads[4].wait()
+    write(v_result, o_result)
+    reads[5].wait()
+    write(v_tokens, o_tokens)
     for copy in writes:
         copy.wait()
 
 
-def run_arrange(gate_up, qkv, out_rows, down):
+def run_arrange(*arrays):
     shape = jax.ShapeDtypeStruct
-    arrays = (gate_up, qkv, out_rows, down)
     square = shape((64, 2048), F32)
     return pl.pallas_call(
         arrange_kernel,
         name="arrange",
-        out_shape=[square] * 4 + [shape((64, 8192), F32)] * 2 + [shape((256, 2048), F32)]
+        out_shape=[shape((128, 2048), BF16)] * 2 + [square] * 4 + [shape((64, 8192), F32)] * 2 + [shape((256, 2048), F32)]
         + [shape((1, 64), F32)] * 4,
-        in_specs=[any_spec()] * 4,
-        out_specs=[any_spec()] * 7 + [vmem_spec()] * 4,
+        in_specs=[any_spec()] * 6,
+        out_specs=[any_spec()] * 9 + [vmem_spec()] * 4,
         scratch_shapes=[pltpu.VMEM(a.shape, a.dtype) for a in arrays]
         + [
             pltpu.VMEM((2, 64, 8192), F32),
             pltpu.VMEM((3, 64, 2048), F32),
             pltpu.VMEM((64, 2048), F32),
             pltpu.VMEM((256, 2048), F32),
-            pltpu.SemaphoreType.DMA((4,)),
-            pltpu.SemaphoreType.DMA((7,)),
+            pltpu.SemaphoreType.DMA((6,)),
+            pltpu.SemaphoreType.DMA((9,)),
         ],
-        compiler_params=pltpu.CompilerParams(vmem_limit_bytes=48 * 1024 * 1024),
+        compiler_params=pltpu.CompilerParams(vmem_limit_bytes=64 * 1024 * 1024),
     )(*arrays)
 
 
 def shards_kernels(tokens, block_pairs, w_query, w_key, w_value, w_out, w_gate, w_up, w_down,
                    gain_query, gain_key, gain_attn, gain_mlp, cotangent):
-    z = lax.axis_index("ctx")
-    f = lax.axis_index("fsdp")
-    start = 256 * (2 * z + f % 2)
-    gains_qk = jnp.stack([
-        lax.dynamic_slice_in_dim(gain_query, start, 256), lax.dynamic_slice_in_dim(gain_key, start, 256)
-    ])
+    gains = [gain_query[None], gain_key[None], gain_attn[None]]
     out, d_mlp, gm_part, branch, scales, *kept = run_forward(
-        block_pairs, gains_qk, gain_attn[None], gain_mlp[None], tokens[0], cotangent[0],
+        block_pairs, *gains, gain_mlp[None], tokens[0], cotangent[0],
         (w_query, w_key, w_value, w_out, w_gate, w_up, w_down),
     )
     d_tokens, down, out_rows, gate_up, qkv = run_backward(
-        gains_qk, gain_attn[None], d_mlp, cotangent[0], branch, scales, gm_part, kept
-    )
-    grads = run_arrange(gate_up, qkv, out_rows, down)
+        *gains, d_mlp, cotangent[0], branch, scales, gm_part, kept
+    )
+    out, d_tokens, *grads = run_arrange(gate_up, qkv, out_rows, down, out, d_tokens)
     return (out[None], d_tokens[None], *grads[:7], *[g[0] for g in grads[7:]])
 
 

time: 479 us -> 468 us (0.977)
  local copies, waits for them, and re-layouts: 8.06 us -> 0 us
    unnamed x14 -> x0, local copies, waits for them, and re-layouts: 6.53 us -> none
where the time goes in v4:
time: 468 us; the launch traced here: 459 us
  Pallas kernels  458 us (98%)
    pallas_call x1, Pallas kernels, run_backward(): pl.pallas_call(backward_kernel, name='backward', out_shape=[shape((128, 2...  256 us
    pallas_call x1, Pallas kernels, run_forward(): pl.pallas_call(forward_kernel, name='forward', out_shape=[shape((128, 204...  196 us

profile of v4, /device:TPU:11, one launch (start us, length us, event | category | flops | bytes accessed | tf_op | source)
XLA Modules:
  0.0 458.8 jit_solution(280263797990300582)
XLA Ops:
  0.6 195.9 %forward.1 = (bf16[128,2048]{1,0:T(8,128)(2,1)}, bf16[128,2048]{1,0:T(8,128)(2,1)}, f32[1,2048]{1,0:T(1,128)}, f32[128,2048]{1,0:T(8,128)}, f32[4,8,256]{2,1,0:T...) custom-call(s32[1,4]{1,0:T(1,128)} %pairs.1, ...), custom_call_target="tpu_custom_call" | custom-call | tf_op jit(solution)/shard_map/forward/pallas_call | solution.py:955
  196.5 255.8 %backward.1 = (bf16[128,2048]{1,0:T(8,128)(2,1)}, bf16[256,2048]{1,0:T(8,128)(2,1)}, bf16[64,2048]{1,0:T(8,128)(2,1)}, bf16[2,4,2,64,1024]{4,3,2,1,0:T(8,128)(2,...) custom-call(f32[1,2048]{1,0:T(1,128)} %bitcast.32, ...), custom_call_target="tpu_custom_call" | custom-call | tf_op jit(solution)/shard_map/backward/pallas_call | solution.py:1571
  452.4 6.0 %arrange.1 = (bf16[128,2048]{1,0:T(8,128)(2,1)}, bf16[128,2048]{1,0:T(8,128)(2,1)}, f32[64,2048]{1,0:T(8,128)}, f32[64,2048]{1,0:T(8,128)}, f32[64,2048]{1,0:T(8...) custom-call(bf16[2,4,2,64,1024]{4,3,2,1,0:T(8,128)(2,1)} %get-tuple-, ...), custom_call_target="tpu_custom_call" | custom-call | tf_op jit(solution)/shard_map/arrange/pallas_call | solution.py:1679

commit v5 on v4

--- a/solution.py
+++ b/solution.py
@@ -791,6 +791,15 @@
     lax.fori_loop(0, 4, branch_step, 0)
     for h in range(2):
         sums[h].pass_on(z, 3)
+    copies = []
+
+    def save(*pairs):
+        for a, b in pairs:
+            copies.append(pltpu.make_async_copy(a, b, out_sem.at[len(copies)]))
+            copies[-1].start()
+
+    save((qkv, o_qkv), (wo, o_wo), (xs, o_x), (raw, o_raw), (heads, o_heads), (probs, o_probs), (att, o_att))
+    save((tab, o_tab))
     for h in range(2):
         sums[h].relay(True)
     ring_u.forward()
@@ -847,6 +856,7 @@
     def flush(h, last):
         sums[h].pass_on(place.order(last - 1), last - 1)
 
+    save((branch_kept, o_branch), (wg, o_g), (wu, o_u))
     lax.fori_loop(0, 1, expand, 0)
     gather_m.arrive_first()
     lax.fori_loop(1, 2, expand, 0)
@@ -872,15 +882,8 @@
     for h in range(2):
         sums[h].relay(True)
 
-    saves = [
-        (qkv, o_qkv), (wo, o_wo), (wg, o_g), (wu, o_u), (wd.at[0], o_dn.at[:, pl.ds(0, 1024)]),
-        (wd.at[1], o_dn.at[:, pl.ds(1024, 1024)]), (xs, o_x), (ms, o_m), (ga, o_ga),
-        (ua, o_ua), (hid, o_hid), (raw, o_raw), (heads, o_heads), (probs, o_probs), (att, o_att),
-        (tab, o_tab), (branch_kept, o_branch),
-    ]
-    copies = [pltpu.make_async_copy(a, b, out_sem.at[i]) for i, (a, b) in enumerate(saves)]
-    for copy in copies:
-        copy.start()
+    save((wd.at[0], o_dn.at[:, pl.ds(0, 1024)]), (wd.at[1], o_dn.at[:, pl.ds(1024, 1024)]), (ms, o_m), (ga, o_ga))
+    save((ua, o_ua), (hid, o_hid))
 
     mlp = jnp.concatenate([sums[h].total() for h in range(2)], axis=1)
     for h in range(2):

time: 468 us -> 463 us (0.989)
    pallas_call x1, Pallas kernels: 196 us -> 190 us  [run_forward(): pl.pallas_call(forward_kernel, name='forward', out_shape=[shape((128, 204...]
where the time goes in v5:
time: 463 us; the launch traced here: 455 us
  Pallas kernels  454 us (98%)
    pallas_call x1, Pallas kernels, run_backward(): pl.pallas_call(backward_kernel, name='backward', out_shape=[shape((128, 2...  258 us
    pallas_call x1, Pallas kernels, run_forward(): pl.pallas_call(forward_kernel, name='forward', out_shape=[shape((128, 204...  190 us

profile of v5, /device:TPU:11, one launch (start us, length us, event | category | flops | bytes accessed | tf_op | source)
XLA Modules:
  0.0 454.7 jit_solution(12281511049384869762)
XLA Ops:
  0.6 189.8 %forward.1 = (bf16[128,2048]{1,0:T(8,128)(2,1)}, bf16[128,2048]{1,0:T(8,128)(2,1)}, f32[1,2048]{1,0:T(1,128)}, f32[128,2048]{1,0:T(8,128)}, f32[4,8,256]{2,1,0:T...) custom-call(s32[1,4]{1,0:T(1,128)} %pairs.1, ...), custom_call_target="tpu_custom_call" | custom-call | tf_op jit(solution)/shard_map/forward/pallas_call | solution.py:958
  190.4 257.8 %backward.1 = (bf16[128,2048]{1,0:T(8,128)(2,1)}, bf16[256,2048]{1,0:T(8,128)(2,1)}, bf16[64,2048]{1,0:T(8,128)(2,1)}, bf16[2,4,2,64,1024]{4,3,2,1,0:T(8,128)(2,...) custom-call(f32[1,2048]{1,0:T(1,128)} %bitcast.32, ...), custom_call_target="tpu_custom_call" | custom-call | tf_op jit(solution)/shard_map/backward/pallas_call | solution.py:1574
  448.2 6.0 %arrange.1 = (bf16[128,2048]{1,0:T(8,128)(2,1)}, bf16[128,2048]{1,0:T(8,128)(2,1)}, f32[64,2048]{1,0:T(8,128)}, f32[64,2048]{1,0:T(8,128)}, f32[64,2048]{1,0:T(8...) custom-call(bf16[2,4,2,64,1024]{4,3,2,1,0:T(8,128)(2,1)} %get-tuple-, ...), custom_call_target="tpu_custom_call" | custom-call | tf_op jit(solution)/shard_map/arrange/pallas_call | solution.py:1682

commit v6 on v5

--- a/solution.py
+++ b/solution.py
@@ -861,6 +861,7 @@
     gather_m.arrive_first()
     lax.fori_loop(1, 2, expand, 0)
     ring_d[0].ready()
+    save((wd.at[0], o_dn.at[:, pl.ds(0, 1024)]))
     contract(0, 0, 2)
     gather_m.arrive_second()
     flush(0, 2)
@@ -868,11 +869,13 @@
     lax.fori_loop(2, 3, expand, 0)
     contract(0, 2, 3)
     ring_d[1].ready()
+    save((wd.at[1], o_dn.at[:, pl.ds(1024, 1024)]))
     flush(0, 3)
     contract(1, 0, 3)
     gather_m.arrive_third()
     flush(1, 3)
     lax.fori_loop(3, 4, expand, 0)
+    save((ms, o_m), (ga, o_ga), (ua, o_ua), (hid, o_hid))
     contract(0, 3, 4)
     contract(1, 3, 4)
     for h in range(2):
@@ -881,9 +884,6 @@
         sums[h].relay(False)
     for h in range(2):
         sums[h].relay(True)
-
-    save((wd.at[0], o_dn.at[:, pl.ds(0, 1024)]), (wd.at[1], o_dn.at[:, pl.ds(1024, 1024)]), (ms, o_m), (ga, o_ga))
-    save((ua, o_ua), (hid, o_hid))
 
     mlp = jnp.concatenate([sums[h].total() for h in range(2)], axis=1)
     for h in range(2):

time: 463 us -> 463 us (level)
  no operation moved by 1% of the time
where the time goes in v6:
time: 463 us; the launch traced here: 455 us
  Pallas kernels  454 us (98%)
    pallas_call x1, Pallas kernels, run_backward(): pl.pallas_call(backward_kernel, name='backward', out_shape=[shape((128, 2...  258 us
    pallas_call x1, Pallas kernels, run_forward(): pl.pallas_call(forward_kernel, name='forward', out_shape=[shape((128, 204...  190 us

profile of v6, /device:TPU:11, one launch (start us, length us, event | category | flops | bytes accessed | tf_op | source)
XLA Modules:
  0.0 454.7 jit_solution(1224635592952340464)
XLA Ops:
  0.6 189.8 %forward.1 = (bf16[128,2048]{1,0:T(8,128)(2,1)}, bf16[128,2048]{1,0:T(8,128)(2,1)}, f32[1,2048]{1,0:T(1,128)}, f32[128,2048]{1,0:T(8,128)}, f32[4,8,256]{2,1,0:T...) custom-call(s32[1,4]{1,0:T(1,128)} %pairs.1, ...), custom_call_target="tpu_custom_call" | custom-call | tf_op jit(solution)/shard_map/forward/pallas_call | solution.py:958
  190.4 257.8 %backward.1 = (bf16[128,2048]{1,0:T(8,128)(2,1)}, bf16[256,2048]{1,0:T(8,128)(2,1)}, bf16[64,2048]{1,0:T(8,128)(2,1)}, bf16[2,4,2,64,1024]{4,3,2,1,0:T(8,128)(2,...) custom-call(f32[1,2048]{1,0:T(1,128)} %bitcast.32, ...), custom_call_target="tpu_custom_call" | custom-call | tf_op jit(solution)/shard_map/backward/pallas_call | solution.py:1574
  448.2 6.0 %arrange.1 = (bf16[128,2048]{1,0:T(8,128)(2,1)}, bf16[128,2048]{1,0:T(8,128)(2,1)}, f32[64,2048]{1,0:T(8,128)}, f32[64,2048]{1,0:T(8,128)}, f32[64,2048]{1,0:T(8...) custom-call(bf16[2,4,2,64,1024]{4,3,2,1,0:T(8,128)(2,1)} %get-tuple-, ...), custom_call_target="tpu_custom_call" | custom-call | tf_op jit(solution)/shard_map/arrange/pallas_call | solution.py:1682
